TPU v7x, 32 devices: a whole 2x2x4 slice. The times are simulated.
32 devices in a mesh: dp: 4 (over y, x), seq: 8 (over z, core).
Axes of the slice: x: 2, y: 2, z: 4, core: 2. Of those that a mesh axis runs over, the one named last changes fastest.
Arguments:
- latents: bfloat16 [4, 1024, 1024], P('dp', 'seq'), may hold values from -6 to 6
- d_out: bfloat16 [4, 1024, 1024], P('dp', 'seq'), may hold values from -6 to 6
- lengths: int32 [4, 4], P('dp'), may hold values from 1 to 898, as said below
- gain_attn: bfloat16 [1024], P(('dp', 'seq')), may hold values from 0.5 to 1.5
- w_query: bfloat16 [1024, 1024], P(('dp', 'seq')), may hold values from -0.1875 to 0.1875
- w_key: bfloat16 [1024, 1024], P(('dp', 'seq')), may hold values from -0.1875 to 0.1875
- w_value: bfloat16 [1024, 1024], P(('dp', 'seq')), may hold values from -0.1875 to 0.1875
- w_out: bfloat16 [1024, 1024], P(('dp', 'seq')), may hold values from -1 to 1
- gain_ffn: bfloat16 [1024], P(('dp', 'seq')), may hold values from 0.5 to 1.5
- w_gate: bfloat16 [1024, 2816], P(('dp', 'seq')), may hold values from -0.1875 to 0.1875
- w_up: bfloat16 [1024, 2816], P(('dp', 'seq')), may hold values from -0.1875 to 0.1875
- w_down: bfloat16 [2816, 1024], P(('dp', 'seq')), may hold values from -0.109375 to 0.109375
Outputs:
- latents_out: bfloat16 [4, 1024, 1024], P('dp', 'seq')
- d_latents: bfloat16 [4, 1024, 1024], P('dp', 'seq')
- grad_gain_attn: float32 [1024], P(('dp', 'seq'))
- grad_w_query: float32 [1024, 1024], P(('dp', 'seq'))
- grad_w_key: float32 [1024, 1024], P(('dp', 'seq'))
- grad_w_value: float32 [1024, 1024], P(('dp', 'seq'))
- grad_w_out: float32 [1024, 1024], P(('dp', 'seq'))
- grad_gain_ffn: float32 [1024], P(('dp', 'seq'))
- grad_w_gate: float32 [1024, 2816], P(('dp', 'seq'))
- grad_w_up: float32 [1024, 2816], P(('dp', 'seq'))
- grad_w_down: float32 [2816, 1024], P(('dp', 'seq'))
Inputs may be any that keep to these rules, and one draw needn't show every extreme that they name: Each row holds the lengths of the 4 patch sequences of one group in order; they sum to 1024; in every group one sequence has the largest length.
All inputs are finite; a program needn't handle non-finite values.
Results may differ from a plain program's by a relative error of at most 0.018.
Values may be sent and summed in bfloat16 or wider, within the bound.
A program may use at most 256 MiB of HBM per device.

v0:
```python
import math

import jax
import jax.numpy as jnp
from jax import lax
from jax.sharding import PartitionSpec as P

HEADS = 16


EPS = 1e-05


def norm_rows(values, gain_vec):
    factor = lax.rsqrt(jnp.mean(values * values, axis=-1, keepdims=True) + EPS)
    normed = values * factor
    return (normed * gain_vec, normed, factor)


def norm_back(grad_out, normed, factor, gain_vec):
    scaled = grad_out * gain_vec
    inner = jnp.mean(scaled * normed, axis=-1, keepdims=True)
    return (factor * (scaled - normed * inner), jnp.sum(grad_out * normed, axis=0))


def dot_left(left, right):
    return lax.dot_general(
        left, right, (((0,), (0,)), ((), ())), preferred_element_type=jnp.float32
    )


def dot_right(left, right):
    return lax.dot_general(
        left, right, (((1,), (1,)), ((), ())), preferred_element_type=jnp.float32
    )


def per_device(
    latents,
    d_out,
    lengths,
    gain_attn,
    w_query,
    w_key,
    w_value,
    w_out,
    gain_ffn,
    w_gate,
    w_up,
    w_down,
):
    g_attn, full_query, full_key, full_value, full_out, g_ffn, full_gate, full_up, full_down = (
        lax.all_gather(gain_attn, ("dp", "seq"), axis=0, tiled=True),
        lax.all_gather(w_query, ("dp", "seq"), axis=0, tiled=True),
        lax.all_gather(w_key, ("dp", "seq"), axis=0, tiled=True),
        lax.all_gather(w_value, ("dp", "seq"), axis=0, tiled=True),
        lax.all_gather(w_out, ("dp", "seq"), axis=0, tiled=True),
        lax.all_gather(gain_ffn, ("dp", "seq"), axis=0, tiled=True),
        lax.all_gather(w_gate, ("dp", "seq"), axis=0, tiled=True),
        lax.all_gather(w_up, ("dp", "seq"), axis=0, tiled=True),
        lax.all_gather(w_down, ("dp", "seq"), axis=0, tiled=True),
    )
    gain_one = g_attn.astype(jnp.float32)
    gain_two = g_ffn.astype(jnp.float32)
    inputs_f = latents[0].astype(jnp.float32)
    row_count, model_width = inputs_f.shape
    head_size = model_width // HEADS
    group_rows = row_count * lax.axis_size("seq")
    here = lax.axis_index("seq") * row_count + jnp.arange(row_count, dtype=jnp.int32)
    seq_lens = lengths[0]
    seq_ends = jnp.cumsum(seq_lens, dtype=jnp.int32)
    begins = jnp.sum(
        jnp.where(seq_ends[None, :] <= here[:, None], seq_lens[None, :], 0), axis=1, dtype=jnp.int32
    )
    key_block = math.gcd(group_rows, 1024)
    block_count = group_rows // key_block
    key_positions = jnp.arange(group_rows, dtype=jnp.int32).reshape(block_count, key_block)
    h_one_f, normed_one, factor_one = norm_rows(inputs_f, gain_one)
    h_one = h_one_f.astype(jnp.bfloat16)
    query_proj = jnp.dot(h_one, full_query, preferred_element_type=jnp.float32).astype(jnp.bfloat16)
    key_proj = jnp.dot(h_one, full_key, preferred_element_type=jnp.float32).astype(jnp.bfloat16)
    value_proj = jnp.dot(h_one, full_value, preferred_element_type=jnp.float32).astype(jnp.bfloat16)
    keys_all, values_all = (
        lax.all_gather(key_proj, "seq", axis=0, tiled=True),
        lax.all_gather(value_proj, "seq", axis=0, tiled=True),
    )
    query_heads = query_proj.reshape(row_count, HEADS, head_size)

    def split_blocks(array):
        return array.reshape(block_count, key_block, HEADS, head_size)

    def block_scores(key_piece, pos_piece):
        scores = (
            jnp.einsum("qhd,khd->hqk", query_heads, key_piece, preferred_element_type=jnp.float32)
            * 0.125
        )
        allowed = (pos_piece[None, :] <= here[:, None]) & (pos_piece[None, :] >= begins[:, None])
        return (scores, allowed[None])

    def max_step(running, pieces):
        key_piece, pos_piece = pieces
        scores, allowed = block_scores(key_piece, pos_piece)
        return (jnp.maximum(running, jnp.max(jnp.where(allowed, scores, -1e30), axis=-1)), None)

    row_max, _ = lax.scan(
        max_step,
        jnp.full((HEADS, row_count), -1e30, jnp.float32),
        (split_blocks(keys_all), key_positions),
    )

    def sum_step(running, pieces):
        key_piece, value_piece, pos_piece = pieces
        scores, allowed = block_scores(key_piece, pos_piece)
        expon = jnp.where(
            allowed, jnp.exp(jnp.where(allowed, scores, -1e30) - row_max[:, :, None]), 0.0
        )
        rounded = expon.astype(jnp.bfloat16)
        total_sum, raw_sum = running
        total_sum = total_sum + jnp.sum(rounded.astype(jnp.float32), axis=-1)
        raw_sum = raw_sum + jnp.einsum(
            "hqk,khd->qhd", rounded, value_piece, preferred_element_type=jnp.float32
        )
        return ((total_sum, raw_sum), None)

    (total_sum, raw_sum), _ = lax.scan(
        sum_step,
        (
            jnp.zeros((HEADS, row_count), jnp.float32),
            jnp.zeros((row_count, HEADS, head_size), jnp.float32),
        ),
        (split_blocks(keys_all), split_blocks(values_all), key_positions),
    )
    totals_rows = jnp.transpose(total_sum)
    attended = raw_sum / totals_rows[:, :, None]
    attended_low = attended.reshape(row_count, model_width).astype(jnp.bfloat16)
    resid = inputs_f + jnp.dot(attended_low, full_out, preferred_element_type=jnp.float32)
    h_two_f, normed_two, factor_two = norm_rows(resid, gain_two)
    h_two = h_two_f.astype(jnp.bfloat16)
    gate_proj = jnp.dot(h_two, full_gate, preferred_element_type=jnp.float32)
    up_proj = jnp.dot(h_two, full_up, preferred_element_type=jnp.float32)
    gate_sigmoid = jax.nn.sigmoid(gate_proj)
    gate_active = gate_proj * gate_sigmoid
    hidden = (gate_active * up_proj).astype(jnp.bfloat16)
    outputs = resid + jnp.dot(hidden, full_down, preferred_element_type=jnp.float32)
    latents_out = outputs.astype(jnp.bfloat16)[None]
    grad_out = d_out[0]
    grad_down = dot_left(hidden, grad_out)
    g_hidden = dot_right(grad_out, full_down)
    g_gate = (g_hidden * up_proj * gate_sigmoid * (1.0 + gate_proj * (1.0 - gate_sigmoid))).astype(
        jnp.bfloat16
    )
    g_up = (g_hidden * gate_active).astype(jnp.bfloat16)
    grad_gate = dot_left(h_two, g_gate)
    grad_up = dot_left(h_two, g_up)
    g_h_two = dot_right(g_gate, full_gate) + dot_right(g_up, full_up)
    g_norm_two, grad_gain_two = norm_back(g_h_two, normed_two, factor_two, gain_two)
    g_resid = grad_out.astype(jnp.float32) + g_norm_two
    g_branch = g_resid.astype(jnp.bfloat16)
    grad_out_proj = dot_left(attended_low, g_branch)
    g_att = dot_right(g_branch, full_out).reshape(row_count, HEADS, head_size).astype(jnp.bfloat16)
    g_att_f = g_att.astype(jnp.float32)
    g_raw = (g_att_f / totals_rows[:, :, None]).astype(jnp.bfloat16)
    g_total = jnp.transpose(-jnp.sum(g_att_f * raw_sum, axis=-1) / (totals_rows * totals_rows))
    keys_back, values_back = (
        lax.all_gather(key_proj, "seq", axis=0, tiled=True),
        lax.all_gather(value_proj, "seq", axis=0, tiled=True),
    )

    def score_grads(key_piece, value_piece, pos_piece):
        scores, allowed = block_scores(key_piece, pos_piece)
        expon = jnp.where(
            allowed, jnp.exp(jnp.where(allowed, scores, -1e30) - row_max[:, :, None]), 0.0
        )
        g_probs = jnp.einsum("qhd,khd->hqk", g_raw, value_piece, preferred_element_type=jnp.float32)
        g_scores = (expon * (g_probs + g_total[:, :, None])).astype(jnp.bfloat16)
        return (expon, g_scores)

    def grad_step(running, pieces):
        key_piece, value_piece, pos_piece = pieces
        expon, g_scores = score_grads(key_piece, value_piece, pos_piece)
        rounded = expon.astype(jnp.bfloat16)
        running = (
            running
            + jnp.einsum("hqk,khd->qhd", g_scores, key_piece, preferred_element_type=jnp.float32)
            * 0.125
        )
        g_key_piece = (
            jnp.einsum("hqk,qhd->khd", g_scores, query_heads, preferred_element_type=jnp.float32)
            * 0.125
        )
        g_value_piece = jnp.einsum(
            "hqk,qhd->khd", rounded, g_raw, preferred_element_type=jnp.float32
        )
        return (running, (g_key_piece, g_value_piece))

    g_query_f, (g_keys, g_values) = lax.scan(
        grad_step,
        jnp.zeros((row_count, HEADS, head_size), jnp.float32),
        (split_blocks(keys_back), split_blocks(values_back), key_positions),
    )
    mine_key, mine_value = (
        lax.psum_scatter(
            g_keys.reshape(group_rows, model_width).astype(jnp.bfloat16),
            "seq",
            scatter_dimension=0,
            tiled=True,
        ).astype(jnp.float32),
        lax.psum_scatter(
            g_values.reshape(group_rows, model_width).astype(jnp.bfloat16),
            "seq",
            scatter_dimension=0,
            tiled=True,
        ).astype(jnp.float32),
    )
    g_key = mine_key.astype(jnp.bfloat16)
    g_value = mine_value.astype(jnp.bfloat16)
    g_query = g_query_f.reshape(row_count, model_width).astype(jnp.bfloat16)
    grad_query = dot_left(h_one, g_query)
    grad_key = dot_left(h_one, g_key)
    grad_value = dot_left(h_one, g_value)
    g_h_one = (
        dot_right(g_query, full_query) + dot_right(g_key, full_key) + dot_right(g_value, full_value)
    )
    g_norm_one, grad_gain_one = norm_back(g_h_one, normed_one, factor_one, gain_one)
    d_latents = (g_resid + g_norm_one).astype(jnp.bfloat16)[None]
    gain_pair = jnp.stack((grad_gain_one, grad_gain_two), axis=1)
    summed = (
        lax.psum_scatter(gain_pair, ("dp", "seq"), scatter_dimension=0, tiled=True),
        lax.psum_scatter(grad_query, ("dp", "seq"), scatter_dimension=0, tiled=True),
        lax.psum_scatter(grad_key, ("dp", "seq"), scatter_dimension=0, tiled=True),
        lax.psum_scatter(grad_value, ("dp", "seq"), scatter_dimension=0, tiled=True),
        lax.psum_scatter(grad_out_proj, ("dp", "seq"), scatter_dimension=0, tiled=True),
        lax.psum_scatter(grad_gate, ("dp", "seq"), scatter_dimension=0, tiled=True),
        lax.psum_scatter(grad_up, ("dp", "seq"), scatter_dimension=0, tiled=True),
        lax.psum_scatter(grad_down, ("dp", "seq"), scatter_dimension=0, tiled=True),
    )
    return (
        latents_out,
        d_latents,
        summed[0][:, 0],
        summed[1],
        summed[2],
        summed[3],
        summed[4],
        summed[0][:, 1],
        summed[5],
        summed[6],
        summed[7],
    )


def solution(mesh):
    return jax.shard_map(
        per_device,
        mesh=mesh,
        in_specs=(
            P("dp", "seq", None),
            P("dp", "seq", None),
            P("dp", None),
            P(("dp", "seq")),
            P(("dp", "seq"), None),
            P(("dp", "seq"), None),
            P(("dp", "seq"), None),
            P(("dp", "seq"), None),
            P(("dp", "seq")),
            P(("dp", "seq"), None),
            P(("dp", "seq"), None),
            P(("dp", "seq"), None),
        ),
        out_specs=(
            P("dp", "seq", None),
            P("dp", "seq", None),
            P(("dp", "seq")),
            P(("dp", "seq"), None),
            P(("dp", "seq"), None),
            P(("dp", "seq"), None),
            P(("dp", "seq"), None),
            P(("dp", "seq")),
            P(("dp", "seq"), None),
            P(("dp", "seq"), None),
            P(("dp", "seq"), None),
        ),
        check_vma=False,
    )
```

profile of v0, /device:TPU:9, one launch (start us, length us, event | category | flops | bytes accessed | tf_op | source)
XLA Modules:
  0.0 1804.9 jit_solution(10298502038612361129)
XLA Ops:
  11.2 39.8 %all-reduce.2 = (bf16[1024]{0:T(1024)(128)(2,1)S(1)}, bf16[1024]{0:T(1024)(128)(2,1)S(1)}) all-reduce(bf16[1024]{0:T(1024)(128)(2,1)S(1)} %dynamic-update-slice, bf16[1024]{0:T(1024)(128)(2,1)S(1)} %dynamic-update-slice.1), channel_id=1, replica_groups=mesh['dp'=4,'seq'=8] {'dp','seq'}, use_global_device_ids=true, to_apply=%add | all-reduce | flops 2048 | bytes 8192
  52.0 16.2 all-gather.16.cloned.1.call-done
  68.2 2.9 convolution_convert_fusion.2
  71.2 55.4 %all-gather.10.cloned.1.call-done = bf16[1024,1024]{1,0:T(8,128)(2,1)} async-done(((bf16[32,1024]{1,0:T(8,128)(2,1)}), bf16[1024,1024]{1,0:T(8,128)(2,1)}) %all-gather.10.cloned.1.call-update) | async-done | bytes 2097168 | tf_op jit(solution)/shard_map/all_gather | solution.py:56
  126.6 2.9 convolution_convert_fusion.4
  132.9 52.1 %all-gather.14.cloned.1.call-done = bf16[1024,1024]{1,0:T(8,128)(2,1)} async-done(((bf16[32,1024]{1,0:T(8,128)(2,1)}), bf16[1024,1024]{1,0:T(8,128)(2,1)}) %all-gather.14.cloned.1.call-update) | async-done | bytes 2097168 | tf_op jit(solution)/shard_map/all_gather | solution.py:54
  185.0 2.1 convolution_convert_fusion.3
  187.2 28.6 %all-gather.18.cloned.1.call-done = bf16[1024,1024]{1,0:T(8,128)(2,1)} async-done(((bf16[128,1024]{1,0:T(8,128)(2,1)}), bf16[1024,1024]{1,0:T(8,128)(2,1)}) %all-gather.18.cloned.1.call-update) | async-done | bytes 2097168 | tf_op jit(solution)/shard_map/all_gather | solution.py:84
  215.8 2.9 copy.40
  218.7 27.8 %all-gather.12.cloned.1.call-done = bf16[1024,1024]{1,0:T(8,128)(2,1)} async-done(((bf16[128,1024]{1,0:T(8,128)(2,1)}), bf16[1024,1024]{1,0:T(8,128)(2,1)}) %all-gather.12.cloned.1.call-update) | async-done | bytes 2097168 | tf_op jit(solution)/shard_map/all_gather | solution.py:85
  246.5 3.9 copy.38
  252.1 2.8 convert_reduce_fusion
  257.6 2.4 divide_convert_fusion.1
  259.9 44.5 %all-gather.20.cloned.1.call-done = bf16[1024,1024]{1,0:T(8,128)(2,1)} async-done(((bf16[32,1024]{1,0:T(8,128)(2,1)}), bf16[1024,1024]{1,0:T(8,128)(2,1)}) %all-gather.20.cloned.1.call-update) | async-done | bytes 2097168 | tf_op jit(solution)/shard_map/all_gather | solution.py:57
  304.5 2.1 multiply_reduce_fusion.3
  307.3 67.7 %all-gather.24.cloned.1.call-done = bf16[1024,2816]{1,0:T(8,128)(2,1)} async-done(((bf16[32,2816]{1,0:T(8,128)(2,1)}), bf16[1024,2816]{1,0:T(8,128)(2,1)}) %all-gather.24.cloned.1.call-update) | async-done | bytes 5767184 | tf_op jit(solution)/shard_map/all_gather | solution.py:60
  374.9 4.7 fusion.47
  379.6 64.5 %all-gather.22.cloned.1.call-done = bf16[1024,2816]{1,0:T(8,128)(2,1)} async-done(((bf16[32,2816]{1,0:T(8,128)(2,1)}), bf16[1024,2816]{1,0:T(8,128)(2,1)}) %all-gather.22.cloned.1.call-update) | async-done | bytes 5767184 | tf_op jit(solution)/shard_map/all_gather | solution.py:59
  444.1 4.7 fusion.46
  448.8 64.5 %all-gather.26.cloned.1.call-done = bf16[2816,1024]{1,0:T(8,128)(2,1)} async-done(((bf16[88,1024]{1,0:T(8,128)(2,1)}), bf16[2816,1024]{1,0:T(8,128)(2,1)}) %all-gather.26.cloned.1.call-update) | async-done | bytes 5767184 | tf_op jit(solution)/shard_map/all_gather | solution.py:61
  513.2 6.9 multiply_convert_fusion.2
  522.1 5.5 multiply_reduce_fusion
  533.6 7.6 multiply_convert_fusion
  543.3 2.0 multiply_convert_fusion.1
  545.3 3.9 copy.42
  549.3 4.4 convolution_convert_fusion
  553.7 4.0 copy.44
  557.8 3.9 fusion.4
  564.1 13.7 reduce-scatter.31.cloned.1.call-done
  577.7 3.4 convolution_add_fusion.1
  581.1 33.4 %reduce-scatter.33.cloned.1.call-done = bf16[128,1024]{1,0:T(8,128)(2,1)} async-done(((bf16[1024,1024]{1,0:T(8,128)(2,1)}), bf16[128,1024]{1,0:T(8,128)(2,1)}) %reduce-scatter.33.cloned.1.call-update) | async-done | bytes 262160
  614.5 2.8 fusion.19
  618.4 3.8 fusion.34
  622.3 2.8 fusion.25
  625.2 2.7 fusion.37
  628.0 2.8 fusion.39
  630.9 6.0 fusion.28
  638.0 5.9 fusion.51
  645.0 5.9 fusion.50
  650.9 4.3 fusion.6
  656.2 89.3 %reduce-scatter.35.cloned.1.call-done = f32[32,2]{1,0:T(8,128)} async-done(((f32[1024,2]{1,0:T(8,128)}), f32[32,2]{1,0:T(8,128)}) %reduce-scatter.35.cloned.1.call-update) | async-done | bytes 272
  747.6 140.5 %reduce-scatter.23.cloned.1.call-done = f32[32,1024]{1,0:T(8,128)} async-done(((f32[1024,1024]{1,0:T(8,128)}), f32[32,1024]{1,0:T(8,128)}) %reduce-scatter.23.cloned.1.call-update) | async-done | bytes 131088 | tf_op jit(solution)/shard_map/reduce_scatter | solution.py:232
  888.1 142.4 %reduce-scatter.17.cloned.1.call-done = f32[32,1024]{1,0:T(8,128)} async-done(((f32[1024,1024]{1,0:T(8,128)}), f32[32,1024]{1,0:T(8,128)}) %reduce-scatter.17.cloned.1.call-update) | async-done | bytes 131088 | tf_op jit(solution)/shard_map/reduce_scatter | solution.py:229
  1030.6 142.2 %reduce-scatter.21.cloned.1.call-done = f32[32,1024]{1,0:T(8,128)} async-done(((f32[1024,1024]{1,0:T(8,128)}), f32[32,1024]{1,0:T(8,128)}) %reduce-scatter.21.cloned.1.call-update) | async-done | bytes 131088 | tf_op jit(solution)/shard_map/reduce_scatter | solution.py:231
  1172.8 142.5 %reduce-scatter.19.cloned.1.call-done = f32[32,1024]{1,0:T(8,128)} async-done(((f32[1024,1024]{1,0:T(8,128)}), f32[32,1024]{1,0:T(8,128)}) %reduce-scatter.19.cloned.1.call-update) | async-done | bytes 131088 | tf_op jit(solution)/shard_map/reduce_scatter | solution.py:230
  1315.2 160.4 %reduce-scatter.29.cloned.1.call-done = f32[88,1024]{1,0:T(8,128)} async-done(((f32[2816,1024]{1,0:T(8,128)}), f32[88,1024]{1,0:T(8,128)}) %reduce-scatter.29.cloned.1.call-update) | async-done | bytes 360464 | tf_op jit(solution)/shard_map/reduce_scatter | solution.py:235
  1475.6 161.2 %reduce-scatter.27.cloned.1.call-done = f32[32,2816]{1,0:T(8,128)} async-done(((f32[1024,2816]{1,0:T(8,128)}), f32[32,2816]{1,0:T(8,128)}) %reduce-scatter.27.cloned.1.call-update) | async-done | bytes 360464 | tf_op jit(solution)/shard_map/reduce_scatter | solution.py:234
  1636.8 161.5 %reduce-scatter.25.cloned.1.call-done = f32[32,2816]{1,0:T(8,128)} async-done(((f32[1024,2816]{1,0:T(8,128)}), f32[32,2816]{1,0:T(8,128)}) %reduce-scatter.25.cloned.1.call-update) | async-done | bytes 360464 | tf_op jit(solution)/shard_map/reduce_scatter | solution.py:233
  (134 shorter events, 32.4 us)
Async XLA Ops:
  7.2 177.8 %copy-start.3 = (bf16[1,128,1024]{2,1,0:T(8,128)(2,1)S(1)}, bf16[1,128,1024]{2,1,0:T(8,128)(2,1)}, u32[]{:S(2)}) copy-start(bf16[1,128,1024]{2,1,0:T(8,128)(2,1)} %param.12) | copy-start | bytes 786436
  7.2 125.2 %copy-start.31 = (s32[1,4]{1,0:T(1,128)S(1)}, s32[1,4]{1,0:T(1,128)}, u32[]{:S(2)}) copy-start(s32[1,4]{1,0:T(1,128)} %param.14) | copy-start | bytes 52
  7.2 61.0 %all-gather.16.cloned.1.call-start = ((), (), s32[]{:S(2)}) async-start(), calls=%async_computation.13 | async-start | bytes 2162688 | tf_op jit(solution)/shard_map/all_gather | solution.py:55
  7.9 118.7 %all-gather.10.cloned.1.call-start = ((), (), s32[]{:S(2)}) async-start(), calls=%async_computation.10 | async-start | bytes 2162688 | tf_op jit(solution)/shard_map/all_gather | solution.py:56
  8.7 176.3 %all-gather.14.cloned.1.call-start = ((), (), s32[]{:S(2)}) async-start(), calls=%async_computation.12 | async-start | bytes 2162688 | tf_op jit(solution)/shard_map/all_gather | solution.py:54
  9.4 206.4 %all-gather.18.cloned.1.call-start = ((), (), s32[]{:S(2)}) async-start(), calls=%async_computation.14 | async-start | bytes 2359296 | tf_op jit(solution)/shard_map/all_gather | solution.py:84
  52.0 135.0 %copy-start.26 = (f32[128]{0:T(128)}, f32[128]{0:T(128)S(1)}, u32[]{:S(2)}) copy-start(f32[128]{0:T(128)S(1)} %add_rsqrt_fusion.1) | copy-start | bytes 1540
  71.2 175.3 %all-gather.12.cloned.1.call-start = ((), (), s32[]{:S(2)}) async-start(), calls=%async_computation.11 | async-start | bytes 2359296 | tf_op jit(solution)/shard_map/all_gather | solution.py:85
  129.5 175.0 %all-gather.20.cloned.1.call-start = ((), (), s32[]{:S(2)}) async-start(), calls=%async_computation.15 | async-start | bytes 2162688 | tf_op jit(solution)/shard_map/all_gather | solution.py:57
  130.1 244.8 %all-gather.24.cloned.1.call-start = ((), (), s32[]{:S(2)}) async-start(), calls=%async_computation.17 | async-start | bytes 5947392 | tf_op jit(solution)/shard_map/all_gather | solution.py:60
  130.8 313.2 %all-gather.22.cloned.1.call-start = ((), (), s32[]{:S(2)}) async-start(), calls=%async_computation.16 | async-start | bytes 5947392 | tf_op jit(solution)/shard_map/all_gather | solution.py:59
  131.6 381.7 %all-gather.26.cloned.1.call-start = ((), (), s32[]{:S(2)}) async-start(), calls=%async_computation.18 | async-start | bytes 5947392 | tf_op jit(solution)/shard_map/all_gather | solution.py:61
  132.3 445.4 %reduce-scatter.31.cloned.1.call-start = ((), (), s32[]{:S(2)}) async-start(), calls=%async_computation.26 | async-start | bytes 2359296
  252.0 3.6 copy-start.2
  252.0 3.5 copy-start.25
  252.1 5.5 copy-start.10
  255.6 2.0 copy-start.1
  259.9 46.7 %copy-start.16 = (bf16[128,16,64]{0,2,1:T(8,128)(2,1)}, bf16[128,16,64]{0,2,1:T(8,128)(2,1)S(1)}, u32[]{:S(2)}) copy-start(bf16[128,16,64]{0,2,1:T(8,128)(2,1)S(1)} %get-tuple-element.103) | copy-start | bytes 786436
  513.2 6.9 copy-start
  520.1 7.5 copy-start.12
  520.1 7.5 copy-start.14
  520.1 2.0 copy-start.30
  522.1 5.5 copy-start.21
  522.1 6.5 copy-start.7
  541.2 2.0 copy-start.4
  549.3 65.2 %reduce-scatter.33.cloned.1.call-start = ((), (), s32[]{:S(2)}) async-start(), calls=%async_computation.27 | async-start | bytes 2359296
  557.7 187.8 %reduce-scatter.35.cloned.1.call-start = ((), (), s32[]{:S(2)}) async-start(), calls=%async_computation.28 | async-start | bytes 540672
  557.8 4.7 copy-start.6
  561.7 52.8 %copy-start.5 = (bf16[1024,1024]{1,0:T(8,128)(2,1)S(1)}, bf16[1024,1024]{1,0:T(8,128)(2,1)}, u32[]{:S(2)}) copy-start(bf16[1024,1024]{1,0:T(8,128)(2,1)} %all-gather.10.cloned.1.call-done) | copy-start | bytes 6291460
  561.7 52.7 %copy-start.27 = (f32[128]{0:T(128)S(1)}, f32[128]{0:T(128)}, u32[]{:S(2)}) copy-start(f32[128]{0:T(128)} %copy-done.26) | copy-start | bytes 1540
  564.1 53.2 %copy-start.28 = (f32[1024]{0:T(1024)S(1)}, f32[1024]{0:T(1024)}, u32[]{:S(2)}) copy-start(f32[1024]{0:T(1024)} %get-tuple-element.75) | copy-start | bytes 12292
  564.1 54.4 %copy-start.17 = (bf16[128,16,64]{0,2,1:T(8,128)(2,1)S(1)}, bf16[128,16,64]{0,2,1:T(8,128)(2,1)}, u32[]{:S(2)}) copy-start(bf16[128,16,64]{0,2,1:T(8,128)(2,1)} %copy-done.16) | copy-start | bytes 786436
  618.4 3.9 copy-start.19
  618.4 269.8 %reduce-scatter.23.cloned.1.call-start = ((), (), s32[]{:S(2)}) async-start(), calls=%async_computation.22 | async-start | bytes 4325376 | tf_op jit(solution)/shard_map/reduce_scatter | solution.py:232
  622.2 2.9 copy-start.24
  622.3 408.3 %reduce-scatter.17.cloned.1.call-start = ((), (), s32[]{:S(2)}) async-start(), calls=%async_computation.19 | async-start | bytes 4325376 | tf_op jit(solution)/shard_map/reduce_scatter | solution.py:229
  625.1 2.9 copy-start.23
  625.1 547.6 %reduce-scatter.21.cloned.1.call-start = ((), (), s32[]{:S(2)}) async-start(), calls=%async_computation.21 | async-start | bytes 4325376 | tf_op jit(solution)/shard_map/reduce_scatter | solution.py:231
  628.0 2.9 copy-start.11
  628.0 2.9 copy-start.22
  628.0 687.2 %reduce-scatter.19.cloned.1.call-start = ((), (), s32[]{:S(2)}) async-start(), calls=%async_computation.20 | async-start | bytes 4325376 | tf_op jit(solution)/shard_map/reduce_scatter | solution.py:230
  630.8 844.7 %reduce-scatter.29.cloned.1.call-start = ((), (), s32[]{:S(2)}) async-start(), calls=%async_computation.25 | async-start | bytes 11894784 | tf_op jit(solution)/shard_map/reduce_scatter | solution.py:235
  636.9 1.1 copy-start.15
  636.9 999.9 %reduce-scatter.27.cloned.1.call-start = ((), (), s32[]{:S(2)}) async-start(), calls=%async_computation.24 | async-start | bytes 11894784 | tf_op jit(solution)/shard_map/reduce_scatter | solution.py:234
  643.9 1.1 copy-start.13
  643.9 1154.4 %reduce-scatter.25.cloned.1.call-start = ((), (), s32[]{:S(2)}) async-start(), calls=%async_computation.23 | async-start | bytes 11894784 | tf_op jit(solution)/shard_map/reduce_scatter | solution.py:233
  650.9 4.4 copy-start.9
  650.9 4.4 copy-start.20
  (3 other events, 2.0 us)
Sparse Core Ops, SparseCore 0:
  11.0 57.1 all-gather.15
  71.2 55.3 all-gather.9
  129.6 55.3 all-gather.13
  187.0 28.8 all-gather.17
  217.9 28.5 all-gather.11
  249.3 55.0 all-gather.19
  307.3 67.5 all-gather.23
  377.8 66.2 all-gather.21
  446.9 66.2 all-gather.25
  549.4 28.2 reduce-scatter.30
  580.0 34.4 reduce-scatter.32
  618.5 127.0 reduce-scatter.34
  748.5 139.5 reduce-scatter.22
  890.9 139.5 reduce-scatter.16
  1033.4 139.3 reduce-scatter.20
  1175.6 139.6 reduce-scatter.18
  1318.1 157.4 reduce-scatter.28
  1478.4 158.3 reduce-scatter.26
  1639.8 158.4 reduce-scatter.24
where the time goes:
time: 1820 us; the launch traced here: 1800 us
  waiting for transfers between devices  1610 us (88%)
  matrix products  99.4 us (5%)
  blocking collectives  39.8 us (2%)
  local copies, waits for them, and re-layouts  30.2 us (2%)
    reduce_scatter x1, waiting for transfers between devices, per_device(): lax.psum_scatter(grad_gate, ('dp', 'seq'), scatter_dimension=0, tiled=True)  162 us
    reduce_scatter x1, waiting for transfers between devices, per_device(): lax.psum_scatter(grad_up, ('dp', 'seq'), scatter_dimension=0, tiled=True)  161 us
    reduce_scatter x1, waiting for transfers between devices, per_device(): lax.psum_scatter(grad_down, ('dp', 'seq'), scatter_dimension=0, tiled=True)  160 us
    reduce_scatter x1, waiting for transfers between devices, per_device(): lax.psum_scatter(grad_key, ('dp', 'seq'), scatter_dimension=0, tiled=True)  142 us
    reduce_scatter x1, waiting for transfers between devices, per_device(): lax.psum_scatter(grad_query, ('dp', 'seq'), scatter_dimension=0, tiled=True)  142 us
    reduce_scatter x1, waiting for transfers between devices, per_device(): lax.psum_scatter(grad_value, ('dp', 'seq'), scatter_dimension=0, tiled=True)  142 us
    unnamed x22, waiting for transfers between devices  141 us
    reduce_scatter x1, waiting for transfers between devices, per_device(): lax.psum_scatter(grad_out_proj, ('dp', 'seq'), scatter_dimension=0, tiled...  141 us
  transfers between devices with their start and end apart: 19, of which 19 were waited for; matrix products, arithmetic and copies ran while one was open for 5% of the time, Pallas kernels for 0%

commit v1 on v0

--- a/solution.py
+++ b/solution.py
@@ -1,8 +1,11 @@
+import functools
 import math
 
 import jax
 import jax.numpy as jnp
 from jax import lax
+from jax.experimental import pallas as pl
+from jax.experimental.pallas import tpu as pltpu
 from jax.sharding import PartitionSpec as P
 
 HEADS = 16
@@ -249,9 +252,890 @@
     )
 
 
+MESH = pl.DeviceIdType.MESH
+BF = jnp.bfloat16
+F32 = jnp.float32
+DP, ZS, CORES = 4, 4, 2
+RANKS = DP * CORES
+
+
+def planes_fit(mesh):
+    return mesh.shape["dp"] == DP and mesh.shape["seq"] == ZS * CORES
+
+
+def dot_nn(left, right):
+    return jnp.dot(left, right, preferred_element_type=F32)
+
+
+def remote(src, dst, send_sem, recv_sem, device):
+    return pltpu.make_async_remote_copy(
+        src_ref=src,
+        dst_ref=dst,
+        send_sem=send_sem,
+        recv_sem=recv_sem,
+        device_id=device,
+        device_id_type=MESH,
+    )
+
+
+def wait_for(ref, sem):
+    pltpu.make_async_copy(ref, ref, sem).wait()
+
+
+def layer_kernel(
+    lat_in,
+    dout_in,
+    lens_in,
+    wqkv_in,
+    wgu_in,
+    wd_in,
+    wo_in,
+    lat_o,
+    dlat_o,
+    gqkv_o,
+    ggu_o,
+    gd_o,
+    go_o,
+    own_l,
+    lens,
+    n_one,
+    n_two,
+    cot,
+    gbr,
+    wqkv,
+    wgu,
+    wd,
+    wo,
+    qkv,
+    att,
+    att_f,
+    tot,
+    probs,
+    gsc,
+    part_a,
+    part_b,
+    part_c,
+    sib,
+    rcv,
+    hid,
+    ggu,
+    gatt,
+    graw_two,
+    q_two,
+    gqkv,
+    dwqkv,
+    dwgu,
+    dwd,
+    dwo,
+    zq,
+    zgu,
+    resid,
+    gres,
+    back,
+    tr_s,
+    tr_r,
+    ln_s,
+    ln_r,
+    wa_s,
+    wa_r,
+    wz_s,
+    wz_r,
+    wd_s,
+    wd_r,
+    wo_s,
+    wo_r,
+    ag_s,
+    ag_r,
+    ag_x,
+    rs_s,
+    rs_r,
+    rs_x,
+    gz_s,
+    gz_r,
+    ga_s,
+    ga_r,
+    gd_s,
+    gd_r,
+    go_s,
+    go_r,
+    tb_s,
+    tb_r,
+):
+    k = lax.axis_index("dp")
+    s = lax.axis_index("seq")
+    z = s // CORES
+    c = s % CORES
+    oc = 1 - c
+    rank = CORES * k + c
+
+    def dev(kk, zz, cc):
+        return (kk, CORES * zz + cc)
+
+    def peer(i):
+        return 2 * ((k // 2 + i // 2) % 2) + (k % 2 + i % 2) % 2
+
+    def zpeer(i):
+        return (z + i) % ZS
+
+    sibling = dev(k, z, oc)
+
+    barrier = pltpu.get_barrier_semaphore()
+    greeted = 0
+    for di in range(4):
+        for dz in range(4):
+            if di or dz:
+                pl.semaphore_signal(
+                    barrier, inc=1, device_id=dev(peer(di), zpeer(dz), c), device_id_type=MESH
+                )
+                greeted += 1
+            if di == 0 or dz == 0:
+                pl.semaphore_signal(
+                    barrier, inc=1, device_id=dev(peer(di), zpeer(dz), oc), device_id_type=MESH
+                )
+                greeted += 1
+    pl.semaphore_wait(barrier, greeted)
+
+    def spread(src, dst_of, which, start):
+        for q in range(4):
+            here = (k == q) & (z == k)
+            piece = src.at[pl.ds(32 * q, 32)]
+
+            @pl.when(here)
+            def _():
+                if start:
+                    pltpu.make_async_copy(piece, dst_of(q), tr_r.at[which, z]).start()
+
+            @pl.when(jnp.logical_not(here))
+            def _():
+                copy = remote(
+                    piece, dst_of(q), tr_s.at[which, q], tr_r.at[which, z], dev(q, k, c)
+                )
+                if start:
+                    copy.start()
+                else:
+                    copy.wait_send()
+
+    def spread_lat(start):
+        spread(lat_in, lambda q: own_l.at[z], 0, start)
+
+    def spread_cot(start):
+        spread(dout_in, lambda q: cot.at[q, z, c], 1, start)
+
+    def spread_lens(start):
+        here = z == k
+
+        @pl.when(here)
+        def _():
+            if start:
+                pltpu.make_async_copy(lens_in, lens, ln_r).start()
+
+        @pl.when(jnp.logical_not(here))
+        def _():
+            copy = remote(lens_in, lens, ln_s, ln_r, dev(z, k, c))
+            if start:
+                copy.start()
+            else:
+                copy.wait_send()
+
+    def plane_weights(src, dst, which, start):
+        for i in range(4):
+            for same in (True, False):
+                cc = c if same else oc
+                target = CORES * peer(i) + cc
+                piece = src.at[target]
+                place = dst.at[k, z, c]
+                if i == 0 and same:
+                    if start:
+                        pltpu.make_async_copy(piece, place, wa_r.at[which, rank]).start()
+                else:
+                    copy = remote(
+                        piece,
+                        place,
+                        wa_s.at[which, 2 * i + (0 if same else 1)],
+                        wa_r.at[which, rank],
+                        dev(peer(i), z, cc),
+                    )
+                    if start:
+                        copy.start()
+                    else:
+                        copy.wait_send()
+
+    def plane_weights_here(dst, which):
+        for kk in range(4):
+            for cc in range(2):
+                wait_for(dst.at[kk, z, cc], wa_r.at[which, CORES * kk + cc])
+
+    def line_weights(dst, which, start):
+        for i in range(1, 4):
+            copy = remote(
+                dst.at[:, z],
+                dst.at[:, z],
+                wz_s.at[which, i],
+                wz_r.at[which, z],
+                dev(k, zpeer(i), c),
+            )
+            if start:
+                copy.start()
+            else:
+                copy.wait_send()
+
+    def line_weights_here(dst, which):
+        for i in range(1, 4):
+            wait_for(dst.at[:, zpeer(i)], wz_r.at[which, zpeer(i)])
+
+    def down_weights(start):
+        for i in range(4):
+            if i == 0:
+                if start:
+                    pltpu.make_async_copy(wd_in, wd.at[z], wd_r.at[z]).start()
+            else:
+                copy = remote(wd_in, wd.at[z], wd_s.at[i], wd_r.at[z], dev(k, zpeer(i), c))
+                if start:
+                    copy.start()
+                else:
+                    copy.wait_send()
+
+    def out_weights(start):
+        to_core = z // 2
+        slot = 2 * (z % 2) + c
+        for i in range(4):
+
+            def send():
+                copy = remote(
+                    wo_in, wo.at[slot], wo_s.at[i], wo_r.at[slot], dev(k, zpeer(i), to_core)
+                )
+                if start:
+                    copy.start()
+                else:
+                    copy.wait_send()
+
+            if i == 0:
+
+                @pl.when(to_core == c)
+                def _():
+                    if start:
+                        pltpu.make_async_copy(wo_in, wo.at[slot], wo_r.at[slot]).start()
+
+                @pl.when(to_core != c)
+                def _():
+                    send()
+
+            else:
+                send()
+
+    def ag_send(buf, which):
+        own = buf.at[k, :, c]
+        for i in (1, 2, 3):
+            remote(
+                own, own, ag_s.at[which, i], ag_r.at[which, k], dev(peer(i), z, c)
+            ).start()
+        remote(own, own, ag_s.at[which, 4], ag_x.at[which, k], sibling).start()
+
+    def ag_relay(buf, which, i):
+        m = peer(i)
+        block = buf.at[m, :, c]
+        wait_for(block, ag_r.at[which, m])
+        remote(block, block, ag_s.at[which, 4 + i], ag_x.at[which, m], sibling).start()
+
+    def ag_other(buf, which, i):
+        m = peer(i)
+        wait_for(buf.at[m, :, oc], ag_x.at[which, m])
+
+    def ag_end(buf, which):
+        own = buf.at[k, :, c]
+        for i in (1, 2, 3):
+            remote(
+                own, own, ag_s.at[which, i], ag_r.at[which, k], dev(peer(i), z, c)
+            ).wait_send()
+        for i in range(4):
+            block = buf.at[peer(i), :, c]
+            remote(
+                block, block, ag_s.at[which, 4 + i], ag_x.at[which, peer(i)], sibling
+            ).wait_send()
+
+    def rs_copy(part, which, i):
+        m = peer(i)
+        return remote(
+            part.at[m, :, oc], sib.at[which, m], rs_s.at[which, i], rs_r.at[which, m], sibling
+        )
+
+    def rs_send_copy(part, which, i):
+        m = peer(i)
+        return remote(
+            part.at[m, :, c],
+            rcv.at[which, k],
+            rs_s.at[which, 4 + i],
+            rs_x.at[which, k],
+            dev(m, z, c),
+        )
+
+    def rs_pair(part, which, i):
+        m = peer(i)
+        wait_for(sib.at[which, m], rs_r.at[which, m])
+        return part[m, :, c].astype(F32) + sib[which, m].astype(F32)
+
+    def rs_forward(part, which):
+        for i in (3, 1, 2):
+            part[peer(i), :, c] = rs_pair(part, which, i).astype(BF)
+            rs_send_copy(part, which, i).start()
+
+    def rs_sum(part, which):
+        total = rs_pair(part, which, 0)
+        for i in (1, 2, 3):
+            m = peer(i)
+            wait_for(rcv.at[which, m], rs_x.at[which, m])
+            total = total + rcv[which, m].astype(F32)
+        return total.reshape(128, 1024)
+
+    def rs_end(part, which):
+        for i in range(4):
+            rs_copy(part, which, i).wait_send()
+        for i in (1, 2, 3):
+            rs_send_copy(part, which, i).wait_send()
+
+    spread_lat(True)
+    spread_lens(True)
+    plane_weights(wqkv_in, wqkv, 0, True)
+    spread_cot(True)
+    plane_weights(wgu_in, wgu, 1, True)
+    plane_weights_here(wqkv, 0)
+    line_weights(wqkv, 0, True)
+    for b in range(4):
+        wait_for(own_l.at[b], tr_r.at[0, b])
+    lat_f = own_l[...].reshape(128, 1024).astype(F32)
+    r_one = lax.rsqrt(jnp.mean(lat_f * lat_f, axis=-1, keepdims=True) + EPS)
+    n_one[k, :, c] = (lat_f * r_one).astype(BF).reshape(4, 32, 1024)
+    ag_send(n_one, 0)
+    out_weights(True)
+    plane_weights_here(wgu, 1)
+    line_weights(wgu, 1, True)
+    down_weights(True)
+    for b in range(4):
+        wait_for(cot.at[k, b, c], tr_r.at[1, b])
+    ag_send(cot, 1)
+
+    line_weights_here(wqkv, 0)
+
+    @pl.loop(0, 4)
+    def _(i):
+        @pl.when(i > 0)
+        def _():
+            ag_relay(n_one, 0, i)
+
+        ag_other(n_one, 0, i)
+        m = peer(i)
+        block = n_one[m].reshape(256, 1024)
+        out = dot_nn(block, wqkv[...].reshape(1024, 384))
+        qkv[:, m] = out.astype(BF).reshape(8, 32, 384)
+
+    wait_for(lens, ln_r)
+    lane = lax.broadcasted_iota(jnp.int32, (128, 128), 1)
+    row = lax.broadcasted_iota(jnp.int32, (128, 128), 0)
+    first = lane < 64
+
+    def two_heads(v):
+        zero = jnp.zeros_like(v)
+        return jnp.concatenate(
+            [jnp.where(first, v, zero), jnp.where(first, zero, v)], axis=0
+        )
+
+    def one_of_two(v):
+        return jnp.where(first, v[:128], v[128:])
+
+    def part_of(t0, t1, col):
+        return qkv[t0:t1, :, :, col * 128 : (col + 1) * 128].reshape((t1 - t0) * 128, 128)
+
+    for t in range(8):
+        span = (t + 1) * 128
+        q = two_heads(part_of(t, t + 1, 0).astype(F32) * 0.125).astype(BF)
+        keys = part_of(0, t + 1, 1)
+        vals = part_of(0, t + 1, 2)
+        pos = row + t * 128
+        begin = jnp.zeros((128, 128), jnp.int32)
+        end = jnp.zeros((1, 128), jnp.int32)
+        for g in range(4):
+            length = lens[g : g + 1, :]
+            end = end + length
+            begin = begin + jnp.where(end <= pos, length, 0)
+        allowed = []
+        for u in range(t + 1):
+            ok = begin <= lane + u * 128
+            if u == t:
+                ok = ok & (lane <= row)
+            allowed.append(ok)
+        allowed = jnp.concatenate(allowed, axis=1)
+        scores = dot_right(q, keys)
+        sums = []
+        raws = []
+        for h in range(2):
+            sc = jnp.where(allowed, scores[h * 128 : (h + 1) * 128], -1e30)
+            top = jnp.max(sc, axis=-1, keepdims=True)
+            expo = jnp.exp(sc - top)
+            low = expo.astype(BF)
+            probs[t, h * 128 : (h + 1) * 128, 0:span] = low
+            sums.append(jnp.sum(low.astype(F32), axis=-1, keepdims=True))
+        raw = dot_nn(probs[t, :, 0:span], vals)
+        both = jnp.where(first, sums[0], sums[1])
+        attended = one_of_two(raw) / both
+        tot[t] = both
+        att_f[t] = attended
+        att[:, t] = attended.astype(BF).reshape(4, 32, 128)
+
+    for i in (1, 2, 3):
+        ag_relay(cot, 1, i)
+    for slot in range(4):
+        wait_for(wo.at[slot], wo_r.at[slot])
+
+    @pl.loop(0, 4)
+    def _(j):
+        i = 3 - j
+        m = peer(i)
+        out = dot_nn(att[m].reshape(256, 128), wo[...].reshape(128, 1024))
+        part_a[m] = out.astype(BF).reshape(4, 2, 32, 1024)
+        rs_copy(part_a, 0, i).start()
+
+    rs_forward(part_a, 0)
+    res = own_l[...].reshape(128, 1024).astype(F32) + rs_sum(part_a, 0)
+    resid[...] = res
+    r_two = lax.rsqrt(jnp.mean(res * res, axis=-1, keepdims=True) + EPS)
+    n_two[k, :, c] = (res * r_two).astype(BF).reshape(4, 32, 1024)
+    ag_send(n_two, 2)
+
+    for i in range(4):
+        ag_other(cot, 1, i)
+    line_weights_here(wgu, 1)
+    for b in range(4):
+        wait_for(wd.at[b], wd_r.at[b])
+
+    @pl.loop(0, 4)
+    def _(i):
+        @pl.when(i > 0)
+        def _():
+            ag_relay(n_two, 2, i)
+
+        ag_other(n_two, 2, i)
+        m = peer(i)
+        gu = dot_nn(n_two[m].reshape(256, 1024), wgu[...].reshape(1024, 768))
+        gate = gu[:, :384]
+        up = gu[:, 384:]
+        sig = jax.nn.sigmoid(gate)
+        active = gate * sig
+        hid[m] = (active * up).astype(BF)
+        g_hid = dot_right(cot[m].reshape(256, 1024), wd[...].reshape(384, 1024))
+        ggu[m, :, :384] = (g_hid * up * sig * (1.0 + gate * (1.0 - sig))).astype(BF)
+        ggu[m, :, 384:] = (g_hid * active).astype(BF)
+        out = dot_right(ggu[m], wgu[...].reshape(1024, 768))
+        part_b[m] = out.astype(BF).reshape(4, 2, 32, 1024)
+        rs_copy(part_b, 1, i).start()
+
+    rs_forward(part_b, 1)
+
+    @pl.loop(0, 4)
+    def _(i):
+        m = peer(i)
+        out = dot_nn(hid[m], wd[...].reshape(384, 1024))
+        part_c[m] = out.astype(BF).reshape(4, 2, 32, 1024)
+        rs_copy(part_c, 2, i).start()
+
+    scaled = rs_sum(part_b, 1)
+    res = resid[...]
+    r_two = lax.rsqrt(jnp.mean(res * res, axis=-1, keepdims=True) + EPS)
+    normed = res * r_two
+    inner = jnp.mean(scaled * normed, axis=-1, keepdims=True)
+    g_res = cot[k, :, c].reshape(128, 1024).astype(F32) + r_two * (scaled - normed * inner)
+    gres[...] = g_res
+    gbr[k, :, c] = g_res.astype(BF).reshape(4, 32, 1024)
+    ag_send(gbr, 3)
+    rs_forward(part_c, 2)
+
+    @pl.loop(0, 4)
+    def _(d):
+        cols = pl.ds(pl.multiple_of(d * 256, 256), 256)
+        left = n_two[:, :, :, :, cols].reshape(1024, 256)
+        out = dot_left(left, ggu[...].reshape(1024, 768))
+        dwgu[d] = out.astype(BF).reshape(4, 2, 32, 768)
+
+    def line_grads(grad, land, which, start):
+        for i in range(1, 4):
+            copy = remote(
+                grad.at[:, zpeer(i)],
+                land.at[z],
+                gz_s.at[which, i],
+                gz_r.at[which, z],
+                dev(k, zpeer(i), c),
+            )
+            if start:
+                copy.start()
+            else:
+                copy.wait_send()
+
+    line_grads(dwgu, zgu, 1, True)
+
+    @pl.loop(0, 4)
+    def _(n):
+        cols = pl.ds(pl.multiple_of(n * 256, 256), 256)
+        right = cot[:, :, :, :, cols].reshape(1024, 256)
+        out = dot_left(hid[...].reshape(1024, 384), right)
+        dwd[:, :, cols] = out.astype(BF).reshape(4, 96, 256)
+
+    def down_grads(start):
+        for i in range(4):
+            src = dwd.at[zpeer(i)]
+            if i == 0:
+                if start:
+                    pltpu.make_async_copy(src, gd_o.at[z], gd_r.at[z]).start()
+            else:
+                copy = remote(src, gd_o.at[z], gd_s.at[i], gd_r.at[z], dev(k, zpeer(i), c))
+                if start:
+                    copy.start()
+                else:
+                    copy.wait_send()
+
+    down_grads(True)
+
+    @pl.loop(0, 4)
+    def _(i):
+        @pl.when(i > 0)
+        def _():
+            ag_relay(gbr, 3, i)
+
+        ag_other(gbr, 3, i)
+        m = peer(i)
+        out = dot_right(gbr[m].reshape(256, 1024), wo[...].reshape(128, 1024))
+        gatt[:, m] = out.astype(BF).reshape(8, 32, 128)
+
+    for t in range(8):
+        span = (t + 1) * 128
+        keys = part_of(0, t + 1, 1)
+        vals = part_of(0, t + 1, 2)
+        ratio = gatt[t].reshape(128, 128).astype(F32) / tot[t]
+        g_raw = two_heads(ratio.astype(BF).astype(F32)).astype(BF)
+        graw_two[t] = g_raw
+        q_two[t] = two_heads(part_of(t, t + 1, 0).astype(F32)).astype(BF)
+        prod = ratio * att_f[t]
+        g_tot = -jnp.sum(two_heads(prod), axis=-1, keepdims=True)
+        g_pr = dot_right(g_raw, vals)
+        g_sc = probs[t, :, 0:span].astype(F32) * (g_pr + g_tot)
+        gsc[t, :, 0:span] = g_sc.astype(BF)
+        g_q = one_of_two(dot_nn(gsc[t, :, 0:span], keys)) * 0.125
+        gqkv[:, t, :, 0:128] = g_q.astype(BF).reshape(4, 32, 128)
+    for u in range(8):
+        cols = slice(u * 128, (u + 1) * 128)
+        rows = (8 - u) * 256
+        g_k = dot_left(gsc[u:, :, cols].reshape(rows, 128), q_two[u:].reshape(rows, 128)) * 0.125
+        g_v = dot_left(probs[u:, :, cols].reshape(rows, 128), graw_two[u:].reshape(rows, 128))
+        gqkv[:, u, :, 128:256] = g_k.astype(BF).reshape(4, 32, 128)
+        gqkv[:, u, :, 256:384] = g_v.astype(BF).reshape(4, 32, 128)
+
+    rs_end(part_a, 0)
+
+    @pl.loop(0, 4)
+    def _(j):
+        i = 3 - j
+        m = peer(i)
+        out = dot_right(gqkv[m].reshape(256, 384), wqkv[...].reshape(1024, 384))
+        part_a[m] = out.astype(BF).reshape(4, 2, 32, 1024)
+        rs_copy(part_a, 3, i).start()
+
+    rs_forward(part_a, 3)
+
+    @pl.loop(0, 4)
+    def _(d):
+        cols = pl.ds(pl.multiple_of(d * 256, 256), 256)
+        left = n_one[:, :, :, :, cols].reshape(1024, 256)
+        out = dot_left(left, gqkv[...].reshape(1024, 384))
+        dwqkv[d] = out.astype(BF).reshape(4, 2, 32, 384)
+
+    line_grads(dwqkv, zq, 0, True)
+
+    @pl.loop(0, 4)
+    def _(n):
+        cols = pl.ds(pl.multiple_of(n * 256, 256), 256)
+        right = gbr[:, :, :, :, cols].reshape(1024, 256)
+        out = dot_left(att[...].reshape(1024, 128), right)
+        dwo[:, :, cols] = out.astype(BF).reshape(4, 32, 256)
+
+    def out_grads(start):
+        for p in range(2):
+            for cs in range(2):
+                zz = 2 * c + p
+                here = (zz == z) & (c == cs)
+                src = dwo.at[2 * p + cs]
+
+                @pl.when(here)
+                def _():
+                    if start:
+                        pltpu.make_async_copy(src, go_o.at[z], go_r.at[z]).start()
+
+                @pl.when(jnp.logical_not(here))
+                def _():
+                    copy = remote(
+                        src, go_o.at[z], go_s.at[2 * p + cs], go_r.at[z], dev(k, zz, cs)
+                    )
+                    if start:
+                        copy.start()
+                    else:
+                        copy.wait_send()
+
+    out_grads(True)
+
+    def gather_back(which, dst, start):
+        for b in range(4):
+            here = (z == k) & (z == b)
+            src = back.at[which, b]
+            place = dst.at[pl.ds(pl.multiple_of(32 * k, 32), 32)]
+
+            @pl.when(here)
+            def _():
+                if start:
+                    pltpu.make_async_copy(src, place, tb_r.at[which, k]).start()
+
+            @pl.when(jnp.logical_not(here))
+            def _():
+                copy = remote(src, place, tb_s.at[which, b], tb_r.at[which, k], dev(z, b, c))
+                if start:
+                    copy.start()
+                else:
+                    copy.wait_send()
+
+    out_f = resid[...] + rs_sum(part_c, 2)
+    back[0] = out_f.astype(BF).reshape(4, 32, 1024)
+    gather_back(0, lat_o, True)
+
+    def line_sum(grad, land, which):
+        total = grad[:, z].astype(F32)
+        for i in range(1, 4):
+            wait_for(land.at[zpeer(i)], gz_r.at[which, zpeer(i)])
+            total = total + land[zpeer(i)].astype(F32)
+        land[z] = total.astype(BF)
+
+    def plane_grads(land, dst, which, start):
+        for i in range(4):
+            m = peer(i)
+            for same in (True, False):
+                cc = c if same else oc
+                src = land.at[z, m, cc]
+                place = dst.at[rank]
+                if i == 0 and same:
+                    if start:
+                        pltpu.make_async_copy(src, place, ga_r.at[which, rank]).start()
+                else:
+                    copy = remote(
+                        src,
+                        place,
+                        ga_s.at[which, 2 * i + (0 if same else 1)],
+                        ga_r.at[which, rank],
+                        dev(m, z, cc),
+                    )
+                    if start:
+                        copy.start()
+                    else:
+                        copy.wait_send()
+
+    line_sum(dwgu, zgu, 1)
+    plane_grads(zgu, ggu_o, 1, True)
+
+    scaled = rs_sum(part_a, 3)
+    lat_f = own_l[...].reshape(128, 1024).astype(F32)
+    r_one = lax.rsqrt(jnp.mean(lat_f * lat_f, axis=-1, keepdims=True) + EPS)
+    normed = lat_f * r_one
+    inner = jnp.mean(scaled * normed, axis=-1, keepdims=True)
+    d_lat = gres[...] + r_one * (scaled - normed * inner)
+    back[1] = d_lat.astype(BF).reshape(4, 32, 1024)
+    gather_back(1, dlat_o, True)
+
+    line_sum(dwqkv, zq, 0)
+    plane_grads(zq, gqkv_o, 0, True)
+
+    for b in range(4):
+        wait_for(gd_o.at[b], gd_r.at[b])
+        wait_for(go_o.at[b], go_r.at[b])
+        for which, dst in ((0, lat_o), (1, dlat_o)):
+            wait_for(dst.at[pl.ds(32 * b, 32)], tb_r.at[which, b])
+    for r in range(RANKS):
+        wait_for(gqkv_o.at[r], ga_r.at[0, r])
+        wait_for(ggu_o.at[r], ga_r.at[1, r])
+    spread_lat(False)
+    spread_cot(False)
+    spread_lens(False)
+    plane_weights(wqkv_in, wqkv, 0, False)
+    plane_weights(wgu_in, wgu, 1, False)
+    line_weights(wqkv, 0, False)
+    line_weights(wgu, 1, False)
+    down_weights(False)
+    out_weights(False)
+    for which, buf in enumerate((n_one, cot, n_two, gbr)):
+        ag_end(buf, which)
+    rs_end(part_b, 1)
+    rs_end(part_c, 2)
+    rs_end(part_a, 3)
+    line_grads(dwgu, zgu, 1, False)
+    line_grads(dwqkv, zq, 0, False)
+    plane_grads(zgu, ggu_o, 1, False)
+    plane_grads(zq, gqkv_o, 0, False)
+    down_grads(False)
+    out_grads(False)
+    gather_back(0, lat_o, False)
+    gather_back(1, dlat_o, False)
+
+
+def run_layer(lat, dout, lens, wqkv_src, wgu_src, wd_src, wo_src):
+    vm = pltpu.VMEM
+    dma = pltpu.SemaphoreType.DMA
+    rows = (4, 4, 2, 32)
+    return pl.pallas_call(
+        layer_kernel,
+        out_shape=(
+            jax.ShapeDtypeStruct((128, 1024), BF),
+            jax.ShapeDtypeStruct((128, 1024), BF),
+            jax.ShapeDtypeStruct((RANKS, 32, 384), BF),
+            jax.ShapeDtypeStruct((RANKS, 32, 768), BF),
+            jax.ShapeDtypeStruct((4, 96, 1024), BF),
+            jax.ShapeDtypeStruct((4, 32, 1024), BF),
+        ),
+        in_specs=[pl.BlockSpec(memory_space=pl.ANY)] * 7,
+        out_specs=[pl.BlockSpec(memory_space=pl.ANY)] * 6,
+        scratch_shapes=[
+            vm((4, 32, 1024), BF),
+            vm((8, 128), jnp.int32),
+            vm(rows + (1024,), BF),
+            vm(rows + (1024,), BF),
+            vm(rows + (1024,), BF),
+            vm(rows + (1024,), BF),
+            vm(rows + (384,), BF),
+            vm(rows + (768,), BF),
+            vm((4, 96, 1024), BF),
+            vm((4, 32, 1024), BF),
+            vm((8, 4, 32, 384), BF),
+            vm((4, 8, 32, 128), BF),
+            vm((8, 128, 128), F32),
+            vm((8, 128, 128), F32),
+            vm((8, 256, 1024), BF),
+            vm((8, 256, 1024), BF),
+            vm(rows + (1024,), BF),
+            vm(rows + (1024,), BF),
+            vm(rows + (1024,), BF),
+            vm((4, 4, 4, 32, 1024), BF),
+            vm((4, 4, 4, 32, 1024), BF),
+            vm((4, 256, 384), BF),
+            vm((4, 256, 768), BF),
+            vm((8, 4, 32, 128), BF),
+            vm((8, 256, 128), BF),
+            vm((8, 256, 128), BF),
+            vm((4, 8, 32, 384), BF),
+            vm(rows + (384,), BF),
+            vm(rows + (768,), BF),
+            vm((4, 96, 1024), BF),
+            vm((4, 32, 1024), BF),
+            vm((4, 4, 2, 32, 384), BF),
+            vm((4, 4, 2, 32, 768), BF),
+            vm((128, 1024), F32),
+            vm((128, 1024), F32),
+            vm((2, 4, 32, 1024), BF),
+            dma((2, 4)),
+            dma((2, 4)),
+            dma,
+            dma,
+            dma((2, 8)),
+            dma((2, 8)),
+            dma((2, 4)),
+            dma((2, 4)),
+            dma((4,)),
+            dma((4,)),
+            dma((4,)),
+            dma((4,)),
+            dma((4, 8)),
+            dma((4, 4)),
+            dma((4, 4)),
+            dma((4, 8)),
+            dma((4, 4)),
+            dma((4, 4)),
+            dma((2, 4)),
+            dma((2, 4)),
+            dma((2, 8)),
+            dma((2, 8)),
+            dma((4,)),
+            dma((4,)),
+            dma((4,)),
+            dma((4,)),
+            dma((2, 4)),
+            dma((2, 4)),
+        ],
+        compiler_params=pltpu.CompilerParams(
+            collective_id=0, has_side_effects=True, vmem_limit_bytes=60 * 1024 * 1024
+        ),
+    )(lat, dout, lens, wqkv_src, wgu_src, wd_src, wo_src)
+
+
+def plane_device(
+    latents,
+    d_out,
+    lengths,
+    gain_attn,
+    w_query,
+    w_key,
+    w_value,
+    w_out,
+    gain_ffn,
+    w_gate,
+    w_up,
+    w_down,
+):
+    gain_one = gain_attn.astype(F32)[:, None]
+    gain_two = gain_ffn.astype(F32)[:, None]
+
+    def heads_of(w):
+        return (w.astype(F32) * gain_one).astype(BF).reshape(32, RANKS, 128)
+
+    wqkv_src = jnp.concatenate(
+        [heads_of(w) for w in (w_query, w_key, w_value)], axis=-1
+    ).transpose(1, 0, 2)
+
+    def units_of(w):
+        w = (w.astype(F32) * gain_two).astype(BF).reshape(32, DP, ZS, CORES, 88)
+        w = jnp.pad(w, ((0, 0), (0, 0), (0, 0), (0, 0), (0, 8)))
+        return w.transpose(1, 3, 0, 2, 4).reshape(RANKS, 32, 384)
+
+    wgu_src = jnp.concatenate([units_of(w_gate), units_of(w_up)], axis=-1)
+    wd_src = jnp.pad(w_down, ((0, 8), (0, 0)))
+    lens = jnp.broadcast_to(jnp.pad(lengths[0], (0, 4))[:, None], (8, 128))
+    lat_o, dlat_o, gqkv, ggu, gd, go = run_layer(
+        latents[0], d_out[0], lens, wqkv_src, wgu_src, wd_src, w_out
+    )
+
+    def rows_of(g):
+        return g.astype(F32).transpose(1, 0, 2).reshape(32, 1024)
+
+    def units_back(g):
+        g = g.astype(F32).reshape(DP, CORES, 32, ZS, 96)[..., :88]
+        return g.transpose(2, 0, 3, 1, 4).reshape(32, 2816)
+
+    n_q, n_k, n_v = (rows_of(gqkv[:, :, i * 128 : (i + 1) * 128]) for i in range(3))
+    n_g, n_u = units_back(ggu[:, :, :384]), units_back(ggu[:, :, 384:])
+    g_gain_one = jnp.sum(
+        n_q * w_query.astype(F32) + n_k * w_key.astype(F32) + n_v * w_value.astype(F32), axis=1
+    )
+    g_gain_two = jnp.sum(n_g * w_gate.astype(F32) + n_u * w_up.astype(F32), axis=1)
+    g_out = jnp.sum(go.astype(F32), axis=0)
+    g_down = jnp.sum(gd.astype(F32), axis=0)[:88]
+    return (
+        lat_o[None],
+        dlat_o[None],
+        g_gain_one,
+        n_q * gain_one,
+        n_k * gain_one,
+        n_v * gain_one,
+        g_out,
+        g_gain_two,
+        n_g * gain_two,
+        n_u * gain_two,
+        g_down,
+    )
+
+
 def solution(mesh):
     return jax.shard_map(
-        per_device,
+        plane_device if planes_fit(mesh) else per_device,
         mesh=mesh,
         in_specs=(
             P("dp", "seq", None),

time: 1820 us -> 243 us (0.13)
  waiting for transfers between devices: 1610 us -> 0 us
  Pallas kernels: 0 us -> 220 us
  matrix products: 99.4 us -> 0 us
  blocking collectives: 39.8 us -> 0 us
  local copies, waits for them, and re-layouts: 30.2 us -> 9.91 us
    reduce_scatter x7 -> x0, waiting for transfers between devices: 1050 us -> none  [the longest x1 162 us: per_device(): lax.psum_scatter(grad_gate, ('dp', 'seq'), scatter_dimension=0, tiled=True)]
    all_gather x9 -> x0, waiting for transfers between devices: 421 us -> none  [the longest x1 67.7 us: per_device(): lax.all_gather(w_up, ('dp', 'seq'), axis=0, tiled=True)]
    pallas_call x0 -> x1, Pallas kernels: none -> 220 us  [run_layer(): pl.pallas_call(layer_kernel, out_shape=(jax.ShapeDtypeStruct((128, 1024),...]
    unnamed x22 -> x0, waiting for transfers between devices: 141 us -> none
    dot_general x27 -> x0, matrix products: 99.4 us -> none  [the longest x7 29.8 us: dot_left(): lax.dot_general(left, right, (((0,), (0,)), ((), ())), preferred_element_...]
    unnamed x1 -> x0, blocking collectives: 39.8 us -> none
    unnamed x73 -> x20, local copies, waits for them, and re-layouts: 20.4 us -> 1.55 us
  transfers between devices with their start and end apart: 19 -> 0, of which waited for: 19 -> 0; matrix products, arithmetic and copies ran while one was open for 5% -> 0% of each run, Pallas kernels for 0% -> 0%
where the time goes in v1:
time: 243 us; the launch traced here: 241 us
  Pallas kernels  220 us (91%)
  other arithmetic  10.1 us (4%)
  local copies, waits for them, and re-layouts  9.91 us (4%)
    pallas_call x1, Pallas kernels, run_layer(): pl.pallas_call(layer_kernel, out_shape=(jax.ShapeDtypeStruct((128, 1024),...  220 us

profile of v1, /device:TPU:9, one launch (start us, length us, event | category | flops | bytes accessed | tf_op | source)
XLA Modules:
  0.0 241.1 jit_solution(15433388936712236579)
XLA Ops:
  0.6 0.7 convert_element_type.58
  1.3 0.7 convert_element_type.65
  2.0 0.7 pad.15
  2.6 0.0 copy-start
  2.6 0.0 copy-start.1
  2.6 0.7 broadcast_in_dim.6.lens_in
  3.3 1.6 pad.18.wd_in
  4.9 1.0 fusion.12
  6.0 0.7 maximum_bitcast_fusion.wqkv_in
  6.7 0.0 copy-done
  6.7 0.0 copy-done.1
  6.7 0.1 fusion
  6.8 0.6 reshape.87
  7.4 0.1 copy.30
  7.5 0.1 pad_bitcast_fusion.1
  7.6 0.2 reshape.88
  7.8 0.6 reshape.89
  8.4 0.1 copy.31
  8.5 0.1 pad_bitcast_fusion
  8.7 0.2 reshape.90
  8.9 0.8 pad_maximum_fusion.wgu_in
  9.7 220.2 %shard_map.203 = (bf16[128,1024]{1,0:T(8,128)(2,1)}, bf16[128,1024]{1,0:T(8,128)(2,1)}, bf16[8,32,384]{2,1,0:T(8,128)(2,1)}, bf16[8,32,768]{2,1,0:T(8,128)(2,1)}...) custom-call(bf16[128,1024]{1,0:T(8,128)(2,1)} %bitcast.49, bf16[128,1024]{1,0:T(8,128)(2,1)} %bitcast.50, ...), custom_call_target="tpu_custom_call" | custom-call | tf_op jit(solution)/shard_map/pallas_call | solution.py:986
  229.9 1.7 convert_reduce_fusion.1
  231.6 0.0 copy-start.8
  231.6 1.3 convert_reduce_fusion
  232.9 0.0 copy-start.5
  232.9 0.0 copy-start.6
  232.9 0.0 copy-start.7
  232.9 0.8 slice.36
  233.7 0.0 copy-done.8
  233.7 0.0 copy-start.2
  233.7 0.0 copy-done.5
  233.8 0.0 copy-done.6
  233.8 0.1 copy-done.7
  233.9 1.4 bitcast_multiply_fusion
  235.3 0.0 copy-done.2
  235.3 0.2 reshape.100
  235.6 0.4 copy.36
  236.0 0.7 reshape.112
  236.7 0.2 reshape.97
  236.9 0.4 copy.35
  237.4 0.7 reshape.110
  238.1 0.0 copy-start.3
  238.1 1.6 broadcast_multiply_fusion
  239.7 0.0 copy-done.4
  239.7 0.7 copy.55
  240.4 0.0 copy-done.3
  240.4 0.7 copy.56
  (7 shorter events, 0.2 us)
Async XLA Ops:
  2.6 4.1 %copy-start = (bf16[32,2816]{1,0:T(8,128)(2,1)S(1)}, bf16[32,2816]{1,0:T(8,128)(2,1)}, u32[]{:S(2)}) copy-start(bf16[32,2816]{1,0:T(8,128)(2,1)} %param.21) | copy-start | bytes 540676
  2.6 4.1 %copy-start.1 = (bf16[32,2816]{1,0:T(8,128)(2,1)S(1)}, bf16[32,2816]{1,0:T(8,128)(2,1)}, u32[]{:S(2)}) copy-start(bf16[32,2816]{1,0:T(8,128)(2,1)} %param.22) | copy-start | bytes 540676
  231.6 2.1 copy-start.8
  232.9 0.8 copy-start.5
  232.9 0.9 copy-start.6
  232.9 0.9 copy-start.7
  233.7 1.6 copy-start.2
  238.1 1.6 copy-start.4
  238.1 2.3 copy-start.3

commit v2 on v1

--- a/solution.py
+++ b/solution.py
@@ -282,13 +282,23 @@
     pltpu.make_async_copy(ref, ref, sem).wait()
 
 
+def on_diagonal(row):
+    at = lax.broadcasted_iota(jnp.int32, (32, 32), 0) == lax.broadcasted_iota(jnp.int32, (32, 32), 1)
+    return jnp.where(at, row.astype(F32), 0.0)
+
+
 def layer_kernel(
     lat_in,
     dout_in,
-    lens_in,
-    wqkv_in,
-    wgu_in,
-    wd_in,
+    lengths_in,
+    gain_one,
+    gain_two,
+    wq_raw,
+    wk_raw,
+    wv_raw,
+    wg_raw,
+    wu_raw,
+    wd_raw,
     wo_in,
     lat_o,
     dlat_o,
@@ -296,7 +306,12 @@
     ggu_o,
     gd_o,
     go_o,
+    lens_in,
+    wqkv_in,
+    wgu_in,
+    wd_in,
     own_l,
+    stop,
     lens,
     n_one,
     n_two,
@@ -317,8 +332,10 @@
     part_c,
     sib,
     rcv,
+    turn,
     hid,
     ggu,
+    slope,
     gatt,
     graw_two,
     q_two,
@@ -329,32 +346,40 @@
     dwo,
     zq,
     zgu,
+    zd,
+    xq,
+    xgu,
+    xd,
+    down_sum,
     resid,
     gres,
     back,
     tr_s,
     tr_r,
+    tx_r,
+    tz_s,
     ln_s,
     ln_r,
     wa_s,
     wa_r,
     wz_s,
     wz_r,
-    wd_s,
     wd_r,
     wo_s,
     wo_r,
     ag_s,
     ag_r,
     ag_x,
+    ag_d,
     rs_s,
     rs_r,
     rs_x,
+    rs_d,
     gz_s,
     gz_r,
+    gx_r,
     ga_s,
     ga_r,
-    gd_s,
     gd_r,
     go_s,
     go_r,
@@ -393,33 +418,92 @@
                     barrier, inc=1, device_id=dev(peer(di), zpeer(dz), oc), device_id_type=MESH
                 )
                 greeted += 1
+
+    def scaled_rows(w, gain):
+        return dot_nn(on_diagonal(gain[...]).astype(BF), w[...])
+
+    for i, w in enumerate((wq_raw, wk_raw, wv_raw)):
+        rows = scaled_rows(w, gain_one).astype(BF)
+        for r in range(RANKS):
+            wqkv_in[r, :, i * 128 : (i + 1) * 128] = rows[:, r * 128 : (r + 1) * 128]
+    wd_in[0:80] = wd_raw[0:80]
+    wd_in[80:96] = jnp.concatenate([wd_raw[80:88], jnp.zeros((8, 1024), BF)], axis=0)
+    tile_row = lax.broadcasted_iota(jnp.int32, (8, 128), 0)
+    tile = jnp.zeros((8, 128), jnp.int32)
+    for i in range(4):
+        tile = jnp.where(tile_row == i, lengths_in[0, i], tile)
+    lens_in[...] = tile
+
+    def units_to_ranks():
+        for i, w in enumerate((wg_raw, wu_raw)):
+            rows = scaled_rows(w, gain_two)
+            gap = jnp.zeros((32, 8), F32)
+            for r in range(RANKS):
+                parts = []
+                for b in range(ZS):
+                    at = 88 * (8 * (r // CORES) + CORES * b + r % CORES)
+                    parts += [rows[:, at : at + 88], gap]
+                wgu_in[r, :, i * 384 : (i + 1) * 384] = jnp.concatenate(parts, axis=1).astype(BF)
+
     pl.semaphore_wait(barrier, greeted)
 
-    def spread(src, dst_of, which, start):
+    def spread(src, final_of, which, start):
         for q in range(4):
-            here = (k == q) & (z == k)
             piece = src.at[pl.ds(32 * q, 32)]
 
-            @pl.when(here)
+            @pl.when((z == k) & (k == q))
             def _():
                 if start:
-                    pltpu.make_async_copy(piece, dst_of(q), tr_r.at[which, z]).start()
-
-            @pl.when(jnp.logical_not(here))
+                    pltpu.make_async_copy(piece, final_of(q, z), tr_r.at[which, z]).start()
+
+            @pl.when((z == k) & (k != q))
             def _():
                 copy = remote(
-                    piece, dst_of(q), tr_s.at[which, q], tr_r.at[which, z], dev(q, k, c)
+                    piece, final_of(q, z), tr_s.at[which, q], tr_r.at[which, z], dev(q, z, c)
                 )
                 if start:
                     copy.start()
                 else:
                     copy.wait_send()
 
-    def spread_lat(start):
-        spread(lat_in, lambda q: own_l.at[z], 0, start)
-
-    def spread_cot(start):
-        spread(dout_in, lambda q: cot.at[q, z, c], 1, start)
+            @pl.when((z != k) & (k != q))
+            def _():
+                copy = remote(
+                    piece, stop.at[which, k], tr_s.at[which, q], tx_r.at[which, k], dev(q, z, c)
+                )
+                if start:
+                    copy.start()
+                else:
+                    copy.wait_send()
+
+    def spread_on(src, final_of, which, start):
+        for i in range(1, 4):
+            g = zpeer(i)
+
+            def send(piece):
+                copy = remote(
+                    piece, final_of(k, z), tz_s.at[which, i], tr_r.at[which, z], dev(k, g, c)
+                )
+                if start:
+                    copy.start()
+                else:
+                    copy.wait_send()
+
+            @pl.when(g == k)
+            def _():
+                send(src.at[pl.ds(pl.multiple_of(32 * k, 32), 32)])
+
+            @pl.when(g != k)
+            def _():
+                if start:
+                    wait_for(stop.at[which, g], tx_r.at[which, g])
+                send(stop.at[which, g])
+
+    def lat_place(q, b):
+        return own_l.at[b]
+
+    def cot_place(q, b):
+        return cot.at[q, b, c]
 
     def spread_lens(start):
         here = z == k
@@ -465,35 +549,72 @@
             for cc in range(2):
                 wait_for(dst.at[kk, z, cc], wa_r.at[which, CORES * kk + cc])
 
-    def line_weights(dst, which, start):
-        for i in range(1, 4):
-            copy = remote(
-                dst.at[:, z],
-                dst.at[:, z],
-                wz_s.at[which, i],
-                wz_r.at[which, z],
-                dev(k, zpeer(i), c),
-            )
-            if start:
-                copy.start()
-            else:
-                copy.wait_send()
-
-    def line_weights_here(dst, which):
-        for i in range(1, 4):
-            wait_for(dst.at[:, zpeer(i)], wz_r.at[which, zpeer(i)])
-
-    def down_weights(start):
-        for i in range(4):
-            if i == 0:
-                if start:
-                    pltpu.make_async_copy(wd_in, wd.at[z], wd_r.at[z]).start()
-            else:
-                copy = remote(wd_in, wd.at[z], wd_s.at[i], wd_r.at[z], dev(k, zpeer(i), c))
+    middle = (z == 1) | (z == 2)
+    near = (1 + z % 2, 2 + z // 2 - 2 * (z % 2))
+    z_end = 3 * (z // 2)
+
+    def far_of(place):
+        return (3 - place, 6 - 3 * place)
+
+    far = far_of(z)
+
+    def line_copy(block, which, slot, b, place, src=None):
+        src = block(b) if src is None else src
+        return remote(src, block(b), wz_s.at[which, slot], wz_r.at[which, b], dev(k, place, c))
+
+    def line_send(block, which, from_ends, from_middle, start=True, src=None):
+        def send(slots):
+            for j in slots:
+                copy = line_copy(block, which, j, z, near[j], src)
                 if start:
                     copy.start()
                 else:
                     copy.wait_send()
+
+        if from_ends:
+
+            @pl.when(jnp.logical_not(middle))
+            def _():
+                send(from_ends)
+
+        if from_middle:
+
+            @pl.when(middle)
+            def _():
+                send(from_middle)
+
+    def line_relay(block, which, j):
+        @pl.when(middle)
+        def _():
+            wait_for(block(far[j]), wz_r.at[which, far[j]])
+            line_copy(block, which, 2 + j, far[j], z_end).start()
+
+    def line_sent(block, which, src=None):
+        line_send(block, which, (0, 1), (0, 1), False, src)
+
+        @pl.when(middle)
+        def _():
+            for j in range(2):
+                line_copy(block, which, 2 + j, far[j], z_end).wait_send()
+
+    def line_here(block, which):
+        @pl.when(middle)
+        def _():
+            wait_for(block(z_end), wz_r.at[which, z_end])
+
+        @pl.when(jnp.logical_not(middle))
+        def _():
+            for i in range(1, 4):
+                wait_for(block(zpeer(i)), wz_r.at[which, zpeer(i)])
+
+    def qkv_block(b):
+        return wqkv.at[:, b]
+
+    def gu_block(h):
+        return lambda b: wgu.at[pl.ds(2 * h, 2), b]
+
+    def down_block(b):
+        return wd.at[b]
 
     def out_weights(start):
         to_core = z // 2
@@ -523,35 +644,50 @@
             else:
                 send()
 
+    def half(j):
+        return pl.ds(2 * j, 2)
+
+    def ag_copy(buf, which, i):
+        own = buf.at[k, :, c]
+        return remote(own, own, ag_s.at[which, i], ag_r.at[which, k], dev(peer(i), z, c))
+
+    def ag_turn(buf, which, i):
+        block = buf.at[peer(i), half(i - 1), c]
+        return remote(
+            block, block, ag_s.at[which, 8 + i], ag_d.at[which, i - 1], dev(peer(3 - i), z, c)
+        )
+
+    def ag_across(buf, which, i):
+        block = buf.at[peer(i), :, c]
+        return remote(
+            block, block, ag_s.at[which, 4 + i], ag_x.at[which, peer(i)], sibling
+        )
+
     def ag_send(buf, which):
-        own = buf.at[k, :, c]
-        for i in (1, 2, 3):
-            remote(
-                own, own, ag_s.at[which, i], ag_r.at[which, k], dev(peer(i), z, c)
-            ).start()
-        remote(own, own, ag_s.at[which, 4], ag_x.at[which, k], sibling).start()
+        for i in (1, 2):
+            ag_copy(buf, which, i).start()
+        ag_across(buf, which, 0).start()
 
     def ag_relay(buf, which, i):
         m = peer(i)
-        block = buf.at[m, :, c]
-        wait_for(block, ag_r.at[which, m])
-        remote(block, block, ag_s.at[which, 4 + i], ag_x.at[which, m], sibling).start()
+        if i < 3:
+            wait_for(buf.at[m, :, c], ag_r.at[which, m])
+            ag_turn(buf, which, i).start()
+        else:
+            for j in range(2):
+                wait_for(buf.at[m, half(j), c], ag_d.at[which, j])
+        ag_across(buf, which, i).start()
 
     def ag_other(buf, which, i):
         m = peer(i)
         wait_for(buf.at[m, :, oc], ag_x.at[which, m])
 
     def ag_end(buf, which):
-        own = buf.at[k, :, c]
-        for i in (1, 2, 3):
-            remote(
-                own, own, ag_s.at[which, i], ag_r.at[which, k], dev(peer(i), z, c)
-            ).wait_send()
+        for i in (1, 2):
+            ag_copy(buf, which, i).wait_send()
+            ag_turn(buf, which, i).wait_send()
         for i in range(4):
-            block = buf.at[peer(i), :, c]
-            remote(
-                block, block, ag_s.at[which, 4 + i], ag_x.at[which, peer(i)], sibling
-            ).wait_send()
+            ag_across(buf, which, i).wait_send()
 
     def rs_copy(part, which, i):
         m = peer(i)
@@ -559,14 +695,23 @@
             part.at[m, :, oc], sib.at[which, m], rs_s.at[which, i], rs_r.at[which, m], sibling
         )
 
-    def rs_send_copy(part, which, i):
+    def rs_part(part, which, i, j):
         m = peer(i)
         return remote(
-            part.at[m, :, c],
-            rcv.at[which, k],
-            rs_s.at[which, 4 + i],
-            rs_x.at[which, k],
+            part.at[m, half(j), c],
+            rcv.at[which, i - 1, half(j)],
+            rs_s.at[which, 2 + 2 * i + j],
+            rs_x.at[which, i - 1, j],
             dev(m, z, c),
+        )
+
+    def rs_turn(part, which, j):
+        return remote(
+            part.at[peer(3), half(j), c],
+            turn.at[which, j],
+            rs_s.at[which, 8 + j],
+            rs_d.at[which, j],
+            dev(peer(j + 1), z, c),
         )
 
     def rs_pair(part, which, i):
@@ -575,58 +720,144 @@
         return part[m, :, c].astype(F32) + sib[which, m].astype(F32)
 
     def rs_forward(part, which):
-        for i in (3, 1, 2):
+        part[peer(3), :, c] = rs_pair(part, which, 3).astype(BF)
+        for j in range(2):
+            rs_turn(part, which, j).start()
+        for i in (1, 2):
             part[peer(i), :, c] = rs_pair(part, which, i).astype(BF)
-            rs_send_copy(part, which, i).start()
+            rs_part(part, which, i, i - 1).start()
+        for j in range(2):
+            wait_for(turn.at[which, j], rs_d.at[which, j])
+            m = peer(2 - j)
+            sums = part[m, half(j), c].astype(F32) + turn[which, j].astype(F32)
+            part[m, half(j), c] = sums.astype(BF)
+            rs_part(part, which, 2 - j, j).start()
 
     def rs_sum(part, which):
         total = rs_pair(part, which, 0)
-        for i in (1, 2, 3):
-            m = peer(i)
-            wait_for(rcv.at[which, m], rs_x.at[which, m])
-            total = total + rcv[which, m].astype(F32)
+        for i in (1, 2):
+            for j in range(2):
+                wait_for(rcv.at[which, i - 1, half(j)], rs_x.at[which, i - 1, j])
+            total = total + rcv[which, i - 1].astype(F32)
         return total.reshape(128, 1024)
 
     def rs_end(part, which):
         for i in range(4):
             rs_copy(part, which, i).wait_send()
-        for i in (1, 2, 3):
-            rs_send_copy(part, which, i).wait_send()
-
-    spread_lat(True)
+        for j in range(2):
+            rs_turn(part, which, j).wait_send()
+            for i in (1, 2):
+                rs_part(part, which, i, j).wait_send()
+
+    def grads_to_far(grad, land, which, j):
+        return remote(
+            grad(far[j]), land.at[z], gz_s.at[which, 1 + j], gz_r.at[which, z], dev(k, far[j], c)
+        )
+
+    def line_grads(grad, land, add, which, start):
+        @pl.when(middle)
+        def _():
+            copy = remote(
+                grad(z_end), land.at[z], gz_s.at[which, 0], gz_r.at[which, z], dev(k, z_end, c)
+            )
+            if start:
+                copy.start()
+            else:
+                copy.wait_send()
+                for j in range(2):
+                    grads_to_far(grad, land, which, j).wait_send()
+
+        @pl.when(jnp.logical_not(middle))
+        def _():
+            mid = 1 + z // 2
+            for j in range(2):
+                copy = remote(
+                    grad(far_of(mid)[j]),
+                    add.at[j],
+                    gz_s.at[which, j],
+                    gx_r.at[which, j],
+                    dev(k, mid, c),
+                )
+                if start:
+                    copy.start()
+                else:
+                    copy.wait_send()
+            copy = remote(
+                grad(mid), land.at[z], gz_s.at[which, 2], gz_r.at[which, z], dev(k, mid, c)
+            )
+            if start:
+                copy.start()
+            else:
+                copy.wait_send()
+
+    def line_grads_relay(grad, land, add, which, j):
+        @pl.when(middle)
+        def _():
+            wait_for(add.at[j], gx_r.at[which, j])
+            mine = grad(far[j])
+            mine[...] = (mine[...].astype(F32) + add[j].astype(F32)).astype(BF)
+            grads_to_far(grad, land, which, j).start()
+
+    def line_sum(grad, land, which):
+        total = grad(z)[...].astype(F32)
+        for j in range(2):
+            wait_for(land.at[near[j]], gz_r.at[which, near[j]])
+            total = total + land[near[j]].astype(F32)
+        return total
+
+    def dwgu_block(b):
+        return dwgu.at[:, b]
+
+    def dwqkv_block(b):
+        return dwqkv.at[:, b]
+
+    def dwd_block(b):
+        return dwd.at[b]
+
+    spread(lat_in, lat_place, 0, True)
+    plane_weights(wqkv_in, wqkv, 0, True)
     spread_lens(True)
-    plane_weights(wqkv_in, wqkv, 0, True)
-    spread_cot(True)
+    line_send(down_block, 2, (0,), (0, 1), src=wd_in)
+    own_down = pltpu.make_async_copy(wd_in, wd.at[z], wd_r)
+    own_down.start()
+    units_to_ranks()
+    spread_on(lat_in, lat_place, 0, True)
     plane_weights(wgu_in, wgu, 1, True)
+    spread(dout_in, cot_place, 1, True)
     plane_weights_here(wqkv, 0)
-    line_weights(wqkv, 0, True)
+    line_send(qkv_block, 0, (0, 1), (0, 1))
     for b in range(4):
         wait_for(own_l.at[b], tr_r.at[0, b])
     lat_f = own_l[...].reshape(128, 1024).astype(F32)
     r_one = lax.rsqrt(jnp.mean(lat_f * lat_f, axis=-1, keepdims=True) + EPS)
     n_one[k, :, c] = (lat_f * r_one).astype(BF).reshape(4, 32, 1024)
     ag_send(n_one, 0)
+    line_relay(down_block, 2, 0)
+    spread_on(dout_in, cot_place, 1, True)
+    line_relay(qkv_block, 0, 0)
+    ag_relay(n_one, 0, 1)
+    ag_relay(n_one, 0, 2)
+    line_relay(qkv_block, 0, 1)
+    line_send(down_block, 2, (1,), (), src=wd_in)
     out_weights(True)
+    ag_relay(n_one, 0, 3)
     plane_weights_here(wgu, 1)
-    line_weights(wgu, 1, True)
-    down_weights(True)
-    for b in range(4):
-        wait_for(cot.at[k, b, c], tr_r.at[1, b])
-    ag_send(cot, 1)
-
-    line_weights_here(wqkv, 0)
+    line_send(gu_block(0), 1, (0, 1), (0, 1))
+    line_send(gu_block(1), 3, (0, 1), (0, 1))
+
+    line_here(qkv_block, 0)
 
     @pl.loop(0, 4)
     def _(i):
-        @pl.when(i > 0)
-        def _():
-            ag_relay(n_one, 0, i)
-
         ag_other(n_one, 0, i)
         m = peer(i)
         block = n_one[m].reshape(256, 1024)
         out = dot_nn(block, wqkv[...].reshape(1024, 384))
         qkv[:, m] = out.astype(BF).reshape(8, 32, 384)
+
+    for b in range(4):
+        wait_for(cot.at[k, b, c], tr_r.at[1, b])
+    ag_send(cot, 1)
 
     wait_for(lens, ln_r)
     lane = lax.broadcasted_iota(jnp.int32, (128, 128), 1)
@@ -681,8 +912,6 @@
         att_f[t] = attended
         att[:, t] = attended.astype(BF).reshape(4, 32, 128)
 
-    for i in (1, 2, 3):
-        ag_relay(cot, 1, i)
     for slot in range(4):
         wait_for(wo.at[slot], wo_r.at[slot])
 
@@ -694,25 +923,33 @@
         part_a[m] = out.astype(BF).reshape(4, 2, 32, 1024)
         rs_copy(part_a, 0, i).start()
 
+    line_relay(down_block, 2, 1)
+    ag_relay(cot, 1, 1)
+    ag_relay(cot, 1, 2)
     rs_forward(part_a, 0)
+    line_relay(gu_block(0), 1, 0)
+    line_relay(gu_block(0), 1, 1)
+    ag_relay(cot, 1, 3)
     res = own_l[...].reshape(128, 1024).astype(F32) + rs_sum(part_a, 0)
     resid[...] = res
     r_two = lax.rsqrt(jnp.mean(res * res, axis=-1, keepdims=True) + EPS)
     n_two[k, :, c] = (res * r_two).astype(BF).reshape(4, 32, 1024)
     ag_send(n_two, 2)
+    line_relay(gu_block(1), 3, 0)
+    line_relay(gu_block(1), 3, 1)
 
     for i in range(4):
         ag_other(cot, 1, i)
-    line_weights_here(wgu, 1)
-    for b in range(4):
-        wait_for(wd.at[b], wd_r.at[b])
+    ag_relay(n_two, 2, 1)
+    ag_relay(n_two, 2, 2)
+    ag_relay(n_two, 2, 3)
+    line_here(down_block, 2)
+    own_down.wait()
+    line_here(gu_block(0), 1)
+    line_here(gu_block(1), 3)
 
     @pl.loop(0, 4)
     def _(i):
-        @pl.when(i > 0)
-        def _():
-            ag_relay(n_two, 2, i)
-
         ag_other(n_two, 2, i)
         m = peer(i)
         gu = dot_nn(n_two[m].reshape(256, 1024), wgu[...].reshape(1024, 768))
@@ -721,14 +958,40 @@
         sig = jax.nn.sigmoid(gate)
         active = gate * sig
         hid[m] = (active * up).astype(BF)
+        slope[m, :, :384] = up * sig * (1.0 + gate * (1.0 - sig))
+        slope[m, :, 384:] = active
+
+    @pl.loop(0, 4)
+    def _(n):
+        cols = pl.ds(pl.multiple_of(n * 256, 256), 256)
+        right = cot[:, :, :, :, cols].reshape(1024, 256)
+        out = dot_left(hid[...].reshape(1024, 384), right)
+        dwd[:, :, cols] = out.astype(BF).reshape(4, 96, 256)
+
+    line_grads(dwd_block, zd, xd, 2, True)
+
+    @pl.loop(0, 4)
+    def _(i):
+        m = peer(i)
         g_hid = dot_right(cot[m].reshape(256, 1024), wd[...].reshape(384, 1024))
-        ggu[m, :, :384] = (g_hid * up * sig * (1.0 + gate * (1.0 - sig))).astype(BF)
-        ggu[m, :, 384:] = (g_hid * active).astype(BF)
+        ggu[m, :, :384] = (g_hid * slope[m, :, :384]).astype(BF)
+        ggu[m, :, 384:] = (g_hid * slope[m, :, 384:]).astype(BF)
         out = dot_right(ggu[m], wgu[...].reshape(1024, 768))
         part_b[m] = out.astype(BF).reshape(4, 2, 32, 1024)
         rs_copy(part_b, 1, i).start()
 
     rs_forward(part_b, 1)
+
+    @pl.loop(0, 4)
+    def _(d):
+        cols = pl.ds(pl.multiple_of(d * 256, 256), 256)
+        left = n_two[:, :, :, :, cols].reshape(1024, 256)
+        out = dot_left(left, ggu[...].reshape(1024, 768))
+        dwgu[d] = out.astype(BF).reshape(4, 2, 32, 768)
+
+    line_grads(dwgu_block, zgu, xgu, 1, True)
+    line_grads_relay(dwd_block, zd, xd, 2, 0)
+    line_grads_relay(dwd_block, zd, xd, 2, 1)
 
     @pl.loop(0, 4)
     def _(i):
@@ -746,59 +1009,15 @@
     gres[...] = g_res
     gbr[k, :, c] = g_res.astype(BF).reshape(4, 32, 1024)
     ag_send(gbr, 3)
+
+    ag_relay(gbr, 3, 1)
+    ag_relay(gbr, 3, 2)
+    ag_relay(gbr, 3, 3)
+    line_grads_relay(dwgu_block, zgu, xgu, 1, 0)
     rs_forward(part_c, 2)
-
-    @pl.loop(0, 4)
-    def _(d):
-        cols = pl.ds(pl.multiple_of(d * 256, 256), 256)
-        left = n_two[:, :, :, :, cols].reshape(1024, 256)
-        out = dot_left(left, ggu[...].reshape(1024, 768))
-        dwgu[d] = out.astype(BF).reshape(4, 2, 32, 768)
-
-    def line_grads(grad, land, which, start):
-        for i in range(1, 4):
-            copy = remote(
-                grad.at[:, zpeer(i)],
-                land.at[z],
-                gz_s.at[which, i],
-                gz_r.at[which, z],
-                dev(k, zpeer(i), c),
-            )
-            if start:
-                copy.start()
-            else:
-                copy.wait_send()
-
-    line_grads(dwgu, zgu, 1, True)
-
-    @pl.loop(0, 4)
-    def _(n):
-        cols = pl.ds(pl.multiple_of(n * 256, 256), 256)
-        right = cot[:, :, :, :, cols].reshape(1024, 256)
-        out = dot_left(hid[...].reshape(1024, 384), right)
-        dwd[:, :, cols] = out.astype(BF).reshape(4, 96, 256)
-
-    def down_grads(start):
-        for i in range(4):
-            src = dwd.at[zpeer(i)]
-            if i == 0:
-                if start:
-                    pltpu.make_async_copy(src, gd_o.at[z], gd_r.at[z]).start()
-            else:
-                copy = remote(src, gd_o.at[z], gd_s.at[i], gd_r.at[z], dev(k, zpeer(i), c))
-                if start:
-                    copy.start()
-                else:
-                    copy.wait_send()
-
-    down_grads(True)
 
     @pl.loop(0, 4)
     def _(i):
-        @pl.when(i > 0)
-        def _():
-            ag_relay(gbr, 3, i)
-
         ag_other(gbr, 3, i)
         m = peer(i)
         out = dot_right(gbr[m].reshape(256, 1024), wo[...].reshape(128, 1024))
@@ -819,6 +1038,7 @@
         gsc[t, :, 0:span] = g_sc.astype(BF)
         g_q = one_of_two(dot_nn(gsc[t, :, 0:span], keys)) * 0.125
         gqkv[:, t, :, 0:128] = g_q.astype(BF).reshape(4, 32, 128)
+    line_grads_relay(dwgu_block, zgu, xgu, 1, 1)
     for u in range(8):
         cols = slice(u * 128, (u + 1) * 128)
         rows = (8 - u) * 256
@@ -837,7 +1057,6 @@
         part_a[m] = out.astype(BF).reshape(4, 2, 32, 1024)
         rs_copy(part_a, 3, i).start()
 
-    rs_forward(part_a, 3)
 
     @pl.loop(0, 4)
     def _(d):
@@ -846,7 +1065,10 @@
         out = dot_left(left, gqkv[...].reshape(1024, 384))
         dwqkv[d] = out.astype(BF).reshape(4, 2, 32, 384)
 
-    line_grads(dwqkv, zq, 0, True)
+    line_grads(dwqkv_block, zq, xq, 0, True)
+    rs_forward(part_a, 3)
+    line_grads_relay(dwqkv_block, zq, xq, 0, 0)
+    line_grads_relay(dwqkv_block, zq, xq, 0, 1)
 
     @pl.loop(0, 4)
     def _(n):
@@ -901,13 +1123,6 @@
     out_f = resid[...] + rs_sum(part_c, 2)
     back[0] = out_f.astype(BF).reshape(4, 32, 1024)
     gather_back(0, lat_o, True)
-
-    def line_sum(grad, land, which):
-        total = grad[:, z].astype(F32)
-        for i in range(1, 4):
-            wait_for(land.at[zpeer(i)], gz_r.at[which, zpeer(i)])
-            total = total + land[zpeer(i)].astype(F32)
-        land[z] = total.astype(BF)
 
     def plane_grads(land, dst, which, start):
         for i in range(4):
@@ -932,9 +1147,6 @@
                     else:
                         copy.wait_send()
 
-    line_sum(dwgu, zgu, 1)
-    plane_grads(zgu, ggu_o, 1, True)
-
     scaled = rs_sum(part_a, 3)
     lat_f = own_l[...].reshape(128, 1024).astype(F32)
     r_one = lax.rsqrt(jnp.mean(lat_f * lat_f, axis=-1, keepdims=True) + EPS)
@@ -943,43 +1155,53 @@
     d_lat = gres[...] + r_one * (scaled - normed * inner)
     back[1] = d_lat.astype(BF).reshape(4, 32, 1024)
     gather_back(1, dlat_o, True)
-
-    line_sum(dwqkv, zq, 0)
+    zgu[z] = line_sum(dwgu_block, zgu, 1).astype(BF)
+    plane_grads(zgu, ggu_o, 1, True)
+
+
+    down_sum[...] = line_sum(dwd_block, zd, 2)
+    down_out = pltpu.make_async_copy(down_sum, gd_o, gd_r)
+    down_out.start()
+    zq[z] = line_sum(dwqkv_block, zq, 0).astype(BF)
     plane_grads(zq, gqkv_o, 0, True)
 
+    for which, dst in ((0, lat_o), (1, dlat_o)):
+        for b in range(4):
+            wait_for(dst.at[pl.ds(32 * b, 32)], tb_r.at[which, b])
     for b in range(4):
-        wait_for(gd_o.at[b], gd_r.at[b])
         wait_for(go_o.at[b], go_r.at[b])
-        for which, dst in ((0, lat_o), (1, dlat_o)):
-            wait_for(dst.at[pl.ds(32 * b, 32)], tb_r.at[which, b])
-    for r in range(RANKS):
-        wait_for(gqkv_o.at[r], ga_r.at[0, r])
-        wait_for(ggu_o.at[r], ga_r.at[1, r])
-    spread_lat(False)
-    spread_cot(False)
+    for which, dst in ((1, ggu_o), (0, gqkv_o)):
+        for r in range(RANKS):
+            wait_for(dst.at[r], ga_r.at[which, r])
+    spread(lat_in, lat_place, 0, False)
+    spread_on(lat_in, lat_place, 0, False)
+    spread(dout_in, cot_place, 1, False)
+    spread_on(dout_in, cot_place, 1, False)
     spread_lens(False)
     plane_weights(wqkv_in, wqkv, 0, False)
     plane_weights(wgu_in, wgu, 1, False)
-    line_weights(wqkv, 0, False)
-    line_weights(wgu, 1, False)
-    down_weights(False)
+    line_sent(qkv_block, 0)
+    line_sent(gu_block(0), 1)
+    line_sent(gu_block(1), 3)
+    line_sent(down_block, 2, wd_in)
+    down_out.wait()
     out_weights(False)
     for which, buf in enumerate((n_one, cot, n_two, gbr)):
         ag_end(buf, which)
     rs_end(part_b, 1)
     rs_end(part_c, 2)
     rs_end(part_a, 3)
-    line_grads(dwgu, zgu, 1, False)
-    line_grads(dwqkv, zq, 0, False)
+    line_grads(dwgu_block, zgu, xgu, 1, False)
+    line_grads(dwqkv_block, zq, xq, 0, False)
+    line_grads(dwd_block, zd, xd, 2, False)
     plane_grads(zgu, ggu_o, 1, False)
     plane_grads(zq, gqkv_o, 0, False)
-    down_grads(False)
     out_grads(False)
     gather_back(0, lat_o, False)
     gather_back(1, dlat_o, False)
 
 
-def run_layer(lat, dout, lens, wqkv_src, wgu_src, wd_src, wo_src):
+def run_layer(lat, dout, lengths, gain_one, gain_two, weights):
     vm = pltpu.VMEM
     dma = pltpu.SemaphoreType.DMA
     rows = (4, 4, 2, 32)
@@ -990,13 +1212,20 @@
             jax.ShapeDtypeStruct((128, 1024), BF),
             jax.ShapeDtypeStruct((RANKS, 32, 384), BF),
             jax.ShapeDtypeStruct((RANKS, 32, 768), BF),
-            jax.ShapeDtypeStruct((4, 96, 1024), BF),
+            jax.ShapeDtypeStruct((96, 1024), F32),
             jax.ShapeDtypeStruct((4, 32, 1024), BF),
         ),
-        in_specs=[pl.BlockSpec(memory_space=pl.ANY)] * 7,
+        in_specs=[pl.BlockSpec(memory_space=pl.ANY)] * 2
+        + [pl.BlockSpec(memory_space=pltpu.SMEM)]
+        + [pl.BlockSpec(memory_space=pltpu.VMEM)] * 9,
         out_specs=[pl.BlockSpec(memory_space=pl.ANY)] * 6,
         scratch_shapes=[
+            vm((8, 128), jnp.int32),
+            vm((RANKS, 32, 384), BF),
+            vm((RANKS, 32, 768), BF),
+            vm((96, 1024), BF),
             vm((4, 32, 1024), BF),
+            vm((2, 4, 32, 1024), BF),
             vm((8, 128), jnp.int32),
             vm(rows + (1024,), BF),
             vm(rows + (1024,), BF),
@@ -1016,9 +1245,11 @@
             vm(rows + (1024,), BF),
             vm(rows + (1024,), BF),
             vm((4, 4, 4, 32, 1024), BF),
-            vm((4, 4, 4, 32, 1024), BF),
+            vm((4, 2, 4, 32, 1024), BF),
+            vm((4, 2, 2, 32, 1024), BF),
             vm((4, 256, 384), BF),
             vm((4, 256, 768), BF),
+            vm((4, 256, 768), F32),
             vm((8, 4, 32, 128), BF),
             vm((8, 256, 128), BF),
             vm((8, 256, 128), BF),
@@ -1029,33 +1260,41 @@
             vm((4, 32, 1024), BF),
             vm((4, 4, 2, 32, 384), BF),
             vm((4, 4, 2, 32, 768), BF),
+            vm((4, 96, 1024), BF),
+            vm((2, 4, 2, 32, 384), BF),
+            vm((2, 4, 2, 32, 768), BF),
+            vm((2, 96, 1024), BF),
+            vm((96, 1024), F32),
             vm((128, 1024), F32),
             vm((128, 1024), F32),
             vm((2, 4, 32, 1024), BF),
+            dma((2, 4)),
+            dma((2, 4)),
             dma((2, 4)),
             dma((2, 4)),
             dma,
             dma,
             dma((2, 8)),
             dma((2, 8)),
-            dma((2, 4)),
-            dma((2, 4)),
+            dma((4, 4)),
+            dma((4, 4)),
+            dma,
             dma((4,)),
             dma((4,)),
-            dma((4,)),
-            dma((4,)),
-            dma((4, 8)),
+            dma((4, 12)),
             dma((4, 4)),
             dma((4, 4)),
-            dma((4, 8)),
+            dma((4, 2)),
+            dma((4, 12)),
             dma((4, 4)),
-            dma((4, 4)),
-            dma((2, 4)),
-            dma((2, 4)),
+            dma((4, 2, 2)),
+            dma((4, 2)),
+            dma((3, 4)),
+            dma((3, 4)),
+            dma((3, 2)),
             dma((2, 8)),
             dma((2, 8)),
-            dma((4,)),
-            dma((4,)),
+            dma,
             dma((4,)),
             dma((4,)),
             dma((2, 4)),
@@ -1064,7 +1303,89 @@
         compiler_params=pltpu.CompilerParams(
             collective_id=0, has_side_effects=True, vmem_limit_bytes=60 * 1024 * 1024
         ),
-    )(lat, dout, lens, wqkv_src, wgu_src, wd_src, wo_src)
+    )(lat, dout, lengths, gain_one, gain_two, *weights)
+
+
+def finish_kernel(
+    lat,
+    dlat,
+    gqkv,
+    ggu,
+    gd,
+    go,
+    gain_one,
+    gain_two,
+    wq,
+    wk,
+    wv,
+    wg,
+    wu,
+    lat_o,
+    dlat_o,
+    g_one_o,
+    gq_o,
+    gk_o,
+    gv_o,
+    go_o,
+    g_two_o,
+    gg_o,
+    gu_o,
+    gd_o,
+):
+    lat_o[0] = lat[...]
+    dlat_o[0] = dlat[...]
+    go_o[...] = (go[0].astype(F32) + go[1].astype(F32)) + (go[2].astype(F32) + go[3].astype(F32))
+    gd_o[...] = gd[0:88]
+    col_one = jnp.sum(on_diagonal(gain_one[...]), axis=1, keepdims=True)
+    col_two = jnp.sum(on_diagonal(gain_two[...]), axis=1, keepdims=True)
+
+    def as_row(acc):
+        return jnp.sum(on_diagonal(jnp.sum(acc, axis=1, keepdims=True)), axis=0, keepdims=True)
+
+    acc = jnp.zeros((32, 128), F32)
+    for i, (w, out) in enumerate(((wq, gq_o), (wk, gk_o), (wv, gv_o))):
+        for r in range(RANKS):
+            cols = slice(r * 128, (r + 1) * 128)
+            part = gqkv[r, :, i * 128 : (i + 1) * 128].astype(F32)
+            out[:, cols] = part * col_one
+            acc = acc + part * w[:, cols].astype(F32)
+    g_one_o[...] = as_row(acc)
+    acc = jnp.zeros((32, 256), F32)
+    for i, (w, out) in enumerate(((wg, gg_o), (wu, gu_o))):
+        parts = [None] * 32
+        for r in range(RANKS):
+            whole = ggu[r, :, i * 384 : (i + 1) * 384].astype(F32)
+            for b in range(ZS):
+                parts[8 * (r // CORES) + CORES * b + r % CORES] = whole[:, b * 96 : b * 96 + 88]
+        rows = jnp.concatenate(parts, axis=1)
+        out[...] = rows * col_two
+        prod = rows * w[...].astype(F32)
+        for n in range(11):
+            acc = acc + prod[:, n * 256 : (n + 1) * 256]
+    g_two_o[...] = as_row(acc)
+
+
+def finish(*arrays):
+    outs = (
+        ((1, 128, 1024), BF),
+        ((1, 128, 1024), BF),
+        ((1, 32), F32),
+        ((32, 1024), F32),
+        ((32, 1024), F32),
+        ((32, 1024), F32),
+        ((32, 1024), F32),
+        ((1, 32), F32),
+        ((32, 2816), F32),
+        ((32, 2816), F32),
+        ((88, 1024), F32),
+    )
+    return pl.pallas_call(
+        finish_kernel,
+        out_shape=tuple(jax.ShapeDtypeStruct(*o) for o in outs),
+        in_specs=[pl.BlockSpec(memory_space=pltpu.VMEM)] * len(arrays),
+        out_specs=[pl.BlockSpec(memory_space=pltpu.VMEM)] * len(outs),
+        compiler_params=pltpu.CompilerParams(vmem_limit_bytes=32 * 1024 * 1024),
+    )(*arrays)
 
 
 def plane_device(
@@ -1081,56 +1402,11 @@
     w_up,
     w_down,
 ):
-    gain_one = gain_attn.astype(F32)[:, None]
-    gain_two = gain_ffn.astype(F32)[:, None]
-
-    def heads_of(w):
-        return (w.astype(F32) * gain_one).astype(BF).reshape(32, RANKS, 128)
-
-    wqkv_src = jnp.concatenate(
-        [heads_of(w) for w in (w_query, w_key, w_value)], axis=-1
-    ).transpose(1, 0, 2)
-
-    def units_of(w):
-        w = (w.astype(F32) * gain_two).astype(BF).reshape(32, DP, ZS, CORES, 88)
-        w = jnp.pad(w, ((0, 0), (0, 0), (0, 0), (0, 0), (0, 8)))
-        return w.transpose(1, 3, 0, 2, 4).reshape(RANKS, 32, 384)
-
-    wgu_src = jnp.concatenate([units_of(w_gate), units_of(w_up)], axis=-1)
-    wd_src = jnp.pad(w_down, ((0, 8), (0, 0)))
-    lens = jnp.broadcast_to(jnp.pad(lengths[0], (0, 4))[:, None], (8, 128))
-    lat_o, dlat_o, gqkv, ggu, gd, go = run_layer(
-        latents[0], d_out[0], lens, wqkv_src, wgu_src, wd_src, w_out
-    )
-
-    def rows_of(g):
-        return g.astype(F32).transpose(1, 0, 2).reshape(32, 1024)
-
-    def units_back(g):
-        g = g.astype(F32).reshape(DP, CORES, 32, ZS, 96)[..., :88]
-        return g.transpose(2, 0, 3, 1, 4).reshape(32, 2816)
-
-    n_q, n_k, n_v = (rows_of(gqkv[:, :, i * 128 : (i + 1) * 128]) for i in range(3))
-    n_g, n_u = units_back(ggu[:, :, :384]), units_back(ggu[:, :, 384:])
-    g_gain_one = jnp.sum(
-        n_q * w_query.astype(F32) + n_k * w_key.astype(F32) + n_v * w_value.astype(F32), axis=1
-    )
-    g_gain_two = jnp.sum(n_g * w_gate.astype(F32) + n_u * w_up.astype(F32), axis=1)
-    g_out = jnp.sum(go.astype(F32), axis=0)
-    g_down = jnp.sum(gd.astype(F32), axis=0)[:88]
-    return (
-        lat_o[None],
-        dlat_o[None],
-        g_gain_one,
-        n_q * gain_one,
-        n_k * gain_one,
-        n_v * gain_one,
-        g_out,
-        g_gain_two,
-        n_g * gain_two,
-        n_u * gain_two,
-        g_down,
-    )
+    gains = gain_attn.reshape(1, 32), gain_ffn.reshape(1, 32)
+    weights = w_query, w_key, w_value, w_gate, w_up, w_down, w_out
+    parts = run_layer(latents[0], d_out[0], lengths, *gains, weights)
+    outs = finish(*parts, *gains, w_query, w_key, w_value, w_gate, w_up)
+    return tuple(o.reshape(32) if o.shape == (1, 32) else o for o in outs)
 
 
 def solution(mesh):

time: 243 us -> 165 us (0.68)
  the two profiles are of different devices: /device:TPU:9 before, /device:TPU:27 now
where the time goes in v2:
time: 165 us
  Pallas kernels  158 us (96%)
  local copies, waits for them, and re-layouts  6.39 us (4%)
    pallas_call x1, Pallas kernels, run_layer(): pl.pallas_call(layer_kernel, out_shape=(jax.ShapeDtypeStruct((128, 1024),...  156 us
    unnamed x26, local copies, waits for them, and re-layouts  6.39 us

profile of v2, /device:TPU:27, one launch (start us, length us, event | category | flops | bytes accessed | tf_op | source)
XLA Modules:
  0.0 164.9 jit_solution(14472791703118969517)
XLA Ops:
  0.6 0.0 copy-start
  0.7 0.0 copy-start.1
  0.7 0.0 copy-start.4
  0.7 0.0 copy-start.5
  0.7 0.0 copy-start.6
  0.7 156.2 %shard_map.203 = (bf16[128,1024]{1,0:T(8,128)(2,1)}, bf16[128,1024]{1,0:T(8,128)(2,1)}, bf16[8,32,384]{2,1,0:T(8,128)(2,1)}, bf16[8,32,768]{2,1,0:T(8,128)(2,1)}...) custom-call(bf16[128,1024]{1,0:T(8,128)(2,1)} %bitcast.10, bf16[128,1024]{1,0:T(8,128)(2,1)} %bitcast.11, ...), custom_call_target="tpu_custom_call" | custom-call | tf_op jit(solution)/shard_map/pallas_call | solution.py:1208
  156.9 0.0 copy-start.11
  156.9 0.0 copy-start.12
  156.9 0.0 copy-done
  156.9 0.0 copy-done.1
  156.9 0.0 copy-done.4
  156.9 0.0 copy-done.5
  156.9 0.0 copy-done.6
  157.0 0.6 copy-done.11
  157.5 0.0 copy-done.12
  157.6 0.0 copy-start.2
  157.6 1.0 copy-done.2
  158.5 0.0 copy-start.3
  158.6 1.0 copy-done.3
  159.5 0.0 copy-start.7
  159.5 0.9 copy-done.7
  160.5 0.0 copy-start.8
  160.5 0.9 copy-done.8
  161.4 0.0 copy-start.9
  161.4 0.9 copy-done.9
  162.4 0.0 copy-start.10
  162.4 0.9 copy-done.10
  163.3 1.6 shard_map.204
Async XLA Ops:
  0.6 156.3 %copy-start = (bf16[32,2816]{1,0:T(8,128)(2,1)S(1)}, bf16[32,2816]{1,0:T(8,128)(2,1)}, u32[]{:S(2)}) copy-start(bf16[32,2816]{1,0:T(8,128)(2,1)} %wg.1) | copy-start | bytes 540676
  0.7 156.3 %copy-start.1 = (bf16[32,2816]{1,0:T(8,128)(2,1)S(1)}, bf16[32,2816]{1,0:T(8,128)(2,1)}, u32[]{:S(2)}) copy-start(bf16[32,2816]{1,0:T(8,128)(2,1)} %wu.1) | copy-start | bytes 540676
  0.7 156.3 %copy-start.4 = (bf16[32,1024]{1,0:T(8,128)(2,1)S(1)}, bf16[32,1024]{1,0:T(8,128)(2,1)}, u32[]{:S(2)}) copy-start(bf16[32,1024]{1,0:T(8,128)(2,1)} %wq.1) | copy-start | bytes 196612
  0.7 156.3 %copy-start.5 = (bf16[32,1024]{1,0:T(8,128)(2,1)S(1)}, bf16[32,1024]{1,0:T(8,128)(2,1)}, u32[]{:S(2)}) copy-start(bf16[32,1024]{1,0:T(8,128)(2,1)} %wk.1) | copy-start | bytes 196612
  0.7 156.3 %copy-start.6 = (bf16[32,1024]{1,0:T(8,128)(2,1)S(1)}, bf16[32,1024]{1,0:T(8,128)(2,1)}, u32[]{:S(2)}) copy-start(bf16[32,1024]{1,0:T(8,128)(2,1)} %wv.1) | copy-start | bytes 196612
  156.9 0.7 copy-start.11
  156.9 0.7 copy-start.12
  157.6 1.0 copy-start.2
  158.5 1.0 copy-start.3
  159.5 0.9 copy-start.7
  160.5 0.9 copy-start.8
  161.4 0.9 copy-start.9
  162.4 0.9 copy-start.10

commit v3 on v2

--- a/solution.py
+++ b/solution.py
@@ -647,32 +647,39 @@
     def half(j):
         return pl.ds(2 * j, 2)
 
-    def ag_copy(buf, which, i):
-        own = buf.at[k, :, c]
-        return remote(own, own, ag_s.at[which, i], ag_r.at[which, k], dev(peer(i), z, c))
+    def ag_copy(buf, which, i, j):
+        own = buf.at[k, half(j), c]
+        return remote(
+            own, own, ag_s.at[which, 2 * i + j], ag_r.at[which, k, j], dev(peer(i), z, c)
+        )
 
     def ag_turn(buf, which, i):
         block = buf.at[peer(i), half(i - 1), c]
         return remote(
-            block, block, ag_s.at[which, 8 + i], ag_d.at[which, i - 1], dev(peer(3 - i), z, c)
+            block, block, ag_s.at[which, 9 + i], ag_d.at[which, i - 1], dev(peer(3 - i), z, c)
         )
 
     def ag_across(buf, which, i):
         block = buf.at[peer(i), :, c]
         return remote(
-            block, block, ag_s.at[which, 4 + i], ag_x.at[which, peer(i)], sibling
+            block, block, ag_s.at[which, 6 + i], ag_x.at[which, peer(i)], sibling
         )
 
     def ag_send(buf, which):
+        for i, j in ((1, 0), (2, 1), (1, 1), (2, 0)):
+            ag_copy(buf, which, i, j).start()
+        ag_across(buf, which, 0).start()
+
+    def ag_corner(buf, which):
         for i in (1, 2):
-            ag_copy(buf, which, i).start()
-        ag_across(buf, which, 0).start()
+            m = peer(i)
+            wait_for(buf.at[m, half(i - 1), c], ag_r.at[which, m, i - 1])
+            ag_turn(buf, which, i).start()
 
     def ag_relay(buf, which, i):
         m = peer(i)
         if i < 3:
-            wait_for(buf.at[m, :, c], ag_r.at[which, m])
-            ag_turn(buf, which, i).start()
+            wait_for(buf.at[m, half(2 - i), c], ag_r.at[which, m, 2 - i])
         else:
             for j in range(2):
                 wait_for(buf.at[m, half(j), c], ag_d.at[which, j])
@@ -684,7 +691,8 @@
 
     def ag_end(buf, which):
         for i in (1, 2):
-            ag_copy(buf, which, i).wait_send()
+            for j in range(2):
+                ag_copy(buf, which, i, j).wait_send()
             ag_turn(buf, which, i).wait_send()
         for i in range(4):
             ag_across(buf, which, i).wait_send()
@@ -719,13 +727,23 @@
         wait_for(sib.at[which, m], rs_r.at[which, m])
         return part[m, :, c].astype(F32) + sib[which, m].astype(F32)
 
-    def rs_forward(part, which):
-        part[peer(3), :, c] = rs_pair(part, which, 3).astype(BF)
-        for j in range(2):
-            rs_turn(part, which, j).start()
-        for i in (1, 2):
-            part[peer(i), :, c] = rs_pair(part, which, i).astype(BF)
+    def rs_halves(part, which, i):
+        m = peer(i)
+        part[m, :, c] = rs_pair(part, which, i).astype(BF)
+        if i == 3:
+            for j in range(2):
+                rs_turn(part, which, j).start()
+        else:
             rs_part(part, which, i, i - 1).start()
+
+    def rs_start(part, which, compute):
+        for i, ready in ((3, None), (1, 3), (2, 1), (0, 2)):
+            compute(i)
+            rs_copy(part, which, i).start()
+            if ready:
+                rs_halves(part, which, ready)
+
+    def rs_corner(part, which):
         for j in range(2):
             wait_for(turn.at[which, j], rs_d.at[which, j])
             m = peer(2 - j)
@@ -832,14 +850,14 @@
     r_one = lax.rsqrt(jnp.mean(lat_f * lat_f, axis=-1, keepdims=True) + EPS)
     n_one[k, :, c] = (lat_f * r_one).astype(BF).reshape(4, 32, 1024)
     ag_send(n_one, 0)
-    line_relay(down_block, 2, 0)
-    spread_on(dout_in, cot_place, 1, True)
     line_relay(qkv_block, 0, 0)
+    ag_corner(n_one, 0)
     ag_relay(n_one, 0, 1)
     ag_relay(n_one, 0, 2)
     line_relay(qkv_block, 0, 1)
+    spread_on(dout_in, cot_place, 1, True)
+    out_weights(True)
     line_send(down_block, 2, (1,), (), src=wd_in)
-    out_weights(True)
     ag_relay(n_one, 0, 3)
     plane_weights_here(wgu, 1)
     line_send(gu_block(0), 1, (0, 1), (0, 1))
@@ -855,9 +873,7 @@
         out = dot_nn(block, wqkv[...].reshape(1024, 384))
         qkv[:, m] = out.astype(BF).reshape(8, 32, 384)
 
-    for b in range(4):
-        wait_for(cot.at[k, b, c], tr_r.at[1, b])
-    ag_send(cot, 1)
+    line_relay(down_block, 2, 0)
 
     wait_for(lens, ln_r)
     lane = lax.broadcasted_iota(jnp.int32, (128, 128), 1)
@@ -912,44 +928,41 @@
         att_f[t] = attended
         att[:, t] = attended.astype(BF).reshape(4, 32, 128)
 
+    for b in range(4):
+        wait_for(cot.at[k, b, c], tr_r.at[1, b])
+    ag_send(cot, 1)
     for slot in range(4):
         wait_for(wo.at[slot], wo_r.at[slot])
 
-    @pl.loop(0, 4)
-    def _(j):
-        i = 3 - j
+    def project_out(i):
         m = peer(i)
         out = dot_nn(att[m].reshape(256, 128), wo[...].reshape(128, 1024))
         part_a[m] = out.astype(BF).reshape(4, 2, 32, 1024)
-        rs_copy(part_a, 0, i).start()
-
+
+    rs_start(part_a, 0, project_out)
     line_relay(down_block, 2, 1)
+    ag_corner(cot, 1)
     ag_relay(cot, 1, 1)
     ag_relay(cot, 1, 2)
-    rs_forward(part_a, 0)
+    rs_corner(part_a, 0)
     line_relay(gu_block(0), 1, 0)
     line_relay(gu_block(0), 1, 1)
-    ag_relay(cot, 1, 3)
     res = own_l[...].reshape(128, 1024).astype(F32) + rs_sum(part_a, 0)
     resid[...] = res
     r_two = lax.rsqrt(jnp.mean(res * res, axis=-1, keepdims=True) + EPS)
     n_two[k, :, c] = (res * r_two).astype(BF).reshape(4, 32, 1024)
     ag_send(n_two, 2)
+    ag_relay(cot, 1, 3)
     line_relay(gu_block(1), 3, 0)
-    line_relay(gu_block(1), 3, 1)
-
-    for i in range(4):
-        ag_other(cot, 1, i)
+
+    ag_corner(n_two, 2)
     ag_relay(n_two, 2, 1)
     ag_relay(n_two, 2, 2)
-    ag_relay(n_two, 2, 3)
-    line_here(down_block, 2)
-    own_down.wait()
+    line_relay(gu_block(1), 3, 1)
     line_here(gu_block(0), 1)
     line_here(gu_block(1), 3)
 
-    @pl.loop(0, 4)
-    def _(i):
+    def feed_forward(i):
         ag_other(n_two, 2, i)
         m = peer(i)
         gu = dot_nn(n_two[m].reshape(256, 1024), wgu[...].reshape(1024, 768))
@@ -961,6 +974,17 @@
         slope[m, :, :384] = up * sig * (1.0 + gate * (1.0 - sig))
         slope[m, :, 384:] = active
 
+    @pl.loop(0, 3)
+    def _(i):
+        feed_forward(i)
+
+    ag_relay(n_two, 2, 3)
+    line_here(down_block, 2)
+    own_down.wait()
+    for i in range(4):
+        ag_other(cot, 1, i)
+    feed_forward(3)
+
     @pl.loop(0, 4)
     def _(n):
         cols = pl.ds(pl.multiple_of(n * 256, 256), 256)
@@ -970,24 +994,31 @@
 
     line_grads(dwd_block, zd, xd, 2, True)
 
-    @pl.loop(0, 4)
-    def _(i):
+    def feed_back(i):
         m = peer(i)
         g_hid = dot_right(cot[m].reshape(256, 1024), wd[...].reshape(384, 1024))
         ggu[m, :, :384] = (g_hid * slope[m, :, :384]).astype(BF)
         ggu[m, :, 384:] = (g_hid * slope[m, :, 384:]).astype(BF)
         out = dot_right(ggu[m], wgu[...].reshape(1024, 768))
         part_b[m] = out.astype(BF).reshape(4, 2, 32, 1024)
-        rs_copy(part_b, 1, i).start()
-
-    rs_forward(part_b, 1)
-
-    @pl.loop(0, 4)
-    def _(d):
+
+    rs_start(part_b, 1, feed_back)
+
+    def units_grad(d):
         cols = pl.ds(pl.multiple_of(d * 256, 256), 256)
         left = n_two[:, :, :, :, cols].reshape(1024, 256)
         out = dot_left(left, ggu[...].reshape(1024, 768))
         dwgu[d] = out.astype(BF).reshape(4, 2, 32, 768)
+
+    @pl.loop(0, 2)
+    def _(d):
+        units_grad(d)
+
+    rs_corner(part_b, 1)
+
+    @pl.loop(2, 4)
+    def _(d):
+        units_grad(d)
 
     line_grads(dwgu_block, zgu, xgu, 1, True)
     line_grads_relay(dwd_block, zd, xd, 2, 0)
@@ -1010,18 +1041,25 @@
     gbr[k, :, c] = g_res.astype(BF).reshape(4, 32, 1024)
     ag_send(gbr, 3)
 
+    ag_corner(gbr, 3)
     ag_relay(gbr, 3, 1)
     ag_relay(gbr, 3, 2)
-    ag_relay(gbr, 3, 3)
-    line_grads_relay(dwgu_block, zgu, xgu, 1, 0)
-    rs_forward(part_c, 2)
-
-    @pl.loop(0, 4)
-    def _(i):
+
+    def attended_grad(i):
         ag_other(gbr, 3, i)
         m = peer(i)
         out = dot_right(gbr[m].reshape(256, 1024), wo[...].reshape(128, 1024))
         gatt[:, m] = out.astype(BF).reshape(8, 32, 128)
+
+    @pl.loop(0, 3)
+    def _(i):
+        attended_grad(i)
+
+    ag_relay(gbr, 3, 3)
+    for i in (3, 1, 2):
+        rs_halves(part_c, 2, i)
+    line_grads_relay(dwgu_block, zgu, xgu, 1, 0)
+    attended_grad(3)
 
     for t in range(8):
         span = (t + 1) * 128
@@ -1039,6 +1077,7 @@
         g_q = one_of_two(dot_nn(gsc[t, :, 0:span], keys)) * 0.125
         gqkv[:, t, :, 0:128] = g_q.astype(BF).reshape(4, 32, 128)
     line_grads_relay(dwgu_block, zgu, xgu, 1, 1)
+    rs_corner(part_c, 2)
     for u in range(8):
         cols = slice(u * 128, (u + 1) * 128)
         rows = (8 - u) * 256
@@ -1049,14 +1088,12 @@
 
     rs_end(part_a, 0)
 
-    @pl.loop(0, 4)
-    def _(j):
-        i = 3 - j
+    def heads_back(i):
         m = peer(i)
         out = dot_right(gqkv[m].reshape(256, 384), wqkv[...].reshape(1024, 384))
         part_a[m] = out.astype(BF).reshape(4, 2, 32, 1024)
-        rs_copy(part_a, 3, i).start()
-
+
+    rs_start(part_a, 3, heads_back)
 
     @pl.loop(0, 4)
     def _(d):
@@ -1066,40 +1103,7 @@
         dwqkv[d] = out.astype(BF).reshape(4, 2, 32, 384)
 
     line_grads(dwqkv_block, zq, xq, 0, True)
-    rs_forward(part_a, 3)
-    line_grads_relay(dwqkv_block, zq, xq, 0, 0)
-    line_grads_relay(dwqkv_block, zq, xq, 0, 1)
-
-    @pl.loop(0, 4)
-    def _(n):
-        cols = pl.ds(pl.multiple_of(n * 256, 256), 256)
-        right = gbr[:, :, :, :, cols].reshape(1024, 256)
-        out = dot_left(att[...].reshape(1024, 128), right)
-        dwo[:, :, cols] = out.astype(BF).reshape(4, 32, 256)
-
-    def out_grads(start):
-        for p in range(2):
-            for cs in range(2):
-                zz = 2 * c + p
-                here = (zz == z) & (c == cs)
-                src = dwo.at[2 * p + cs]
-
-                @pl.when(here)
-                def _():
-                    if start:
-                        pltpu.make_async_copy(src, go_o.at[z], go_r.at[z]).start()
-
-                @pl.when(jnp.logical_not(here))
-                def _():
-                    copy = remote(
-                        src, go_o.at[z], go_s.at[2 * p + cs], go_r.at[z], dev(k, zz, cs)
-                    )
-                    if start:
-                        copy.start()
-                    else:
-                        copy.wait_send()
-
-    out_grads(True)
+    rs_corner(part_a, 3)
 
     def gather_back(which, dst, start):
         for b in range(4):
@@ -1147,6 +1151,10 @@
                     else:
                         copy.wait_send()
 
+    zgu[z] = line_sum(dwgu_block, zgu, 1).astype(BF)
+    plane_grads(zgu, ggu_o, 1, True)
+    line_grads_relay(dwqkv_block, zq, xq, 0, 0)
+    line_grads_relay(dwqkv_block, zq, xq, 0, 1)
     scaled = rs_sum(part_a, 3)
     lat_f = own_l[...].reshape(128, 1024).astype(F32)
     r_one = lax.rsqrt(jnp.mean(lat_f * lat_f, axis=-1, keepdims=True) + EPS)
@@ -1155,12 +1163,39 @@
     d_lat = gres[...] + r_one * (scaled - normed * inner)
     back[1] = d_lat.astype(BF).reshape(4, 32, 1024)
     gather_back(1, dlat_o, True)
-    zgu[z] = line_sum(dwgu_block, zgu, 1).astype(BF)
-    plane_grads(zgu, ggu_o, 1, True)
-
-
+
+    @pl.loop(0, 4)
+    def _(n):
+        cols = pl.ds(pl.multiple_of(n * 256, 256), 256)
+        right = gbr[:, :, :, :, cols].reshape(1024, 256)
+        out = dot_left(att[...].reshape(1024, 128), right)
+        dwo[:, :, cols] = out.astype(BF).reshape(4, 32, 256)
+
+    def out_grads(start):
+        for p in range(2):
+            for cs in range(2):
+                zz = 2 * c + p
+                here = (zz == z) & (c == cs)
+                src = dwo.at[2 * p + cs]
+
+                @pl.when(here)
+                def _():
+                    if start:
+                        pltpu.make_async_copy(src, go_o.at[z], go_r.at[z]).start()
+
+                @pl.when(jnp.logical_not(here))
+                def _():
+                    copy = remote(
+                        src, go_o.at[z], go_s.at[2 * p + cs], go_r.at[z], dev(k, zz, cs)
+                    )
+                    if start:
+                        copy.start()
+                    else:
+                        copy.wait_send()
+
+    out_grads(True)
     down_sum[...] = line_sum(dwd_block, zd, 2)
-    down_out = pltpu.make_async_copy(down_sum, gd_o, gd_r)
+    down_out = pltpu.make_async_copy(down_sum.at[pl.ds(0, 88)], gd_o, gd_r)
     down_out.start()
     zq[z] = line_sum(dwqkv_block, zq, 0).astype(BF)
     plane_grads(zq, gqkv_o, 0, True)
@@ -1212,7 +1247,7 @@
             jax.ShapeDtypeStruct((128, 1024), BF),
             jax.ShapeDtypeStruct((RANKS, 32, 384), BF),
             jax.ShapeDtypeStruct((RANKS, 32, 768), BF),
-            jax.ShapeDtypeStruct((96, 1024), F32),
+            jax.ShapeDtypeStruct((88, 1024), F32),
             jax.ShapeDtypeStruct((4, 32, 1024), BF),
         ),
         in_specs=[pl.BlockSpec(memory_space=pl.ANY)] * 2
@@ -1282,7 +1317,7 @@
             dma((4,)),
             dma((4,)),
             dma((4, 12)),
-            dma((4, 4)),
+            dma((4, 4, 2)),
             dma((4, 4)),
             dma((4, 2)),
             dma((4, 12)),
@@ -1309,10 +1344,10 @@
 def finish_kernel(
     lat,
     dlat,
-    gqkv,
-    ggu,
+    gqkv_in,
+    ggu_in,
     gd,
-    go,
+    go_in,
     gain_one,
     gain_two,
     wq,
@@ -1331,17 +1366,23 @@
     gg_o,
     gu_o,
     gd_o,
+    gqkv,
+    ggu,
+    go,
+    sems,
 ):
-    lat_o[0] = lat[...]
-    dlat_o[0] = dlat[...]
-    go_o[...] = (go[0].astype(F32) + go[1].astype(F32)) + (go[2].astype(F32) + go[3].astype(F32))
-    gd_o[...] = gd[0:88]
+    moves = ((gqkv_in, gqkv), (ggu_in, ggu), (go_in, go))
+    moves += ((lat, lat_o.at[0]), (dlat, dlat_o.at[0]), (gd, gd_o))
+    copies = [pltpu.make_async_copy(src, dst, sems.at[i]) for i, (src, dst) in enumerate(moves)]
+    for copy in copies:
+        copy.start()
     col_one = jnp.sum(on_diagonal(gain_one[...]), axis=1, keepdims=True)
     col_two = jnp.sum(on_diagonal(gain_two[...]), axis=1, keepdims=True)
 
     def as_row(acc):
         return jnp.sum(on_diagonal(jnp.sum(acc, axis=1, keepdims=True)), axis=0, keepdims=True)
 
+    copies[0].wait()
     acc = jnp.zeros((32, 128), F32)
     for i, (w, out) in enumerate(((wq, gq_o), (wk, gk_o), (wv, gv_o))):
         for r in range(RANKS):
@@ -1350,6 +1391,7 @@
             out[:, cols] = part * col_one
             acc = acc + part * w[:, cols].astype(F32)
     g_one_o[...] = as_row(acc)
+    copies[1].wait()
     acc = jnp.zeros((32, 256), F32)
     for i, (w, out) in enumerate(((wg, gg_o), (wu, gu_o))):
         parts = [None] * 32
@@ -1363,6 +1405,10 @@
         for n in range(11):
             acc = acc + prod[:, n * 256 : (n + 1) * 256]
     g_two_o[...] = as_row(acc)
+    copies[2].wait()
+    go_o[...] = (go[0].astype(F32) + go[1].astype(F32)) + (go[2].astype(F32) + go[3].astype(F32))
+    for copy in copies[3:]:
+        copy.wait()
 
 
 def finish(*arrays):
@@ -1379,12 +1425,20 @@
         ((32, 2816), F32),
         ((88, 1024), F32),
     )
+    hbm = pl.BlockSpec(memory_space=pltpu.HBM)
+    vmem = pl.BlockSpec(memory_space=pltpu.VMEM)
     return pl.pallas_call(
         finish_kernel,
         out_shape=tuple(jax.ShapeDtypeStruct(*o) for o in outs),
-        in_specs=[pl.BlockSpec(memory_space=pltpu.VMEM)] * len(arrays),
-        out_specs=[pl.BlockSpec(memory_space=pltpu.VMEM)] * len(outs),
-        compiler_params=pltpu.CompilerParams(vmem_limit_bytes=32 * 1024 * 1024),
+        in_specs=[hbm] * 6 + [vmem] * 7,
+        out_specs=[vmem] * len(outs),
+        scratch_shapes=[
+            pltpu.VMEM((RANKS, 32, 384), BF),
+            pltpu.VMEM((RANKS, 32, 768), BF),
+            pltpu.VMEM((4, 32, 1024), BF),
+            pltpu.SemaphoreType.DMA((6,)),
+        ],
+        compiler_params=pltpu.CompilerParams(vmem_limit_bytes=60 * 1024 * 1024),
     )(*arrays)
 
 

time: 165 us -> 159 us (0.964)
  the two profiles are of different devices: /device:TPU:27 before, /device:TPU:9 now
where the time goes in v3:
time: 159 us; the launch traced here: 158 us
  Pallas kernels  158 us (99%)
    pallas_call x1, Pallas kernels, run_layer(): pl.pallas_call(layer_kernel, out_shape=(jax.ShapeDtypeStruct((128, 1024),...  154 us
    pallas_call x1, Pallas kernels, finish(): pl.pallas_call(finish_kernel, out_shape=tuple((jax.ShapeDtypeStruct(*o) f...  4.04 us

profile of v3, /device:TPU:9, one launch (start us, length us, event | category | flops | bytes accessed | tf_op | source)
XLA Modules:
  0.0 158.4 jit_solution(13752779751925351543)
XLA Ops:
  0.6 153.5 %shard_map.203 = (bf16[128,1024]{1,0:T(8,128)(2,1)}, bf16[128,1024]{1,0:T(8,128)(2,1)}, bf16[8,32,384]{2,1,0:T(8,128)(2,1)}, bf16[8,32,768]{2,1,0:T(8,128)(2,1)}...) custom-call(bf16[128,1024]{1,0:T(8,128)(2,1)} %bitcast.6, bf16[128,1024]{1,0:T(8,128)(2,1)} %bitcast.7, ...), custom_call_target="tpu_custom_call" | custom-call | tf_op jit(solution)/shard_map/pallas_call | solution.py:1243
  154.2 4.0 %shard_map.204 = (bf16[1,128,1024]{2,1,0:T(8,128)(2,1)}, bf16[1,128,1024]{2,1,0:T(8,128)(2,1)}, f32[1,32]{1,0:T(1,128)}, f32[32,1024]{1,0:T(8,128)}, f32[32,1024...) custom-call(bf16[128,1024]{1,0:T(8,128)(2,1)} %get-tuple-element.28., ...), custom_call_target="tpu_custom_call" | custom-call | tf_op jit(solution)/shard_map/pallas_call | solution.py:1430

commit v4 on v3

--- a/solution.py
+++ b/solution.py
@@ -257,6 +257,11 @@
 F32 = jnp.float32
 DP, ZS, CORES = 4, 4, 2
 RANKS = DP * CORES
+GU = (1, 3, 4)
+
+
+def units_of(rank):
+    return [8 * (rank // CORES) + CORES * b + rank % CORES for b in range(ZS)]
 
 
 def planes_fit(mesh):
@@ -426,8 +431,10 @@
         rows = scaled_rows(w, gain_one).astype(BF)
         for r in range(RANKS):
             wqkv_in[r, :, i * 128 : (i + 1) * 128] = rows[:, r * 128 : (r + 1) * 128]
-    wd_in[0:80] = wd_raw[0:80]
-    wd_in[80:96] = jnp.concatenate([wd_raw[80:88], jnp.zeros((8, 1024), BF)], axis=0)
+    wd_in[0] = wd_raw[0:32]
+    wd_in[1] = wd_raw[32:64]
+    wd_in[2, 0:16] = wd_raw[64:80]
+    wd_in[2, 16:32] = jnp.concatenate([wd_raw[80:88], jnp.zeros((8, 1024), BF)], axis=0)
     tile_row = lax.broadcasted_iota(jnp.int32, (8, 128), 0)
     tile = jnp.zeros((8, 128), jnp.int32)
     for i in range(4):
@@ -435,15 +442,17 @@
     lens_in[...] = tile
 
     def units_to_ranks():
-        for i, w in enumerate((wg_raw, wu_raw)):
-            rows = scaled_rows(w, gain_two)
-            gap = jnp.zeros((32, 8), F32)
-            for r in range(RANKS):
-                parts = []
-                for b in range(ZS):
-                    at = 88 * (8 * (r // CORES) + CORES * b + r % CORES)
-                    parts += [rows[:, at : at + 88], gap]
-                wgu_in[r, :, i * 384 : (i + 1) * 384] = jnp.concatenate(parts, axis=1).astype(BF)
+        both = [scaled_rows(w, gain_two) for w in (wg_raw, wu_raw)]
+        gap = jnp.zeros((32, 8), F32)
+        for r in range(RANKS):
+            for j in range(3):
+                for i, rows in enumerate(both):
+                    parts = []
+                    for unit in units_of(r):
+                        at = 88 * unit + 32 * j
+                        parts += [rows[:, at : at + 32]] if j < 2 else [rows[:, at : at + 24], gap]
+                    lo = 256 * j + 128 * i
+                    wgu_in[r, :, lo : lo + 128] = jnp.concatenate(parts, axis=1).astype(BF)
 
     pl.semaphore_wait(barrier, greeted)
 
@@ -554,7 +563,7 @@
     z_end = 3 * (z // 2)
 
     def far_of(place):
-        return (3 - place, 6 - 3 * place)
+        return (6 - 3 * place, 3 - place)
 
     far = far_of(z)
 
@@ -610,11 +619,11 @@
     def qkv_block(b):
         return wqkv.at[:, b]
 
-    def gu_block(h):
-        return lambda b: wgu.at[pl.ds(2 * h, 2), b]
+    def gu_block(j):
+        return lambda b: wgu.at[:, b, :, :, 256 * j : 256 * j + 256]
 
     def down_block(b):
-        return wd.at[b]
+        return wd.at[:, b]
 
     def out_weights(start):
         to_core = z // 2
@@ -772,19 +781,7 @@
             grad(far[j]), land.at[z], gz_s.at[which, 1 + j], gz_r.at[which, z], dev(k, far[j], c)
         )
 
-    def line_grads(grad, land, add, which, start):
-        @pl.when(middle)
-        def _():
-            copy = remote(
-                grad(z_end), land.at[z], gz_s.at[which, 0], gz_r.at[which, z], dev(k, z_end, c)
-            )
-            if start:
-                copy.start()
-            else:
-                copy.wait_send()
-                for j in range(2):
-                    grads_to_far(grad, land, which, j).wait_send()
-
+    def line_adds(grad, land, add, which, start):
         @pl.when(jnp.logical_not(middle))
         def _():
             mid = 1 + z // 2
@@ -800,6 +797,23 @@
                     copy.start()
                 else:
                     copy.wait_send()
+
+    def line_near(grad, land, add, which, start):
+        @pl.when(middle)
+        def _():
+            copy = remote(
+                grad(z_end), land.at[z], gz_s.at[which, 0], gz_r.at[which, z], dev(k, z_end, c)
+            )
+            if start:
+                copy.start()
+            else:
+                copy.wait_send()
+                for j in range(2):
+                    grads_to_far(grad, land, which, j).wait_send()
+
+        @pl.when(jnp.logical_not(middle))
+        def _():
+            mid = 1 + z // 2
             copy = remote(
                 grad(mid), land.at[z], gz_s.at[which, 2], gz_r.at[which, z], dev(k, mid, c)
             )
@@ -808,6 +822,10 @@
             else:
                 copy.wait_send()
 
+    def line_grads(grad, land, add, which, start):
+        line_adds(grad, land, add, which, start)
+        line_near(grad, land, add, which, start)
+
     def line_grads_relay(grad, land, add, which, j):
         @pl.when(middle)
         def _():
@@ -823,27 +841,30 @@
             total = total + land[near[j]].astype(F32)
         return total
 
-    def dwgu_block(b):
-        return dwgu.at[:, b]
+    def dwgu_block(j):
+        return lambda b: dwgu.at[pl.ds(2 * j, 2), b]
+
+    def units_line(j):
+        return dwgu_block(j), zgu.at[:, pl.ds(2 * j, 2)], xgu.at[:, pl.ds(2 * j, 2)], (1, 5)[j]
 
     def dwqkv_block(b):
         return dwqkv.at[:, b]
 
-    def dwd_block(b):
-        return dwd.at[b]
+    def dwd_block(j):
+        return lambda b: dwd.at[j, b]
 
     spread(lat_in, lat_place, 0, True)
     plane_weights(wqkv_in, wqkv, 0, True)
     spread_lens(True)
-    line_send(down_block, 2, (0,), (0, 1), src=wd_in)
-    own_down = pltpu.make_async_copy(wd_in, wd.at[z], wd_r)
+    out_weights(True)
+    own_down = pltpu.make_async_copy(wd_in, wd.at[:, z], wd_r)
     own_down.start()
     units_to_ranks()
     spread_on(lat_in, lat_place, 0, True)
     plane_weights(wgu_in, wgu, 1, True)
     spread(dout_in, cot_place, 1, True)
     plane_weights_here(wqkv, 0)
-    line_send(qkv_block, 0, (0, 1), (0, 1))
+    line_send(qkv_block, 0, (1, 0), (0, 1))
     for b in range(4):
         wait_for(own_l.at[b], tr_r.at[0, b])
     lat_f = own_l[...].reshape(128, 1024).astype(F32)
@@ -852,16 +873,13 @@
     ag_send(n_one, 0)
     line_relay(qkv_block, 0, 0)
     ag_corner(n_one, 0)
+    line_relay(qkv_block, 0, 1)
+    plane_weights_here(wgu, 1)
+    for j in range(2):
+        line_send(gu_block(j), GU[j], (1, 0), (0, 1))
     ag_relay(n_one, 0, 1)
     ag_relay(n_one, 0, 2)
-    line_relay(qkv_block, 0, 1)
-    spread_on(dout_in, cot_place, 1, True)
-    out_weights(True)
-    line_send(down_block, 2, (1,), (), src=wd_in)
     ag_relay(n_one, 0, 3)
-    plane_weights_here(wgu, 1)
-    line_send(gu_block(0), 1, (0, 1), (0, 1))
-    line_send(gu_block(1), 3, (0, 1), (0, 1))
 
     line_here(qkv_block, 0)
 
@@ -873,7 +891,9 @@
         out = dot_nn(block, wqkv[...].reshape(1024, 384))
         qkv[:, m] = out.astype(BF).reshape(8, 32, 384)
 
-    line_relay(down_block, 2, 0)
+    spread_on(dout_in, cot_place, 1, True)
+    line_send(gu_block(2), GU[2], (1, 0), (0, 1))
+    line_send(down_block, 2, (1, 0), (0, 1), src=wd_in)
 
     wait_for(lens, ln_r)
     lane = lax.broadcasted_iota(jnp.int32, (128, 128), 1)
@@ -928,9 +948,7 @@
         att_f[t] = attended
         att[:, t] = attended.astype(BF).reshape(4, 32, 128)
 
-    for b in range(4):
-        wait_for(cot.at[k, b, c], tr_r.at[1, b])
-    ag_send(cot, 1)
+    line_relay(gu_block(0), GU[0], 0)
     for slot in range(4):
         wait_for(wo.at[slot], wo_r.at[slot])
 
@@ -940,69 +958,100 @@
         part_a[m] = out.astype(BF).reshape(4, 2, 32, 1024)
 
     rs_start(part_a, 0, project_out)
-    line_relay(down_block, 2, 1)
-    ag_corner(cot, 1)
-    ag_relay(cot, 1, 1)
-    ag_relay(cot, 1, 2)
+    line_relay(gu_block(0), GU[0], 1)
+    line_relay(gu_block(1), GU[1], 0)
     rs_corner(part_a, 0)
-    line_relay(gu_block(0), 1, 0)
-    line_relay(gu_block(0), 1, 1)
+    line_relay(gu_block(1), GU[1], 1)
+    line_relay(gu_block(2), GU[2], 0)
     res = own_l[...].reshape(128, 1024).astype(F32) + rs_sum(part_a, 0)
     resid[...] = res
     r_two = lax.rsqrt(jnp.mean(res * res, axis=-1, keepdims=True) + EPS)
     n_two[k, :, c] = (res * r_two).astype(BF).reshape(4, 32, 1024)
     ag_send(n_two, 2)
-    ag_relay(cot, 1, 3)
-    line_relay(gu_block(1), 3, 0)
+    for b in range(4):
+        wait_for(cot.at[k, b, c], tr_r.at[1, b])
+    ag_send(cot, 1)
+    line_relay(gu_block(2), GU[2], 1)
 
     ag_corner(n_two, 2)
+    line_relay(down_block, 2, 0)
     ag_relay(n_two, 2, 1)
     ag_relay(n_two, 2, 2)
-    line_relay(gu_block(1), 3, 1)
-    line_here(gu_block(0), 1)
-    line_here(gu_block(1), 3)
-
-    def feed_forward(i):
-        ag_other(n_two, 2, i)
+    line_relay(down_block, 2, 1)
+    ag_corner(cot, 1)
+
+    def feed_forward(j, i):
         m = peer(i)
-        gu = dot_nn(n_two[m].reshape(256, 1024), wgu[...].reshape(1024, 768))
-        gate = gu[:, :384]
-        up = gu[:, 384:]
+        lo, mid, hi = 256 * j, 256 * j + 128, 256 * j + 256
+        gu = dot_nn(n_two[m].reshape(256, 1024), wgu[:, :, :, :, lo:hi].reshape(1024, 256))
+        gate = gu[:, :128]
+        up = gu[:, 128:]
         sig = jax.nn.sigmoid(gate)
         active = gate * sig
-        hid[m] = (active * up).astype(BF)
-        slope[m, :, :384] = up * sig * (1.0 + gate * (1.0 - sig))
-        slope[m, :, 384:] = active
+        hid[m, :, 128 * j : 128 * j + 128] = (active * up).astype(BF)
+        slope[m, :, lo:mid] = up * sig * (1.0 + gate * (1.0 - sig))
+        slope[m, :, mid:hi] = active
+
+    def down_grad(j):
+        left = hid[:, :, 128 * j : 128 * j + 128].reshape(1024, 128)
+
+        @pl.loop(0, 4)
+        def _(n):
+            cols = pl.ds(pl.multiple_of(n * 256, 256), 256)
+            right = cot[:, :, :, :, cols].reshape(1024, 256)
+            dwd[j, :, :, cols] = dot_left(left, right).astype(BF).reshape(4, 32, 256)
+
+        line_grads(dwd_block(j), zd.at[j], xd.at[j], 2 + j, True)
+
+    line_here(gu_block(0), GU[0])
 
     @pl.loop(0, 3)
     def _(i):
-        feed_forward(i)
+        ag_other(n_two, 2, i)
+        feed_forward(0, i)
 
     ag_relay(n_two, 2, 3)
+    ag_other(n_two, 2, 3)
+    feed_forward(0, 3)
+    for i in (1, 2):
+        ag_relay(cot, 1, i)
+    line_here(gu_block(1), GU[1])
+
+    @pl.loop(0, 4)
+    def _(i):
+        feed_forward(1, i)
+
+    ag_relay(cot, 1, 3)
+    for i in range(4):
+        ag_other(cot, 1, i)
+    down_grad(0)
+    down_grad(1)
+    line_here(gu_block(2), GU[2])
+
+    @pl.loop(0, 4)
+    def _(i):
+        feed_forward(2, i)
+
+    down_grad(2)
     line_here(down_block, 2)
     own_down.wait()
-    for i in range(4):
-        ag_other(cot, 1, i)
-    feed_forward(3)
-
-    @pl.loop(0, 4)
-    def _(n):
-        cols = pl.ds(pl.multiple_of(n * 256, 256), 256)
-        right = cot[:, :, :, :, cols].reshape(1024, 256)
-        out = dot_left(hid[...].reshape(1024, 384), right)
-        dwd[:, :, cols] = out.astype(BF).reshape(4, 96, 256)
-
-    line_grads(dwd_block, zd, xd, 2, True)
 
     def feed_back(i):
         m = peer(i)
         g_hid = dot_right(cot[m].reshape(256, 1024), wd[...].reshape(384, 1024))
-        ggu[m, :, :384] = (g_hid * slope[m, :, :384]).astype(BF)
-        ggu[m, :, 384:] = (g_hid * slope[m, :, 384:]).astype(BF)
+        for j in range(6):
+            cols = slice(128 * j, 128 * j + 128)
+            part = g_hid[:, 128 * (j // 2) : 128 * (j // 2) + 128]
+            ggu[m, :, cols] = (part * slope[m, :, cols]).astype(BF)
         out = dot_right(ggu[m], wgu[...].reshape(1024, 768))
         part_b[m] = out.astype(BF).reshape(4, 2, 32, 1024)
 
+    def down_relay(j):
+        for i in range(2):
+            line_grads_relay(dwd_block(j), zd.at[j], xd.at[j], 2 + j, i)
+
     rs_start(part_b, 1, feed_back)
+    down_relay(0)
 
     def units_grad(d):
         cols = pl.ds(pl.multiple_of(d * 256, 256), 256)
@@ -1015,14 +1064,17 @@
         units_grad(d)
 
     rs_corner(part_b, 1)
+    down_relay(1)
 
     @pl.loop(2, 4)
     def _(d):
         units_grad(d)
 
-    line_grads(dwgu_block, zgu, xgu, 1, True)
-    line_grads_relay(dwd_block, zd, xd, 2, 0)
-    line_grads_relay(dwd_block, zd, xd, 2, 1)
+    for j in range(2):
+        line_adds(*units_line(j), True)
+    for j in range(2):
+        line_near(*units_line(j), True)
+    down_relay(2)
 
     @pl.loop(0, 4)
     def _(i):
@@ -1044,6 +1096,7 @@
     ag_corner(gbr, 3)
     ag_relay(gbr, 3, 1)
     ag_relay(gbr, 3, 2)
+    line_grads_relay(*units_line(0), 0)
 
     def attended_grad(i):
         ag_other(gbr, 3, i)
@@ -1058,8 +1111,9 @@
     ag_relay(gbr, 3, 3)
     for i in (3, 1, 2):
         rs_halves(part_c, 2, i)
-    line_grads_relay(dwgu_block, zgu, xgu, 1, 0)
+    line_grads_relay(*units_line(0), 1)
     attended_grad(3)
+    line_grads_relay(*units_line(1), 0)
 
     for t in range(8):
         span = (t + 1) * 128
@@ -1076,7 +1130,36 @@
         gsc[t, :, 0:span] = g_sc.astype(BF)
         g_q = one_of_two(dot_nn(gsc[t, :, 0:span], keys)) * 0.125
         gqkv[:, t, :, 0:128] = g_q.astype(BF).reshape(4, 32, 128)
-    line_grads_relay(dwgu_block, zgu, xgu, 1, 1)
+    @pl.loop(0, 4)
+    def _(n):
+        cols = pl.ds(pl.multiple_of(n * 256, 256), 256)
+        right = gbr[:, :, :, :, cols].reshape(1024, 256)
+        out = dot_left(att[...].reshape(1024, 128), right)
+        dwo[:, :, cols] = out.astype(BF).reshape(4, 32, 256)
+
+    def out_grads(start):
+        for p in range(2):
+            for cs in range(2):
+                zz = 2 * c + p
+                here = (zz == z) & (c == cs)
+                src = dwo.at[2 * p + cs]
+
+                @pl.when(here)
+                def _():
+                    if start:
+                        pltpu.make_async_copy(src, go_o.at[z], go_r.at[z]).start()
+
+                @pl.when(jnp.logical_not(here))
+                def _():
+                    copy = remote(
+                        src, go_o.at[z], go_s.at[2 * p + cs], go_r.at[z], dev(k, zz, cs)
+                    )
+                    if start:
+                        copy.start()
+                    else:
+                        copy.wait_send()
+
+    line_grads_relay(*units_line(1), 1)
     rs_corner(part_c, 2)
     for u in range(8):
         cols = slice(u * 128, (u + 1) * 128)
@@ -1103,7 +1186,9 @@
         dwqkv[d] = out.astype(BF).reshape(4, 2, 32, 384)
 
     line_grads(dwqkv_block, zq, xq, 0, True)
+    out_grads(True)
     rs_corner(part_a, 3)
+
 
     def gather_back(which, dst, start):
         for b in range(4):
@@ -1151,7 +1236,9 @@
                     else:
                         copy.wait_send()
 
-    zgu[z] = line_sum(dwgu_block, zgu, 1).astype(BF)
+    for j in range(2):
+        grad, land, _, which = units_line(j)
+        land[z] = line_sum(grad, land, which).astype(BF)
     plane_grads(zgu, ggu_o, 1, True)
     line_grads_relay(dwqkv_block, zq, xq, 0, 0)
     line_grads_relay(dwqkv_block, zq, xq, 0, 1)
@@ -1164,37 +1251,8 @@
     back[1] = d_lat.astype(BF).reshape(4, 32, 1024)
     gather_back(1, dlat_o, True)
 
-    @pl.loop(0, 4)
-    def _(n):
-        cols = pl.ds(pl.multiple_of(n * 256, 256), 256)
-        right = gbr[:, :, :, :, cols].reshape(1024, 256)
-        out = dot_left(att[...].reshape(1024, 128), right)
-        dwo[:, :, cols] = out.astype(BF).reshape(4, 32, 256)
-
-    def out_grads(start):
-        for p in range(2):
-            for cs in range(2):
-                zz = 2 * c + p
-                here = (zz == z) & (c == cs)
-                src = dwo.at[2 * p + cs]
-
-                @pl.when(here)
-                def _():
-                    if start:
-                        pltpu.make_async_copy(src, go_o.at[z], go_r.at[z]).start()
-
-                @pl.when(jnp.logical_not(here))
-                def _():
-                    copy = remote(
-                        src, go_o.at[z], go_s.at[2 * p + cs], go_r.at[z], dev(k, zz, cs)
-                    )
-                    if start:
-                        copy.start()
-                    else:
-                        copy.wait_send()
-
-    out_grads(True)
-    down_sum[...] = line_sum(dwd_block, zd, 2)
+    for j in range(3):
+        down_sum[32 * j : 32 * j + 32] = line_sum(dwd_block(j), zd.at[j], 2 + j)
     down_out = pltpu.make_async_copy(down_sum.at[pl.ds(0, 88)], gd_o, gd_r)
     down_out.start()
     zq[z] = line_sum(dwqkv_block, zq, 0).astype(BF)
@@ -1216,8 +1274,8 @@
     plane_weights(wqkv_in, wqkv, 0, False)
     plane_weights(wgu_in, wgu, 1, False)
     line_sent(qkv_block, 0)
-    line_sent(gu_block(0), 1)
-    line_sent(gu_block(1), 3)
+    for j in range(3):
+        line_sent(gu_block(j), GU[j])
     line_sent(down_block, 2, wd_in)
     down_out.wait()
     out_weights(False)
@@ -1226,9 +1284,11 @@
     rs_end(part_b, 1)
     rs_end(part_c, 2)
     rs_end(part_a, 3)
-    line_grads(dwgu_block, zgu, xgu, 1, False)
+    for j in range(2):
+        line_grads(*units_line(j), False)
     line_grads(dwqkv_block, zq, xq, 0, False)
-    line_grads(dwd_block, zd, xd, 2, False)
+    for j in range(3):
+        line_grads(dwd_block(j), zd.at[j], xd.at[j], 2 + j, False)
     plane_grads(zgu, ggu_o, 1, False)
     plane_grads(zq, gqkv_o, 0, False)
     out_grads(False)
@@ -1258,7 +1318,7 @@
             vm((8, 128), jnp.int32),
             vm((RANKS, 32, 384), BF),
             vm((RANKS, 32, 768), BF),
-            vm((96, 1024), BF),
+            vm((3, 32, 1024), BF),
             vm((4, 32, 1024), BF),
             vm((2, 4, 32, 1024), BF),
             vm((8, 128), jnp.int32),
@@ -1268,7 +1328,7 @@
             vm(rows + (1024,), BF),
             vm(rows + (384,), BF),
             vm(rows + (768,), BF),
-            vm((4, 96, 1024), BF),
+            vm((3, 4, 32, 1024), BF),
             vm((4, 32, 1024), BF),
             vm((8, 4, 32, 384), BF),
             vm((4, 8, 32, 128), BF),
@@ -1291,14 +1351,14 @@
             vm((4, 8, 32, 384), BF),
             vm(rows + (384,), BF),
             vm(rows + (768,), BF),
-            vm((4, 96, 1024), BF),
+            vm((3, 4, 32, 1024), BF),
             vm((4, 32, 1024), BF),
             vm((4, 4, 2, 32, 384), BF),
             vm((4, 4, 2, 32, 768), BF),
-            vm((4, 96, 1024), BF),
+            vm((3, 4, 32, 1024), BF),
             vm((2, 4, 2, 32, 384), BF),
             vm((2, 4, 2, 32, 768), BF),
-            vm((2, 96, 1024), BF),
+            vm((3, 2, 32, 1024), BF),
             vm((96, 1024), F32),
             vm((128, 1024), F32),
             vm((128, 1024), F32),
@@ -1311,8 +1371,8 @@
             dma,
             dma((2, 8)),
             dma((2, 8)),
-            dma((4, 4)),
-            dma((4, 4)),
+            dma((5, 4)),
+            dma((5, 4)),
             dma,
             dma((4,)),
             dma((4,)),
@@ -1324,9 +1384,9 @@
             dma((4, 4)),
             dma((4, 2, 2)),
             dma((4, 2)),
-            dma((3, 4)),
-            dma((3, 4)),
-            dma((3, 2)),
+            dma((6, 4)),
+            dma((6, 4)),
+            dma((6, 2)),
             dma((2, 8)),
             dma((2, 8)),
             dma,
@@ -1394,11 +1454,12 @@
     copies[1].wait()
     acc = jnp.zeros((32, 256), F32)
     for i, (w, out) in enumerate(((wg, gg_o), (wu, gu_o))):
-        parts = [None] * 32
+        parts = [None] * 96
         for r in range(RANKS):
-            whole = ggu[r, :, i * 384 : (i + 1) * 384].astype(F32)
-            for b in range(ZS):
-                parts[8 * (r // CORES) + CORES * b + r % CORES] = whole[:, b * 96 : b * 96 + 88]
+            for j in range(3):
+                third = ggu[r, :, 256 * j + 128 * i : 256 * j + 128 * i + 128].astype(F32)
+                for b, unit in enumerate(units_of(r)):
+                    parts[3 * unit + j] = third[:, 32 * b : 32 * b + (24 if j == 2 else 32)]
         rows = jnp.concatenate(parts, axis=1)
         out[...] = rows * col_two
         prod = rows * w[...].astype(F32)

time: 159 us -> 153 us (0.962)
  Pallas kernels: 158 us -> 151 us
    pallas_call x1, Pallas kernels: 154 us -> 147 us  [run_layer(): pl.pallas_call(layer_kernel, out_shape=(jax.ShapeDtypeStruct((128, 1024),...]
where the time goes in v4:
time: 153 us; the launch traced here: 152 us
  Pallas kernels  151 us (99%)
    pallas_call x1, Pallas kernels, run_layer(): pl.pallas_call(layer_kernel, out_shape=(jax.ShapeDtypeStruct((128, 1024),...  147 us
    pallas_call x1, Pallas kernels, finish(): pl.pallas_call(finish_kernel, out_shape=tuple((jax.ShapeDtypeStruct(*o) f...  4.2 us

profile of v4, /device:TPU:9, one launch (start us, length us, event | category | flops | bytes accessed | tf_op | source)
XLA Modules:
  0.0 152.1 jit_solution(3975545578244768570)
XLA Ops:
  0.6 147.1 %shard_map.203 = (bf16[128,1024]{1,0:T(8,128)(2,1)}, bf16[128,1024]{1,0:T(8,128)(2,1)}, bf16[8,32,384]{2,1,0:T(8,128)(2,1)}, bf16[8,32,768]{2,1,0:T(8,128)(2,1)}...) custom-call(bf16[128,1024]{1,0:T(8,128)(2,1)} %bitcast.6, bf16[128,1024]{1,0:T(8,128)(2,1)} %bitcast.7, ...), custom_call_target="tpu_custom_call" | custom-call | tf_op jit(solution)/shard_map/pallas_call | solution.py:1303
  147.7 4.2 %shard_map.204 = (bf16[1,128,1024]{2,1,0:T(8,128)(2,1)}, bf16[1,128,1024]{2,1,0:T(8,128)(2,1)}, f32[1,32]{1,0:T(1,128)}, f32[32,1024]{1,0:T(8,128)}, f32[32,1024...) custom-call(bf16[128,1024]{1,0:T(8,128)(2,1)} %get-tuple-element.28., ...), custom_call_target="tpu_custom_call" | custom-call | tf_op jit(solution)/shard_map/pallas_call | solution.py:1491

commit v5 on v4

--- a/solution.py
+++ b/solution.py
@@ -296,6 +296,21 @@
     lat_in,
     dout_in,
     lengths_in,
+    gain_one_in,
+    gain_two_in,
+    wq_in,
+    wk_in,
+    wv_in,
+    wg_in,
+    wu_in,
+    wd_rows_in,
+    wo_in,
+    lat_o,
+    dlat_o,
+    gqkv_o,
+    ggu_o,
+    gd_o,
+    go_o,
     gain_one,
     gain_two,
     wq_raw,
@@ -304,13 +319,7 @@
     wg_raw,
     wu_raw,
     wd_raw,
-    wo_in,
-    lat_o,
-    dlat_o,
-    gqkv_o,
-    ggu_o,
-    gd_o,
-    go_o,
+    in_r,
     lens_in,
     wqkv_in,
     wgu_in,
@@ -352,6 +361,8 @@
     zq,
     zgu,
     zd,
+    zo,
+    xo,
     xq,
     xgu,
     xd,
@@ -388,6 +399,8 @@
     gd_r,
     go_s,
     go_r,
+    go_x,
+    go_z,
     tb_s,
     tb_r,
 ):
@@ -408,6 +421,20 @@
         return (z + i) % ZS
 
     sibling = dev(k, z, oc)
+
+    loads = (
+        (gain_one_in, gain_one),
+        (gain_two_in, gain_two),
+        (wq_in, wq_raw),
+        (wk_in, wk_raw),
+        (wv_in, wv_raw),
+        (wd_rows_in, wd_raw),
+        (wg_in, wg_raw),
+        (wu_in, wu_raw),
+    )
+    loads = [pltpu.make_async_copy(src, dst, in_r.at[i]) for i, (src, dst) in enumerate(loads)]
+    for load in loads:
+        load.start()
 
     barrier = pltpu.get_barrier_semaphore()
     greeted = 0
@@ -427,20 +454,6 @@
     def scaled_rows(w, gain):
         return dot_nn(on_diagonal(gain[...]).astype(BF), w[...])
 
-    for i, w in enumerate((wq_raw, wk_raw, wv_raw)):
-        rows = scaled_rows(w, gain_one).astype(BF)
-        for r in range(RANKS):
-            wqkv_in[r, :, i * 128 : (i + 1) * 128] = rows[:, r * 128 : (r + 1) * 128]
-    wd_in[0] = wd_raw[0:32]
-    wd_in[1] = wd_raw[32:64]
-    wd_in[2, 0:16] = wd_raw[64:80]
-    wd_in[2, 16:32] = jnp.concatenate([wd_raw[80:88], jnp.zeros((8, 1024), BF)], axis=0)
-    tile_row = lax.broadcasted_iota(jnp.int32, (8, 128), 0)
-    tile = jnp.zeros((8, 128), jnp.int32)
-    for i in range(4):
-        tile = jnp.where(tile_row == i, lengths_in[0, i], tile)
-    lens_in[...] = tile
-
     def units_to_ranks():
         both = [scaled_rows(w, gain_two) for w in (wg_raw, wu_raw)]
         gap = jnp.zeros((32, 8), F32)
@@ -453,6 +466,12 @@
                         parts += [rows[:, at : at + 32]] if j < 2 else [rows[:, at : at + 24], gap]
                     lo = 256 * j + 128 * i
                     wgu_in[r, :, lo : lo + 128] = jnp.concatenate(parts, axis=1).astype(BF)
+
+    tile_row = lax.broadcasted_iota(jnp.int32, (8, 128), 0)
+    tile = jnp.zeros((8, 128), jnp.int32)
+    for i in range(4):
+        tile = jnp.where(tile_row == i, lengths_in[0, i], tile)
+    lens_in[...] = tile
 
     pl.semaphore_wait(barrier, greeted)
 
@@ -625,33 +644,62 @@
     def down_block(b):
         return wd.at[:, b]
 
-    def out_weights(start):
-        to_core = z // 2
-        slot = 2 * (z % 2) + c
-        for i in range(4):
-
-            def send():
-                copy = remote(
-                    wo_in, wo.at[slot], wo_s.at[i], wo_r.at[slot], dev(k, zpeer(i), to_core)
-                )
+    side = z // 2
+
+    def out_block(b):
+        return wo.at[pl.ds(2 * (b % 2), 2)]
+
+    def out_across(start):
+        place = wo.at[2 * (z % 2) + c]
+
+        @pl.when(c == side)
+        def _():
+            if start:
+                pltpu.make_async_copy(wo_in, place, wo_r.at[c]).start()
+
+        @pl.when(c != side)
+        def _():
+            copy = remote(wo_in, place, wo_s.at[0], wo_r.at[c], sibling)
+            if start:
+                copy.start()
+            else:
+                copy.wait_send()
+
+    def out_along(start):
+        @pl.when(c == side)
+        def _():
+            if start:
+                for i in range(2):
+                    wait_for(wo.at[2 * (z % 2) + i], wo_r.at[i])
+            for j in (1, 0):
+                copy = line_copy(out_block, 5, j, z, near[j])
                 if start:
                     copy.start()
                 else:
                     copy.wait_send()
 
-            if i == 0:
-
-                @pl.when(to_core == c)
-                def _():
-                    if start:
-                        pltpu.make_async_copy(wo_in, wo.at[slot], wo_r.at[slot]).start()
-
-                @pl.when(to_core != c)
-                def _():
-                    send()
-
-            else:
-                send()
+    def out_relay(start):
+        @pl.when(middle & (c != side))
+        def _():
+            for j in range(2):
+                if start:
+                    wait_for(out_block(far[j]), wz_r.at[5, far[j]])
+                copy = line_copy(out_block, 5, 2 + j, far[j], z_end)
+                if start:
+                    copy.start()
+                else:
+                    copy.wait_send()
+
+    def out_here():
+        @pl.when(c == side)
+        def _():
+            other = 4 * side + 1 - z
+            wait_for(out_block(other), wz_r.at[5, other])
+
+        @pl.when((c != side) & jnp.logical_not(middle))
+        def _():
+            for j in range(2):
+                wait_for(out_block(2 * c + j), wz_r.at[5, 2 * c + j])
 
     def half(j):
         return pl.ds(2 * j, 2)
@@ -853,18 +901,105 @@
     def dwd_block(j):
         return lambda b: dwd.at[j, b]
 
+    def out_grads_add(start):
+        @pl.when((c != side) & jnp.logical_not(middle))
+        def _():
+            copy = remote(dwo, xo, go_s.at[0], go_x, dev(k, 1 + side, c))
+            if start:
+                copy.start()
+            else:
+                copy.wait_send()
+
+    def out_grads_near(start):
+        @pl.when(c == side)
+        def _():
+            other = 4 * side + 1 - z
+            copy = remote(
+                dwo.at[pl.ds(2 * (other % 2), 2)], zo.at[0], go_s.at[0], go_z.at[0], dev(k, other, c)
+            )
+            if start:
+                copy.start()
+            else:
+                copy.wait_send()
+
+    def out_grads_relay(start):
+        @pl.when((c != side) & middle)
+        def _():
+            if start:
+                wait_for(xo, go_x)
+                dwo[...] = (dwo[...].astype(F32) + xo[...].astype(F32)).astype(BF)
+            for p in range(2):
+                copy = remote(
+                    dwo.at[pl.ds(2 * p, 2)], zo.at[1], go_s.at[p], go_z.at[1], dev(k, 2 * c + p, c)
+                )
+                if start:
+                    copy.start()
+                else:
+                    copy.wait_send()
+
+    def out_grads_home(start):
+        @pl.when(c == side)
+        def _():
+            mine = dwo.at[pl.ds(2 * (z % 2), 2)]
+            if start:
+                total = mine[...].astype(F32)
+                for j in range(2):
+                    wait_for(zo.at[j], go_z.at[j])
+                    total = total + zo[j].astype(F32)
+                mine[...] = total.astype(BF)
+                pltpu.make_async_copy(dwo.at[2 * (z % 2) + c], go_o, go_r).start()
+            copy = remote(dwo.at[2 * (z % 2) + oc], go_o, go_s.at[1], go_r, sibling)
+            if start:
+                copy.start()
+            else:
+                copy.wait_send()
+
+    def gather_back(which, dst, start):
+        for b in range(4):
+            here = (z == k) & (z == b)
+            src = back.at[which, b]
+            place = dst.at[pl.ds(pl.multiple_of(32 * k, 32), 32)]
+
+            @pl.when(here)
+            def _():
+                if start:
+                    pltpu.make_async_copy(src, place, tb_r.at[which, k]).start()
+
+            @pl.when(jnp.logical_not(here))
+            def _():
+                copy = remote(src, place, tb_s.at[which, b], tb_r.at[which, k], dev(z, b, c))
+                if start:
+                    copy.start()
+                else:
+                    copy.wait_send()
+
     spread(lat_in, lat_place, 0, True)
+    for load in loads[:5]:
+        load.wait()
+    for i, w in enumerate((wq_raw, wk_raw, wv_raw)):
+        rows = scaled_rows(w, gain_one).astype(BF)
+        for r in range(RANKS):
+            wqkv_in[r, :, i * 128 : (i + 1) * 128] = rows[:, r * 128 : (r + 1) * 128]
     plane_weights(wqkv_in, wqkv, 0, True)
     spread_lens(True)
-    out_weights(True)
+    loads[5].wait()
+    wd_in[0] = wd_raw[0:32]
+    wd_in[1] = wd_raw[32:64]
+    wd_in[2, 0:16] = wd_raw[64:80]
+    wd_in[2, 16:32] = jnp.concatenate([wd_raw[80:88], jnp.zeros((8, 1024), BF)], axis=0)
+    out_across(True)
     own_down = pltpu.make_async_copy(wd_in, wd.at[:, z], wd_r)
     own_down.start()
+    out_along(True)
+    for load in loads[6:]:
+        load.wait()
     units_to_ranks()
     spread_on(lat_in, lat_place, 0, True)
     plane_weights(wgu_in, wgu, 1, True)
     spread(dout_in, cot_place, 1, True)
     plane_weights_here(wqkv, 0)
     line_send(qkv_block, 0, (1, 0), (0, 1))
+    out_relay(True)
     for b in range(4):
         wait_for(own_l.at[b], tr_r.at[0, b])
     lat_f = own_l[...].reshape(128, 1024).astype(F32)
@@ -874,6 +1009,7 @@
     line_relay(qkv_block, 0, 0)
     ag_corner(n_one, 0)
     line_relay(qkv_block, 0, 1)
+    spread_on(dout_in, cot_place, 1, True)
     plane_weights_here(wgu, 1)
     for j in range(2):
         line_send(gu_block(j), GU[j], (1, 0), (0, 1))
@@ -891,10 +1027,12 @@
         out = dot_nn(block, wqkv[...].reshape(1024, 384))
         qkv[:, m] = out.astype(BF).reshape(8, 32, 384)
 
-    spread_on(dout_in, cot_place, 1, True)
     line_send(gu_block(2), GU[2], (1, 0), (0, 1))
     line_send(down_block, 2, (1, 0), (0, 1), src=wd_in)
 
+    for b in range(4):
+        wait_for(cot.at[k, b, c], tr_r.at[1, b])
+    ag_send(cot, 1)
     wait_for(lens, ln_r)
     lane = lax.broadcasted_iota(jnp.int32, (128, 128), 1)
     row = lax.broadcasted_iota(jnp.int32, (128, 128), 0)
@@ -949,8 +1087,7 @@
         att[:, t] = attended.astype(BF).reshape(4, 32, 128)
 
     line_relay(gu_block(0), GU[0], 0)
-    for slot in range(4):
-        wait_for(wo.at[slot], wo_r.at[slot])
+    out_here()
 
     def project_out(i):
         m = peer(i)
@@ -958,9 +1095,12 @@
         part_a[m] = out.astype(BF).reshape(4, 2, 32, 1024)
 
     rs_start(part_a, 0, project_out)
+    ag_corner(cot, 1)
     line_relay(gu_block(0), GU[0], 1)
     line_relay(gu_block(1), GU[1], 0)
     rs_corner(part_a, 0)
+    for i in (1, 2):
+        ag_relay(cot, 1, i)
     line_relay(gu_block(1), GU[1], 1)
     line_relay(gu_block(2), GU[2], 0)
     res = own_l[...].reshape(128, 1024).astype(F32) + rs_sum(part_a, 0)
@@ -968,9 +1108,7 @@
     r_two = lax.rsqrt(jnp.mean(res * res, axis=-1, keepdims=True) + EPS)
     n_two[k, :, c] = (res * r_two).astype(BF).reshape(4, 32, 1024)
     ag_send(n_two, 2)
-    for b in range(4):
-        wait_for(cot.at[k, b, c], tr_r.at[1, b])
-    ag_send(cot, 1)
+    ag_relay(cot, 1, 3)
     line_relay(gu_block(2), GU[2], 1)
 
     ag_corner(n_two, 2)
@@ -978,7 +1116,6 @@
     ag_relay(n_two, 2, 1)
     ag_relay(n_two, 2, 2)
     line_relay(down_block, 2, 1)
-    ag_corner(cot, 1)
 
     def feed_forward(j, i):
         m = peer(i)
@@ -995,12 +1132,7 @@
     def down_grad(j):
         left = hid[:, :, 128 * j : 128 * j + 128].reshape(1024, 128)
 
-        @pl.loop(0, 4)
-        def _(n):
-            cols = pl.ds(pl.multiple_of(n * 256, 256), 256)
-            right = cot[:, :, :, :, cols].reshape(1024, 256)
-            dwd[j, :, :, cols] = dot_left(left, right).astype(BF).reshape(4, 32, 256)
-
+        dwd[j] = dot_left(left, cot[...].reshape(1024, 1024)).astype(BF).reshape(4, 32, 1024)
         line_grads(dwd_block(j), zd.at[j], xd.at[j], 2 + j, True)
 
     line_here(gu_block(0), GU[0])
@@ -1013,18 +1145,15 @@
     ag_relay(n_two, 2, 3)
     ag_other(n_two, 2, 3)
     feed_forward(0, 3)
-    for i in (1, 2):
-        ag_relay(cot, 1, i)
+    for i in range(4):
+        ag_other(cot, 1, i)
+    down_grad(0)
     line_here(gu_block(1), GU[1])
 
     @pl.loop(0, 4)
     def _(i):
         feed_forward(1, i)
 
-    ag_relay(cot, 1, 3)
-    for i in range(4):
-        ag_other(cot, 1, i)
-    down_grad(0)
     down_grad(1)
     line_here(gu_block(2), GU[2])
 
@@ -1063,6 +1192,7 @@
     def _(d):
         units_grad(d)
 
+    line_adds(*units_line(0), True)
     rs_corner(part_b, 1)
     down_relay(1)
 
@@ -1070,8 +1200,7 @@
     def _(d):
         units_grad(d)
 
-    for j in range(2):
-        line_adds(*units_line(j), True)
+    line_adds(*units_line(1), True)
     for j in range(2):
         line_near(*units_line(j), True)
     down_relay(2)
@@ -1137,28 +1266,6 @@
         out = dot_left(att[...].reshape(1024, 128), right)
         dwo[:, :, cols] = out.astype(BF).reshape(4, 32, 256)
 
-    def out_grads(start):
-        for p in range(2):
-            for cs in range(2):
-                zz = 2 * c + p
-                here = (zz == z) & (c == cs)
-                src = dwo.at[2 * p + cs]
-
-                @pl.when(here)
-                def _():
-                    if start:
-                        pltpu.make_async_copy(src, go_o.at[z], go_r.at[z]).start()
-
-                @pl.when(jnp.logical_not(here))
-                def _():
-                    copy = remote(
-                        src, go_o.at[z], go_s.at[2 * p + cs], go_r.at[z], dev(k, zz, cs)
-                    )
-                    if start:
-                        copy.start()
-                    else:
-                        copy.wait_send()
-
     line_grads_relay(*units_line(1), 1)
     rs_corner(part_c, 2)
     for u in range(8):
@@ -1185,33 +1292,16 @@
         out = dot_left(left, gqkv[...].reshape(1024, 384))
         dwqkv[d] = out.astype(BF).reshape(4, 2, 32, 384)
 
-    line_grads(dwqkv_block, zq, xq, 0, True)
-    out_grads(True)
+    line_adds(dwqkv_block, zq, xq, 0, True)
+    out_grads_add(True)
+    out_grads_near(True)
     rs_corner(part_a, 3)
 
-
-    def gather_back(which, dst, start):
-        for b in range(4):
-            here = (z == k) & (z == b)
-            src = back.at[which, b]
-            place = dst.at[pl.ds(pl.multiple_of(32 * k, 32), 32)]
-
-            @pl.when(here)
-            def _():
-                if start:
-                    pltpu.make_async_copy(src, place, tb_r.at[which, k]).start()
-
-            @pl.when(jnp.logical_not(here))
-            def _():
-                copy = remote(src, place, tb_s.at[which, b], tb_r.at[which, k], dev(z, b, c))
-                if start:
-                    copy.start()
-                else:
-                    copy.wait_send()
 
     out_f = resid[...] + rs_sum(part_c, 2)
     back[0] = out_f.astype(BF).reshape(4, 32, 1024)
     gather_back(0, lat_o, True)
+    line_near(dwqkv_block, zq, xq, 0, True)
 
     def plane_grads(land, dst, which, start):
         for i in range(4):
@@ -1236,10 +1326,6 @@
                     else:
                         copy.wait_send()
 
-    for j in range(2):
-        grad, land, _, which = units_line(j)
-        land[z] = line_sum(grad, land, which).astype(BF)
-    plane_grads(zgu, ggu_o, 1, True)
     line_grads_relay(dwqkv_block, zq, xq, 0, 0)
     line_grads_relay(dwqkv_block, zq, xq, 0, 1)
     scaled = rs_sum(part_a, 3)
@@ -1250,6 +1336,11 @@
     d_lat = gres[...] + r_one * (scaled - normed * inner)
     back[1] = d_lat.astype(BF).reshape(4, 32, 1024)
     gather_back(1, dlat_o, True)
+    out_grads_relay(True)
+    for j in range(2):
+        grad, land, _, which = units_line(j)
+        land[z] = line_sum(grad, land, which).astype(BF)
+    plane_grads(zgu, ggu_o, 1, True)
 
     for j in range(3):
         down_sum[32 * j : 32 * j + 32] = line_sum(dwd_block(j), zd.at[j], 2 + j)
@@ -1257,12 +1348,12 @@
     down_out.start()
     zq[z] = line_sum(dwqkv_block, zq, 0).astype(BF)
     plane_grads(zq, gqkv_o, 0, True)
+    out_grads_home(True)
 
     for which, dst in ((0, lat_o), (1, dlat_o)):
         for b in range(4):
             wait_for(dst.at[pl.ds(32 * b, 32)], tb_r.at[which, b])
-    for b in range(4):
-        wait_for(go_o.at[b], go_r.at[b])
+    wait_for(go_o, go_r)
     for which, dst in ((1, ggu_o), (0, gqkv_o)):
         for r in range(RANKS):
             wait_for(dst.at[r], ga_r.at[which, r])
@@ -1278,7 +1369,9 @@
         line_sent(gu_block(j), GU[j])
     line_sent(down_block, 2, wd_in)
     down_out.wait()
-    out_weights(False)
+    out_across(False)
+    out_along(False)
+    out_relay(False)
     for which, buf in enumerate((n_one, cot, n_two, gbr)):
         ag_end(buf, which)
     rs_end(part_b, 1)
@@ -1291,7 +1384,10 @@
         line_grads(dwd_block(j), zd.at[j], xd.at[j], 2 + j, False)
     plane_grads(zgu, ggu_o, 1, False)
     plane_grads(zq, gqkv_o, 0, False)
-    out_grads(False)
+    out_grads_add(False)
+    out_grads_near(False)
+    out_grads_relay(False)
+    out_grads_home(False)
     gather_back(0, lat_o, False)
     gather_back(1, dlat_o, False)
 
@@ -1308,13 +1404,22 @@
             jax.ShapeDtypeStruct((RANKS, 32, 384), BF),
             jax.ShapeDtypeStruct((RANKS, 32, 768), BF),
             jax.ShapeDtypeStruct((88, 1024), F32),
-            jax.ShapeDtypeStruct((4, 32, 1024), BF),
+            jax.ShapeDtypeStruct((32, 1024), BF),
         ),
         in_specs=[pl.BlockSpec(memory_space=pl.ANY)] * 2
         + [pl.BlockSpec(memory_space=pltpu.SMEM)]
-        + [pl.BlockSpec(memory_space=pltpu.VMEM)] * 9,
+        + [pl.BlockSpec(memory_space=pl.ANY)] * 9,
         out_specs=[pl.BlockSpec(memory_space=pl.ANY)] * 6,
         scratch_shapes=[
+            vm((1, 32), BF),
+            vm((1, 32), BF),
+            vm((32, 1024), BF),
+            vm((32, 1024), BF),
+            vm((32, 1024), BF),
+            vm((32, 2816), BF),
+            vm((32, 2816), BF),
+            vm((88, 1024), BF),
+            dma((8,)),
             vm((8, 128), jnp.int32),
             vm((RANKS, 32, 384), BF),
             vm((RANKS, 32, 768), BF),
@@ -1356,6 +1461,8 @@
             vm((4, 4, 2, 32, 384), BF),
             vm((4, 4, 2, 32, 768), BF),
             vm((3, 4, 32, 1024), BF),
+            vm((2, 2, 32, 1024), BF),
+            vm((4, 32, 1024), BF),
             vm((2, 4, 2, 32, 384), BF),
             vm((2, 4, 2, 32, 768), BF),
             vm((3, 2, 32, 1024), BF),
@@ -1371,11 +1478,11 @@
             dma,
             dma((2, 8)),
             dma((2, 8)),
-            dma((5, 4)),
-            dma((5, 4)),
+            dma((6, 4)),
+            dma((6, 4)),
             dma,
-            dma((4,)),
-            dma((4,)),
+            dma((1,)),
+            dma((2,)),
             dma((4, 12)),
             dma((4, 4, 2)),
             dma((4, 4)),
@@ -1390,8 +1497,10 @@
             dma((2, 8)),
             dma((2, 8)),
             dma,
-            dma((4,)),
-            dma((4,)),
+            dma((2,)),
+            dma,
+            dma,
+            dma((2,)),
             dma((2, 4)),
             dma((2, 4)),
         ],
@@ -1429,31 +1538,54 @@
     gqkv,
     ggu,
     go,
+    lat_v,
+    dlat_v,
+    gd_v,
+    g_one_v,
+    gq_v,
+    gk_v,
+    gv_v,
+    go_v,
+    g_two_v,
+    gg_v,
+    gu_v,
     sems,
+    out_sems,
 ):
-    moves = ((gqkv_in, gqkv), (ggu_in, ggu), (go_in, go))
-    moves += ((lat, lat_o.at[0]), (dlat, dlat_o.at[0]), (gd, gd_o))
+    moves = ((gqkv_in, gqkv), (ggu_in, ggu), (go_in, go), (lat, lat_v), (dlat, dlat_v), (gd, gd_v))
     copies = [pltpu.make_async_copy(src, dst, sems.at[i]) for i, (src, dst) in enumerate(moves)]
     for copy in copies:
         copy.start()
+    leaving = []
+
+    def leave(src, dst):
+        copy = pltpu.make_async_copy(src, dst, out_sems.at[len(leaving)])
+        copy.start()
+        leaving.append(copy)
+
     col_one = jnp.sum(on_diagonal(gain_one[...]), axis=1, keepdims=True)
     col_two = jnp.sum(on_diagonal(gain_two[...]), axis=1, keepdims=True)
 
     def as_row(acc):
         return jnp.sum(on_diagonal(jnp.sum(acc, axis=1, keepdims=True)), axis=0, keepdims=True)
 
+    for copy, src, dst in ((copies[3], lat_v, lat_o.at[0]), (copies[4], dlat_v, dlat_o.at[0]), (copies[5], gd_v, gd_o)):
+        copy.wait()
+        leave(src, dst)
     copies[0].wait()
     acc = jnp.zeros((32, 128), F32)
-    for i, (w, out) in enumerate(((wq, gq_o), (wk, gk_o), (wv, gv_o))):
+    for i, (w, out) in enumerate(((wq, gq_v), (wk, gk_v), (wv, gv_v))):
         for r in range(RANKS):
             cols = slice(r * 128, (r + 1) * 128)
             part = gqkv[r, :, i * 128 : (i + 1) * 128].astype(F32)
             out[:, cols] = part * col_one
             acc = acc + part * w[:, cols].astype(F32)
-    g_one_o[...] = as_row(acc)
+        leave(out, (gq_o, gk_o, gv_o)[i])
+    g_one_v[...] = as_row(acc)
+    leave(g_one_v, g_one_o)
     copies[1].wait()
     acc = jnp.zeros((32, 256), F32)
-    for i, (w, out) in enumerate(((wg, gg_o), (wu, gu_o))):
+    for i, (w, out) in enumerate(((wg, gg_v), (wu, gu_v))):
         parts = [None] * 96
         for r in range(RANKS):
             for j in range(3):
@@ -1462,13 +1594,16 @@
                     parts[3 * unit + j] = third[:, 32 * b : 32 * b + (24 if j == 2 else 32)]
         rows = jnp.concatenate(parts, axis=1)
         out[...] = rows * col_two
+        leave(out, (gg_o, gu_o)[i])
         prod = rows * w[...].astype(F32)
         for n in range(11):
             acc = acc + prod[:, n * 256 : (n + 1) * 256]
-    g_two_o[...] = as_row(acc)
+    g_two_v[...] = as_row(acc)
+    leave(g_two_v, g_two_o)
     copies[2].wait()
-    go_o[...] = (go[0].astype(F32) + go[1].astype(F32)) + (go[2].astype(F32) + go[3].astype(F32))
-    for copy in copies[3:]:
+    go_v[...] = go[...].astype(F32)
+    leave(go_v, go_o)
+    for copy in leaving:
         copy.wait()
 
 
@@ -1492,12 +1627,24 @@
         finish_kernel,
         out_shape=tuple(jax.ShapeDtypeStruct(*o) for o in outs),
         in_specs=[hbm] * 6 + [vmem] * 7,
-        out_specs=[vmem] * len(outs),
+        out_specs=[pl.BlockSpec(memory_space=pl.ANY)] * len(outs),
         scratch_shapes=[
             pltpu.VMEM((RANKS, 32, 384), BF),
             pltpu.VMEM((RANKS, 32, 768), BF),
-            pltpu.VMEM((4, 32, 1024), BF),
+            pltpu.VMEM((32, 1024), BF),
+            pltpu.VMEM((128, 1024), BF),
+            pltpu.VMEM((128, 1024), BF),
+            pltpu.VMEM((88, 1024), F32),
+            pltpu.VMEM((1, 32), F32),
+            pltpu.VMEM((32, 1024), F32),
+            pltpu.VMEM((32, 1024), F32),
+            pltpu.VMEM((32, 1024), F32),
+            pltpu.VMEM((32, 1024), F32),
+            pltpu.VMEM((1, 32), F32),
+            pltpu.VMEM((32, 2816), F32),
+            pltpu.VMEM((32, 2816), F32),
             pltpu.SemaphoreType.DMA((6,)),
+            pltpu.SemaphoreType.DMA((11,)),
         ],
         compiler_params=pltpu.CompilerParams(vmem_limit_bytes=60 * 1024 * 1024),
     )(*arrays)

time: 153 us -> 149 us (0.974)
  Pallas kernels: 151 us -> 148 us
    pallas_call x1, Pallas kernels: 147 us -> 144 us  [run_layer(): pl.pallas_call(layer_kernel, out_shape=(jax.ShapeDtypeStruct((128, 1024),...]
where the time goes in v5:
time: 149 us
  Pallas kernels  148 us (99%)
    pallas_call x1, Pallas kernels, run_layer(): pl.pallas_call(layer_kernel, out_shape=(jax.ShapeDtypeStruct((128, 1024),...  144 us
    pallas_call x1, Pallas kernels, finish(): pl.pallas_call(finish_kernel, out_shape=tuple((jax.ShapeDtypeStruct(*o) f...  4.1 us

profile of v5, /device:TPU:9, one launch (start us, length us, event | category | flops | bytes accessed | tf_op | source)
XLA Modules:
  0.0 148.7 jit_solution(13785200449121504695)
XLA Ops:
  0.6 143.8 %shard_map.203 = (bf16[128,1024]{1,0:T(8,128)(2,1)}, bf16[128,1024]{1,0:T(8,128)(2,1)}, bf16[8,32,384]{2,1,0:T(8,128)(2,1)}, bf16[8,32,768]{2,1,0:T(8,128)(2,1)}...) custom-call(bf16[128,1024]{1,0:T(8,128)(2,1)} %bitcast.6, bf16[128,1024]{1,0:T(8,128)(2,1)} %bitcast.7, s32[1,4]{1,0:T(1,128)} %lengths_in.1, ...), custom_call_target="tpu_custom_call" | custom-call | tf_op jit(solution)/shard_map/pallas_call | solution.py:1399
  144.4 4.1 %shard_map.204 = (bf16[1,128,1024]{2,1,0:T(8,128)(2,1)}, bf16[1,128,1024]{2,1,0:T(8,128)(2,1)}, f32[1,32]{1,0:T(1,128)}, f32[32,1024]{1,0:T(8,128)}, f32[32,1024...) custom-call(bf16[128,1024]{1,0:T(8,128)(2,1)} %get-tuple-element.28., ...), custom_call_target="tpu_custom_call" | custom-call | tf_op jit(solution)/shard_map/pallas_call | solution.py:1626

commit v6 on v5

--- a/solution.py
+++ b/solution.py
@@ -1095,6 +1095,8 @@
         part_a[m] = out.astype(BF).reshape(4, 2, 32, 1024)
 
     rs_start(part_a, 0, project_out)
+    for t in range(8):
+        q_two[t] = two_heads(part_of(t, t + 1, 0).astype(F32)).astype(BF)
     ag_corner(cot, 1)
     line_relay(gu_block(0), GU[0], 1)
     line_relay(gu_block(1), GU[1], 0)
@@ -1251,7 +1253,6 @@
         ratio = gatt[t].reshape(128, 128).astype(F32) / tot[t]
         g_raw = two_heads(ratio.astype(BF).astype(F32)).astype(BF)
         graw_two[t] = g_raw
-        q_two[t] = two_heads(part_of(t, t + 1, 0).astype(F32)).astype(BF)
         prod = ratio * att_f[t]
         g_tot = -jnp.sum(two_heads(prod), axis=-1, keepdims=True)
         g_pr = dot_right(g_raw, vals)
@@ -1259,15 +1260,7 @@
         gsc[t, :, 0:span] = g_sc.astype(BF)
         g_q = one_of_two(dot_nn(gsc[t, :, 0:span], keys)) * 0.125
         gqkv[:, t, :, 0:128] = g_q.astype(BF).reshape(4, 32, 128)
-    @pl.loop(0, 4)
-    def _(n):
-        cols = pl.ds(pl.multiple_of(n * 256, 256), 256)
-        right = gbr[:, :, :, :, cols].reshape(1024, 256)
-        out = dot_left(att[...].reshape(1024, 128), right)
-        dwo[:, :, cols] = out.astype(BF).reshape(4, 32, 256)
-
     line_grads_relay(*units_line(1), 1)
-    rs_corner(part_c, 2)
     for u in range(8):
         cols = slice(u * 128, (u + 1) * 128)
         rows = (8 - u) * 256
@@ -1276,6 +1269,7 @@
         gqkv[:, u, :, 128:256] = g_k.astype(BF).reshape(4, 32, 128)
         gqkv[:, u, :, 256:384] = g_v.astype(BF).reshape(4, 32, 128)
 
+    rs_corner(part_c, 2)
     rs_end(part_a, 0)
 
     def heads_back(i):
@@ -1285,14 +1279,13 @@
 
     rs_start(part_a, 3, heads_back)
 
-    @pl.loop(0, 4)
-    def _(d):
-        cols = pl.ds(pl.multiple_of(d * 256, 256), 256)
-        left = n_one[:, :, :, :, cols].reshape(1024, 256)
+    for d in range(2):
+        left = n_one[:, :, :, :, 512 * d : 512 * d + 512].reshape(1024, 512)
         out = dot_left(left, gqkv[...].reshape(1024, 384))
-        dwqkv[d] = out.astype(BF).reshape(4, 2, 32, 384)
+        dwqkv[2 * d : 2 * d + 2] = out.astype(BF).reshape(2, 4, 2, 32, 384)
 
     line_adds(dwqkv_block, zq, xq, 0, True)
+    dwo[...] = dot_left(att[...].reshape(1024, 128), gbr[...].reshape(1024, 1024)).astype(BF).reshape(4, 32, 1024)
     out_grads_add(True)
     out_grads_near(True)
     rs_corner(part_a, 3)

time: 149 us -> 147 us (0.987)
  Pallas kernels: 148 us -> 146 us
    pallas_call x1, Pallas kernels: 144 us -> 142 us  [run_layer(): pl.pallas_call(layer_kernel, out_shape=(jax.ShapeDtypeStruct((128, 1024),...]
where the time goes in v6:
time: 147 us
  Pallas kernels  146 us (99%)
    pallas_call x1, Pallas kernels, run_layer(): pl.pallas_call(layer_kernel, out_shape=(jax.ShapeDtypeStruct((128, 1024),...  142 us
    pallas_call x1, Pallas kernels, finish(): pl.pallas_call(finish_kernel, out_shape=tuple((jax.ShapeDtypeStruct(*o) f...  4.1 us

profile of v6, /device:TPU:9, one launch (start us, length us, event | category | flops | bytes accessed | tf_op | source)
XLA Modules:
  0.0 147.0 jit_solution(9220176716187228140)
XLA Ops:
  0.6 142.1 %shard_map.203 = (bf16[128,1024]{1,0:T(8,128)(2,1)}, bf16[128,1024]{1,0:T(8,128)(2,1)}, bf16[8,32,384]{2,1,0:T(8,128)(2,1)}, bf16[8,32,768]{2,1,0:T(8,128)(2,1)}...) custom-call(bf16[128,1024]{1,0:T(8,128)(2,1)} %bitcast.6, bf16[128,1024]{1,0:T(8,128)(2,1)} %bitcast.7, s32[1,4]{1,0:T(1,128)} %lengths_in.1, ...), custom_call_target="tpu_custom_call" | custom-call | tf_op jit(solution)/shard_map/pallas_call | solution.py:1392
  142.8 4.1 %shard_map.204 = (bf16[1,128,1024]{2,1,0:T(8,128)(2,1)}, bf16[1,128,1024]{2,1,0:T(8,128)(2,1)}, f32[1,32]{1,0:T(1,128)}, f32[32,1024]{1,0:T(8,128)}, f32[32,1024...) custom-call(bf16[128,1024]{1,0:T(8,128)(2,1)} %get-tuple-element.28., ...), custom_call_target="tpu_custom_call" | custom-call | tf_op jit(solution)/shard_map/pallas_call | solution.py:1619

commit v7 on v6

--- a/solution.py
+++ b/solution.py
@@ -1131,6 +1131,18 @@
         slope[m, :, lo:mid] = up * sig * (1.0 + gate * (1.0 - sig))
         slope[m, :, mid:hi] = active
 
+    def feed_forward_rows(j, at, count):
+        lo, mid, hi = 256 * j, 256 * j + 128, 256 * j + 256
+        rows = pl.ds(at, count)
+        gu = dot_nn(n_two[rows].reshape(256 * count, 1024), wgu[:, :, :, :, lo:hi].reshape(1024, 256))
+        gate = gu[:, :128]
+        up = gu[:, 128:]
+        sig = jax.nn.sigmoid(gate)
+        active = gate * sig
+        hid[rows, :, 128 * j : 128 * j + 128] = (active * up).astype(BF).reshape(count, 256, 128)
+        slope[rows, :, lo:mid] = (up * sig * (1.0 + gate * (1.0 - sig))).reshape(count, 256, 128)
+        slope[rows, :, mid:hi] = active.reshape(count, 256, 128)
+
     def down_grad(j):
         left = hid[:, :, 128 * j : 128 * j + 128].reshape(1024, 128)
 
@@ -1152,16 +1164,16 @@
     down_grad(0)
     line_here(gu_block(1), GU[1])
 
-    @pl.loop(0, 4)
+    @pl.loop(0, 2)
     def _(i):
-        feed_forward(1, i)
+        feed_forward_rows(1, 2 * i, 2)
 
     down_grad(1)
     line_here(gu_block(2), GU[2])
 
-    @pl.loop(0, 4)
+    @pl.loop(0, 2)
     def _(i):
-        feed_forward(2, i)
+        feed_forward_rows(2, 2 * i, 2)
 
     down_grad(2)
     line_here(down_block, 2)
@@ -1185,22 +1197,18 @@
     down_relay(0)
 
     def units_grad(d):
-        cols = pl.ds(pl.multiple_of(d * 256, 256), 256)
-        left = n_two[:, :, :, :, cols].reshape(1024, 256)
+        cols = slice(512 * d, 512 * d + 512)
+        left = n_two[:, :, :, :, cols].reshape(1024, 512)
         out = dot_left(left, ggu[...].reshape(1024, 768))
-        dwgu[d] = out.astype(BF).reshape(4, 2, 32, 768)
-
-    @pl.loop(0, 2)
-    def _(d):
-        units_grad(d)
+        dwgu[2 * d : 2 * d + 2] = out.astype(BF).reshape(2, 4, 2, 32, 768)
+
+    units_grad(0)
 
     line_adds(*units_line(0), True)
     rs_corner(part_b, 1)
     down_relay(1)
 
-    @pl.loop(2, 4)
-    def _(d):
-        units_grad(d)
+    units_grad(1)
 
     line_adds(*units_line(1), True)
     for j in range(2):

time: 147 us -> 147 us (level)
  no operation moved by 1% of the time
where the time goes in v7:
time: 147 us
  Pallas kernels  146 us (99%)
    pallas_call x1, Pallas kernels, run_layer(): pl.pallas_call(layer_kernel, out_shape=(jax.ShapeDtypeStruct((128, 1024),...  142 us
    pallas_call x1, Pallas kernels, finish(): pl.pallas_call(finish_kernel, out_shape=tuple((jax.ShapeDtypeStruct(*o) f...  4.1 us

profile of v7, /device:TPU:9, one launch (start us, length us, event | category | flops | bytes accessed | tf_op | source)
XLA Modules:
  0.0 147.0 jit_solution(12294760319106186555)
XLA Ops:
  0.6 142.1 %shard_map.203 = (bf16[128,1024]{1,0:T(8,128)(2,1)}, bf16[128,1024]{1,0:T(8,128)(2,1)}, bf16[8,32,384]{2,1,0:T(8,128)(2,1)}, bf16[8,32,768]{2,1,0:T(8,128)(2,1)}...) custom-call(bf16[128,1024]{1,0:T(8,128)(2,1)} %bitcast.6, bf16[128,1024]{1,0:T(8,128)(2,1)} %bitcast.7, s32[1,4]{1,0:T(1,128)} %lengths_in.1, ...), custom_call_target="tpu_custom_call" | custom-call | tf_op jit(solution)/shard_map/pallas_call | solution.py:1400
  142.8 4.1 %shard_map.204 = (bf16[1,128,1024]{2,1,0:T(8,128)(2,1)}, bf16[1,128,1024]{2,1,0:T(8,128)(2,1)}, f32[1,32]{1,0:T(1,128)}, f32[32,1024]{1,0:T(8,128)}, f32[32,1024...) custom-call(bf16[128,1024]{1,0:T(8,128)(2,1)} %get-tuple-element.28., ...), custom_call_target="tpu_custom_call" | custom-call | tf_op jit(solution)/shard_map/pallas_call | solution.py:1627
